TPU v7x, 32 devices: a whole 2x2x4 slice. The times are simulated.
32 devices in a mesh: seq: 8 (over z, x), tm: 4 (over y, core).
Axes of the slice: x: 2, y: 2, z: 4, core: 2. Of those that a mesh axis runs over, the one named last changes fastest.
Arguments:
- latent: bfloat16 [8, 4096], P(None, ('seq', 'tm')), may hold values from -6 to 6
- first_kernel: bfloat16 [3, 3, 3, 16, 512], replicated, may hold values from -0.3125 to 0.3125
- first_bias: float32 [512], replicated, may hold values from -3 to 3
- first_gain: float32 [512], replicated, may hold values from 0.1 to 1.9
- second_kernel: bfloat16 [3, 3, 3, 512, 256], replicated, may hold values from -0.0546875 to 0.0546875
- second_bias: float32 [256], replicated, may hold values from -3 to 3
- second_gain: float32 [256], replicated, may hold values from 0.1 to 1.9
- final_kernel: bfloat16 [3, 3, 3, 256, 128], replicated, may hold values from -0.078125 to 0.078125
- final_bias: float32 [128], replicated, may hold values from -2 to 2
Outputs:
- decoded: bfloat16 [8, 32, 128, 128], P('tm', 'seq')
All inputs are finite; a program needn't handle non-finite values.
Results may differ from a plain program's by a relative error of at most 0.0051.
Values may be sent and summed in bfloat16 or wider, within the bound.
No kernel may reach another device: no remote copies, remote signals or barrier semaphores. Data moves between devices by JAX's collectives and lax.ppermute only.
A program may use at most 64 MiB of HBM per device.

v0:
```python
import jax
import jax.numpy as jnp
from jax import lax
from jax.sharding import PartitionSpec as P

RH = 1


def passed_along(array, axis, by):
    devices = lax.axis_size(axis)
    pairs = [(i, i + by) for i in range(devices) if 0 <= i + by < devices]
    return lax.ppermute(array, axis, pairs)


def padded_2(array, sides, width):
    for axis, dim in sides:
        devices, length = (lax.axis_size(axis), array.shape[dim])
        up = [(i, (i + 1) % devices) for i in range(devices - 1)]
        down = [(j, i) for i, j in up]
        last = lax.slice_in_dim(array, length - width, length, axis=dim)
        first = lax.slice_in_dim(array, 0, width, axis=dim)
        before = lax.ppermute(last, axis, up)
        after = lax.ppermute(first, axis, down)
        array = jnp.concatenate([before, array, after], axis=dim)
    return array


def conv_taps(padded, kernel, offset):
    frames = padded.shape[0] - 2
    height = padded.shape[1] - 2
    columns = padded.shape[2] - 2
    in_channels = padded.shape[3]
    out_channels = kernel.shape[4]
    summed = jnp.zeros((frames, height, columns, out_channels), jnp.float32)
    for time_tap in range(3):
        for row_tap in range(3):
            slab_rows = padded[time_tap : time_tap + frames, row_tap : row_tap + height]
            stacked = jnp.concatenate(
                [slab_rows[:, :, col_tap : col_tap + columns] for col_tap in range(3)], axis=3
            )
            matrix = kernel[time_tap, row_tap].reshape(3 * in_channels, out_channels)
            summed = summed + jnp.einsum(
                "abcd,de->abce", stacked, matrix, preferred_element_type=jnp.float32
            )
    return summed + offset


def activate(hidden, norm_gain):
    factor = lax.rsqrt(jnp.mean(hidden * hidden, axis=3, keepdims=True) + 1e-06)
    return jax.nn.silu(hidden * factor * norm_gain).astype(jnp.bfloat16)


def causal_frames(tensor, before):
    repeated = jnp.concatenate([tensor[:1], tensor[:1]], axis=0)
    at_start = lax.axis_index("tm") == 0
    return jnp.concatenate([jnp.where(at_start, repeated, before), tensor], axis=0)


def edge_rows(tensor, extended):
    top_row = jnp.where(lax.axis_index("seq") == 0, tensor[:, :1], extended[:, :1])
    bottom_row = jnp.where(
        lax.axis_index("seq") == lax.axis_size("seq") - 1, tensor[:, -1:], extended[:, -1:]
    )
    return jnp.concatenate([top_row, tensor, bottom_row], axis=1)


def double_size(tensor):
    return jnp.repeat(jnp.repeat(tensor, 2, axis=1), 2, axis=2)


def pad_columns(tensor):
    return jnp.pad(tensor, ((0, 0), (0, 0), (1, 1), (0, 0)), mode="edge")


def per_device(
    latent,
    first_kernel,
    first_bias,
    first_gain,
    second_kernel,
    second_bias,
    second_gain,
    final_kernel,
    final_bias,
):
    tm_count = lax.axis_size("tm")
    frame_count = latent.shape[0] // tm_count
    channels = first_kernel.shape[3]
    tokens = lax.all_to_all(latent, "tm", split_axis=0, concat_axis=1, tiled=True)
    latent_grid = tokens.reshape(frame_count, RH, -1, channels)
    before = passed_along(latent_grid, "tm", 1)
    with_time = causal_frames(latent_grid, before)
    beside = padded_2(with_time, (("seq", 1),), 1)
    padded = pad_columns(edge_rows(with_time, beside))
    first_act = activate(conv_taps(padded, first_kernel, first_bias), first_gain)
    before = passed_along(first_act, "tm", 1)
    with_time = causal_frames(first_act, before)
    beside = padded_2(with_time, (("seq", 1),), 1)
    widened = double_size(edge_rows(with_time, beside))
    hidden = conv_taps(pad_columns(widened[:, 1:-1]), second_kernel, second_bias)
    second_act = activate(hidden, second_gain)
    before = passed_along(second_act, "tm", 1)
    with_time = causal_frames(second_act, before)
    beside = padded_2(with_time, (("seq", 1),), 1)
    extended = edge_rows(with_time, beside)
    enlarged = double_size(extended)[:, 1:-1]
    decoded = conv_taps(pad_columns(enlarged), final_kernel, final_bias)
    return decoded.astype(jnp.bfloat16)


def solution(mesh):
    placed = (P(None, ("seq", "tm")), P(), P(), P(), P(), P(), P(), P(), P())
    return jax.shard_map(
        per_device,
        mesh=mesh,
        in_specs=placed,
        out_specs=P("tm", "seq", None, None),
        check_vma=False,
    )
```

profile of v0, /device:TPU:12, one launch (start us, length us, event | category | flops | bytes accessed | tf_op | source)
XLA Modules:
  0.0 92.7 jit_solution(7900740025680816793)
XLA Ops:
  0.0 3.7 %all-to-all-start = ((bf16[4,2,128]{2,1,0:T(2,128)(2,1)}), bf16[4,2,128]{2,1,0:T(2,128)(2,1)S(1)}, u32[]{:S(2)}, u32[]{:S(2)}) async-start(bf16[4,2,128]{2,1,0:T(2,128)(2,1)} %bitcast.215), calls=%async_computation | async-start | bytes 4096 | tf_op jit(solution)/shard_map/all_to_all | solution.py:89
  3.7 1.0 %fusion.257 = (bf16[1,1,3,16,512]{4,3,2,1,0:T(8,128)(2,1)S(1)}, bf16[1,1,3,16,512]{4,3,2,1,0:T(8,128)(2,1)S(1)}, bf16[1,1,3,16,512]{4,3,2,1,0:T(8,128)(2,1)S(1)}...) fusion(bf16[3,3,3,16,512]{4,3,2,1,0:T(8,128)(2,1)} %param.10), kind=kLoop, calls=%fused_computation.359 | loop fusion | bytes 884736 | tf_op jit(solution)/shard_map/slice | solution.py:41
  4.7 0.6 all-to-all-done
  5.5 1.9 %collective-permute-start = (bf16[2,1,32,16]{3,2,0,1:T(8,128)(2,1)S(1)}, bf16[2,1,32,16]{3,2,0,1:T(8,128)(2,1)S(1)}, u32[]{:S(2)}, u32[]{:S(2)}) collective-permute-start(bf16[2,1,32,16]{3,2,0,1:T(8,128)(2,1)S(1)} %reshape.105), channel_id=1, source_target_pairs={{0,1},{1,2},{2,3},{4,5},{5,6},{6,7},{8,9},{9,10},{10,11},{12,13},{... | collective-permute-start | bytes 6152 | tf_op jit(solution)/shard_map/ppermute | solution.py:12
  7.5 3.0 %collective-permute-done = bf16[2,1,32,16]{3,2,0,1:T(8,128)(2,1)S(1)} collective-permute-done((bf16[2,1,32,16]{3,2,0,1:T(8,128)(2,1)S(1)}, bf16[2,1,32,16]{3,2,0,1:T(8,128)(2,1)S(1)}, u32[]{:S(2)}, u32[]{:S(2)}) %collective-permute-start) | collective-permute-done | bytes 2080 | tf_op jit(solution)/shard_map/ppermute | solution.py:12
  10.5 3.3 %collective-permute-start.2 = (bf16[4,1,32,16]{3,2,0,1:T(8,128)(2,1)S(1)}, bf16[4,1,32,16]{3,2,0,1:T(8,128)(2,1)S(1)}, u32[]{:S(2)}, u32[]{:S(2)}) collective-permute-start(bf16[4,1,32,16]{3,2,0,1:T(8,128)(2,1)S(1)} %pad_maximum_fusion.14), channel_id=1, source_target_pairs={{4,0},{8,4},{12,8},{16,12},{20,16},{24,20},{28,24},{5,1},{9,5},{13... | collective-permute-start | bytes 12296 | tf_op jit(solution)/shard_map/ppermute | solution.py:23
  13.8 2.6 %collective-permute-start.1 = (bf16[4,1,32,16]{3,2,0,1:T(8,128)(2,1)S(1)}, bf16[4,1,32,16]{3,2,0,1:T(8,128)(2,1)S(1)}, u32[]{:S(2)}, u32[]{:S(2)}) collective-permute-start(bf16[4,1,32,16]{3,2,0,1:T(8,128)(2,1)S(1)} %pad_maximum_fusion.14), channel_id=1, source_target_pairs={{0,4},{4,8},{8,12},{12,16},{16,20},{20,24},{24,28},{1,5},{5,9},{9,... | collective-permute-start | bytes 12296 | tf_op jit(solution)/shard_map/ppermute | solution.py:22
  16.4 4.1 %collective-permute-done.1 = bf16[4,1,32,16]{3,2,0,1:T(8,128)(2,1)S(1)} collective-permute-done((bf16[4,1,32,16]{3,2,0,1:T(8,128)(2,1)S(1)}, bf16[4,1,32,16]{3,2,0,1:T(8,128)(2,1)S(1)}, u32[]{:S(2)}, u32[]{:S(2)}) %collective-permute-start.1) | collective-permute-done | bytes 4128 | tf_op jit(solution)/shard_map/ppermute | solution.py:22
  20.9 0.2 convolution_add_fusion.15
  21.2 0.2 convolution_add_fusion.14
  21.4 0.2 convolution_add_fusion.13
  21.6 0.2 convolution_add_fusion.12
  21.8 0.2 convolution_add_fusion.11
  22.0 0.2 convolution_add_fusion.10
  22.2 0.2 convolution_add_fusion.9
  22.4 0.3 multiply_reduce_fusion.1
  23.0 1.9 %collective-permute-start.3 = (bf16[2,1,32,512]{3,2,0,1:T(8,128)(2,1)S(1)}, bf16[2,1,32,512]{3,2,0,1:T(8,128)(2,1)S(1)}, u32[]{:S(2)}, u32[]{:S(2)}) collective-permute-start(bf16[2,1,32,512]{3,2,0,1:T(8,128)(2,1)S(1)} %fusion.289), channel_id=1, source_target_pairs={{0,1},{1,2},{2,3},{4,5},{5,6},{6,7},{8,9},{9,10},{10,11},{12,13},{... | collective-permute-start | bytes 196616 | tf_op jit(solution)/shard_map/ppermute | solution.py:12
  24.9 3.6 %collective-permute-done.3 = bf16[2,1,32,512]{3,2,0,1:T(8,128)(2,1)S(1)} collective-permute-done((bf16[2,1,32,512]{3,2,0,1:T(8,128)(2,1)S(1)}, bf16[2,1,32,512]{3,2,0,1:T(8,128)(2,1)S(1)}, u32[]{:S(2)}, u32[]{:S(2)}) %collective-permute-start.3) | collective-permute-done | bytes 65568 | tf_op jit(solution)/shard_map/ppermute | solution.py:12
  28.6 1.9 %collective-permute-start.5 = (bf16[4,1,32,512]{3,2,0,1:T(8,128)(2,1)S(1)}, bf16[4,1,32,512]{3,2,0,1:T(8,128)(2,1)S(1)}, u32[]{:S(2)}, u32[]{:S(2)}) collective-permute-start(bf16[4,1,32,512]{3,2,0,1:T(8,128)(2,1)S(1)} %pad_maximum_fusion.13), channel_id=1, source_target_pairs={{4,0},{8,4},{12,8},{16,12},{20,16},{24,20},{28,24},{5,1},{9,5},{13... | collective-permute-start | bytes 393224 | tf_op jit(solution)/shard_map/ppermute | solution.py:23
  30.6 3.9 %collective-permute-start.4 = (bf16[4,1,32,512]{3,2,0,1:T(8,128)(2,1)S(1)}, bf16[4,1,32,512]{3,2,0,1:T(8,128)(2,1)S(1)}, u32[]{:S(2)}, u32[]{:S(2)}) collective-permute-start(bf16[4,1,32,512]{3,2,0,1:T(8,128)(2,1)S(1)} %pad_maximum_fusion.13), channel_id=1, source_target_pairs={{0,4},{4,8},{8,12},{12,16},{16,20},{20,24},{24,28},{1,5},{5,9},{9,... | collective-permute-start | bytes 393224 | tf_op jit(solution)/shard_map/ppermute | solution.py:22
  34.5 5.9 %fusion.251 = (bf16[1,1,3,512,256]{4,3,2,1,0:T(8,128)(2,1)}, bf16[1,1,3,512,256]{4,3,2,1,0:T(8,128)(2,1)}, bf16[1,1,3,512,256]{4,3,2,1,0:T(8,128)(2,1)}, bf16[1,...) fusion(bf16[3,3,3,512,256]{4,3,2,1,0:T(8,128)(2,1)} %param.13), kind=kLoop, calls=%fused_computation.353 | loop fusion | bytes 14155776 | tf_op jit(solution)/shard_map/slice | solution.py:41
  40.6 1.1 %broadcast_in_dim.9 = bf16[4,6,32,2,512]{4,3,2,1,0:T(2,128)(2,1)S(1)} broadcast(bf16[4,6,32,512]{3,2,1,0:T(8,128)(2,1)S(1)} %bitcast.184), dimensions={0,1,2,4} | broadcast | bytes 2359296 | tf_op jit(solution)/shard_map/broadcast_in_dim | solution.py:68
  41.7 0.6 reshape.116
  42.6 0.3 fusion.255
  42.8 0.6 fusion.152
  43.4 0.4 fusion.160
  43.9 0.7 copy-done.9
  44.6 0.4 fusion.94
  45.1 0.4 convolution_add_fusion.7
  45.5 0.8 copy-done.7
  46.2 0.4 convolution_add_fusion.6
  46.6 0.8 copy-done.6
  47.4 0.4 convolution_add_fusion.5
  47.7 0.8 copy-done.5
  48.5 0.4 convolution_add_fusion.4
  48.9 0.8 copy-done.4
  49.6 0.4 convolution_add_fusion.3
  50.0 0.8 copy-done.3
  50.8 0.4 convolution_add_fusion.2
  51.1 0.8 copy-done.2
  51.9 0.4 convolution_add_fusion.1
  52.3 0.8 copy-done.1
  53.0 0.5 multiply_reduce_fusion
  53.9 2.1 %collective-permute-start.6 = (bf16[2,2,64,256]{3,2,1,0:T(8,128)(2,1)S(1)}, bf16[2,2,64,256]{3,2,1,0:T(8,128)(2,1)S(1)}, u32[]{:S(2)}, u32[]{:S(2)}) collective-permute-start(bf16[2,2,64,256]{3,2,1,0:T(8,128)(2,1)S(1)} %multiply_convert_fusion), channel_id=1, source_target_pairs={{0,1},{1,2},{2,3},{4,5},{5,6},{6,7},{8,9},{9,10},{10,11},{12,13},{... | collective-permute-start | bytes 393224 | tf_op jit(solution)/shard_map/ppermute | solution.py:12
  55.9 4.3 %collective-permute-done.6 = bf16[2,2,64,256]{3,2,1,0:T(8,128)(2,1)S(1)} collective-permute-done((bf16[2,2,64,256]{3,2,1,0:T(8,128)(2,1)S(1)}, bf16[2,2,64,256]{3,2,1,0:T(8,128)(2,1)S(1)}, u32[]{:S(2)}, u32[]{:S(2)}) %collective-permute-start.6) | collective-permute-done | bytes 131104 | tf_op jit(solution)/shard_map/ppermute | solution.py:12
  60.3 2.9 %collective-permute-start.7 = (bf16[4,1,64,256]{3,2,1,0:T(8,128)(2,1)S(1)}, bf16[4,1,64,256]{3,2,1,0:T(8,128)(2,1)S(1)}, u32[]{:S(2)}, u32[]{:S(2)}) collective-permute-start(bf16[4,1,64,256]{3,2,1,0:T(8,128)(2,1)S(1)} %pad_maximum_fusion.12), channel_id=1, source_target_pairs={{0,4},{4,8},{8,12},{12,16},{16,20},{20,24},{24,28},{1,5},{5,9},{9,... | collective-permute-start | bytes 393224 | tf_op jit(solution)/shard_map/ppermute | solution.py:22
  63.2 4.8 %collective-permute-done.7 = bf16[4,1,64,256]{3,2,1,0:T(8,128)(2,1)S(1)} collective-permute-done((bf16[4,1,64,256]{3,2,1,0:T(8,128)(2,1)S(1)}, bf16[4,1,64,256]{3,2,1,0:T(8,128)(2,1)S(1)}, u32[]{:S(2)}, u32[]{:S(2)}) %collective-permute-start.7) | collective-permute-done | bytes 131104 | tf_op jit(solution)/shard_map/ppermute | solution.py:22
  68.1 2.1 %collective-permute-start.8 = (bf16[4,1,64,256]{3,2,1,0:T(8,128)(2,1)S(1)}, bf16[4,1,64,256]{3,2,1,0:T(8,128)(2,1)S(1)}, u32[]{:S(2)}, u32[]{:S(2)}) collective-permute-start(bf16[4,1,64,256]{3,2,1,0:T(8,128)(2,1)S(1)} %get-tuple-element.6), channel_id=1, source_target_pairs={{4,0},{8,4},{12,8},{16,12},{20,16},{24,20},{28,24},{5,1},{9,5},{13... | collective-permute-start | bytes 393224 | tf_op jit(solution)/shard_map/ppermute | solution.py:23
  70.2 0.9 fusion.254
  71.1 3.9 %collective-permute-done.8 = bf16[4,1,64,256]{3,2,1,0:T(8,128)(2,1)S(1)} collective-permute-done((bf16[4,1,64,256]{3,2,1,0:T(8,128)(2,1)S(1)}, bf16[4,1,64,256]{3,2,1,0:T(8,128)(2,1)S(1)}, u32[]{:S(2)}, u32[]{:S(2)}) %collective-permute-start.8) | collective-permute-done | bytes 131104 | tf_op jit(solution)/shard_map/ppermute | solution.py:23
  75.2 3.0 %broadcast_in_dim.22 = bf16[4,8,64,2,256]{4,3,2,1,0:T(2,128)(2,1)} broadcast(bf16[4,8,64,256]{3,2,1,0:T(8,128)(2,1)S(1)} %bitcast.183), dimensions={0,1,2,4} | broadcast | bytes 3145728 | tf_op jit(solution)/shard_map/broadcast_in_dim | solution.py:68
  78.1 2.7 %reshape.118 = bf16[4,8,128,256]{3,2,1,0:T(8,128)(2,1)S(1)} reshape(bf16[4,8,64,2,256]{4,3,2,1,0:T(2,128)(2,1)} %broadcast_in_dim.22) | data formatting | bytes 4194304 | tf_op jit(solution)/shard_map/reshape | solution.py:68
  81.1 0.6 fusion.252
  81.6 2.4 %fusion.144 = (bf16[2,4,128,256]{3,2,1,0:T(8,128)(2,1)S(1)}, bf16[2,4,128,256]{3,2,1,0:T(8,128)(2,1)S(1)}, bf16[2,4,128,256]{3,2,1,0:T(8,128)(2,1)S(1)}, bf16[2,...) fusion(bf16[4,6,128,256]{3,2,1,0:T(8,128)(2,1)S(1)} %slice.793,, ...), kind=kLoop, calls=%fused_computation.204 | loop fusion | flops 8388608 | bytes 5779456 | tf_op jit(solution)/shard_map/jit(_pad)/concatenate | solution.py:72
  84.1 2.3 %fusion.136 = (bf16[2,4,128,256]{3,2,1,0:T(8,128)(2,1)S(1)}, bf16[2,4,128,256]{3,2,1,0:T(8,128)(2,1)S(1)}, bf16[2,4,128,256]{3,2,1,0:T(8,128)(2,1)S(1)}, bf16[2,...) fusion(bf16[4,6,128,256]{3,2,1,0:T(8,128)(2,1)S(1)} %slice.793,, ...), kind=kLoop, calls=%fused_computation.196 | loop fusion | flops 8388608 | bytes 5779456 | tf_op jit(solution)/shard_map/jit(_pad)/concatenate | solution.py:72
  86.4 0.8 fusion.1
  87.3 0.6 fusion.7
  87.9 0.6 fusion.74
  88.5 0.6 fusion.71
  89.0 0.6 fusion.68
  89.6 0.6 fusion.65
  90.2 0.6 fusion.62
  90.8 0.6 fusion.59
  91.4 1.3 %fusion.83 = bf16[2,4,128,128]{3,2,1,0:T(8,128)(2,1)} fusion(f32[2,4,128,128]{3,2,1,0:T(8,128)S(1)} %fusion.1, f32[2,4,128,128]{3,2,1,0:T(8,128)S(1)} %fusion.59, bf16[768,128,1,1]{1,0,3,2:T(8,128)(2,1)S(1)} %bitcast.194, bf16[2,4,128,256]{3,2,1,0:T(8,128)(2,1)S(1)} %get-tuple-element.44, bf16[2,4,128,256]{3,2,1,0:T(8,128)(2,1)S(1)} %get-tuple-element.16, ...), kind=kOutput, calls=%fused_computation.97 | convolution fusion | flops 206569472 | bytes 3080704 | tf_op jit(solution)/shard_map/abcd,de->abce/dot_general | solution.py:42
  (64 shorter events, 2.3 us)
Async XLA Ops:
  0.0 5.4 %all-to-all-start = ((bf16[4,2,128]{2,1,0:T(2,128)(2,1)}), bf16[4,2,128]{2,1,0:T(2,128)(2,1)S(1)}, u32[]{:S(2)}, u32[]{:S(2)}) async-start(bf16[4,2,128]{2,1,0:T(2,128)(2,1)} %bitcast.215), calls=%async_computation | async-start | bytes 4096 | tf_op jit(solution)/shard_map/all_to_all | solution.py:89
  5.5 5.1 %collective-permute-start = (bf16[2,1,32,16]{3,2,0,1:T(8,128)(2,1)S(1)}, bf16[2,1,32,16]{3,2,0,1:T(8,128)(2,1)S(1)}, u32[]{:S(2)}, u32[]{:S(2)}) collective-permute-start(bf16[2,1,32,16]{3,2,0,1:T(8,128)(2,1)S(1)} %reshape.105), channel_id=1, source_target_pairs={{0,1},{1,2},{2,3},{4,5},{5,6},{6,7},{8,9},{9,10},{10,11},{12,13},{... | collective-permute-start | bytes 6152 | tf_op jit(solution)/shard_map/ppermute | solution.py:12
  10.5 5.9 %collective-permute-start.2 = (bf16[4,1,32,16]{3,2,0,1:T(8,128)(2,1)S(1)}, bf16[4,1,32,16]{3,2,0,1:T(8,128)(2,1)S(1)}, u32[]{:S(2)}, u32[]{:S(2)}) collective-permute-start(bf16[4,1,32,16]{3,2,0,1:T(8,128)(2,1)S(1)} %pad_maximum_fusion.14), channel_id=1, source_target_pairs={{4,0},{8,4},{12,8},{16,12},{20,16},{24,20},{28,24},{5,1},{9,5},{13... | collective-permute-start | bytes 12296 | tf_op jit(solution)/shard_map/ppermute | solution.py:23
  13.8 6.7 %collective-permute-start.1 = (bf16[4,1,32,16]{3,2,0,1:T(8,128)(2,1)S(1)}, bf16[4,1,32,16]{3,2,0,1:T(8,128)(2,1)S(1)}, u32[]{:S(2)}, u32[]{:S(2)}) collective-permute-start(bf16[4,1,32,16]{3,2,0,1:T(8,128)(2,1)S(1)} %pad_maximum_fusion.14), channel_id=1, source_target_pairs={{0,4},{4,8},{8,12},{12,16},{16,20},{20,24},{24,28},{1,5},{5,9},{9,... | collective-permute-start | bytes 12296 | tf_op jit(solution)/shard_map/ppermute | solution.py:22
  20.6 1.8 %copy-start.13 = (f32[512]{0:T(512)S(1)}, f32[512]{0:T(512)}, u32[]{:S(2)}) copy-start(f32[512]{0:T(512)} %param.11) | copy-start | bytes 6148
  20.7 2.0 %copy-start.12 = (f32[512]{0:T(512)S(1)}, f32[512]{0:T(512)}, u32[]{:S(2)}) copy-start(f32[512]{0:T(512)} %param.12) | copy-start | bytes 6148
  23.0 5.6 %collective-permute-start.3 = (bf16[2,1,32,512]{3,2,0,1:T(8,128)(2,1)S(1)}, bf16[2,1,32,512]{3,2,0,1:T(8,128)(2,1)S(1)}, u32[]{:S(2)}, u32[]{:S(2)}) collective-permute-start(bf16[2,1,32,512]{3,2,0,1:T(8,128)(2,1)S(1)} %fusion.289), channel_id=1, source_target_pairs={{0,1},{1,2},{2,3},{4,5},{5,6},{6,7},{8,9},{9,10},{10,11},{12,13},{... | collective-permute-start | bytes 196616 | tf_op jit(solution)/shard_map/ppermute | solution.py:12
  28.6 11.8 %collective-permute-start.5 = (bf16[4,1,32,512]{3,2,0,1:T(8,128)(2,1)S(1)}, bf16[4,1,32,512]{3,2,0,1:T(8,128)(2,1)S(1)}, u32[]{:S(2)}, u32[]{:S(2)}) collective-permute-start(bf16[4,1,32,512]{3,2,0,1:T(8,128)(2,1)S(1)} %pad_maximum_fusion.13), channel_id=1, source_target_pairs={{4,0},{8,4},{12,8},{16,12},{20,16},{24,20},{28,24},{5,1},{9,5},{13... | collective-permute-start | bytes 393224 | tf_op jit(solution)/shard_map/ppermute | solution.py:23
  30.6 9.8 %collective-permute-start.4 = (bf16[4,1,32,512]{3,2,0,1:T(8,128)(2,1)S(1)}, bf16[4,1,32,512]{3,2,0,1:T(8,128)(2,1)S(1)}, u32[]{:S(2)}, u32[]{:S(2)}) collective-permute-start(bf16[4,1,32,512]{3,2,0,1:T(8,128)(2,1)S(1)} %pad_maximum_fusion.13), channel_id=1, source_target_pairs={{0,4},{4,8},{8,12},{12,16},{16,20},{20,24},{24,28},{1,5},{5,9},{9,... | collective-permute-start | bytes 393224 | tf_op jit(solution)/shard_map/ppermute | solution.py:22
  43.4 1.1 %copy-start.9 = (bf16[1,1,3,512,256]{4,3,2,1,0:T(8,128)(2,1)S(1)}, bf16[1,1,3,512,256]{4,3,2,1,0:T(8,128)(2,1)}, u32[]{:S(2)}) copy-start(bf16[1,1,3,512,256]{4,3,2,1,0:T(8,128)(2,1)} %get-tuple-element.14) | copy-start | bytes 2359300
  43.9 1.2 %copy-start.8 = (bf16[1,1,3,512,256]{4,3,2,1,0:T(8,128)(2,1)S(1)}, bf16[1,1,3,512,256]{4,3,2,1,0:T(8,128)(2,1)}, u32[]{:S(2)}) copy-start(bf16[1,1,3,512,256]{4,3,2,1,0:T(8,128)(2,1)} %get-tuple-element.13) | copy-start | bytes 2359300
  45.1 1.1 %copy-start.7 = (bf16[1,1,3,512,256]{4,3,2,1,0:T(8,128)(2,1)S(1)}, bf16[1,1,3,512,256]{4,3,2,1,0:T(8,128)(2,1)}, u32[]{:S(2)}) copy-start(bf16[1,1,3,512,256]{4,3,2,1,0:T(8,128)(2,1)} %get-tuple-element.12) | copy-start | bytes 2359300
  46.2 1.1 %copy-start.6 = (bf16[1,1,3,512,256]{4,3,2,1,0:T(8,128)(2,1)S(1)}, bf16[1,1,3,512,256]{4,3,2,1,0:T(8,128)(2,1)}, u32[]{:S(2)}) copy-start(bf16[1,1,3,512,256]{4,3,2,1,0:T(8,128)(2,1)} %get-tuple-element.11) | copy-start | bytes 2359300
  47.4 1.1 %copy-start.5 = (bf16[1,1,3,512,256]{4,3,2,1,0:T(8,128)(2,1)S(1)}, bf16[1,1,3,512,256]{4,3,2,1,0:T(8,128)(2,1)}, u32[]{:S(2)}) copy-start(bf16[1,1,3,512,256]{4,3,2,1,0:T(8,128)(2,1)} %get-tuple-element.10) | copy-start | bytes 2359300
  48.5 1.1 %copy-start.4 = (bf16[1,1,3,512,256]{4,3,2,1,0:T(8,128)(2,1)S(1)}, bf16[1,1,3,512,256]{4,3,2,1,0:T(8,128)(2,1)}, u32[]{:S(2)}) copy-start(bf16[1,1,3,512,256]{4,3,2,1,0:T(8,128)(2,1)} %get-tuple-element.9) | copy-start | bytes 2359300
  49.6 1.1 %copy-start.3 = (bf16[1,1,3,512,256]{4,3,2,1,0:T(8,128)(2,1)S(1)}, bf16[1,1,3,512,256]{4,3,2,1,0:T(8,128)(2,1)}, u32[]{:S(2)}) copy-start(bf16[1,1,3,512,256]{4,3,2,1,0:T(8,128)(2,1)} %get-tuple-element.8) | copy-start | bytes 2359300
  50.8 1.1 %copy-start.2 = (bf16[1,1,3,512,256]{4,3,2,1,0:T(8,128)(2,1)S(1)}, bf16[1,1,3,512,256]{4,3,2,1,0:T(8,128)(2,1)}, u32[]{:S(2)}) copy-start(bf16[1,1,3,512,256]{4,3,2,1,0:T(8,128)(2,1)} %get-tuple-element.15) | copy-start | bytes 2359300
  51.9 1.1 %copy-start.1 = (bf16[1,1,3,512,256]{4,3,2,1,0:T(8,128)(2,1)S(1)}, bf16[1,1,3,512,256]{4,3,2,1,0:T(8,128)(2,1)}, u32[]{:S(2)}) copy-start(bf16[1,1,3,512,256]{4,3,2,1,0:T(8,128)(2,1)} %get-tuple-element.7) | copy-start | bytes 2359300
  51.9 1.1 %copy-start.15 = (f32[256]{0:T(256)S(1)}, f32[256]{0:T(256)}, u32[]{:S(2)}) copy-start(f32[256]{0:T(256)} %param.14) | copy-start | bytes 3076
  53.0 0.7 copy-start.14
  53.5 16.7 %copy-start = (bf16[3,3,3,256,128]{4,3,2,1,0:T(8,128)(2,1)S(1)}, bf16[3,3,3,256,128]{4,3,2,1,0:T(8,128)(2,1)}, u32[]{:S(2)}) copy-start(bf16[3,3,3,256,128]{4,3,2,1,0:T(8,128)(2,1)} %param.16) | copy-start | bytes 5308420
  53.9 6.4 %collective-permute-start.6 = (bf16[2,2,64,256]{3,2,1,0:T(8,128)(2,1)S(1)}, bf16[2,2,64,256]{3,2,1,0:T(8,128)(2,1)S(1)}, u32[]{:S(2)}, u32[]{:S(2)}) collective-permute-start(bf16[2,2,64,256]{3,2,1,0:T(8,128)(2,1)S(1)} %multiply_convert_fusion), channel_id=1, source_target_pairs={{0,1},{1,2},{2,3},{4,5},{5,6},{6,7},{8,9},{9,10},{10,11},{12,13},{... | collective-permute-start | bytes 393224 | tf_op jit(solution)/shard_map/ppermute | solution.py:12
  60.3 7.8 %collective-permute-start.7 = (bf16[4,1,64,256]{3,2,1,0:T(8,128)(2,1)S(1)}, bf16[4,1,64,256]{3,2,1,0:T(8,128)(2,1)S(1)}, u32[]{:S(2)}, u32[]{:S(2)}) collective-permute-start(bf16[4,1,64,256]{3,2,1,0:T(8,128)(2,1)S(1)} %pad_maximum_fusion.12), channel_id=1, source_target_pairs={{0,4},{4,8},{8,12},{12,16},{16,20},{20,24},{24,28},{1,5},{5,9},{9,... | collective-permute-start | bytes 393224 | tf_op jit(solution)/shard_map/ppermute | solution.py:22
  68.1 6.9 %collective-permute-start.8 = (bf16[4,1,64,256]{3,2,1,0:T(8,128)(2,1)S(1)}, bf16[4,1,64,256]{3,2,1,0:T(8,128)(2,1)S(1)}, u32[]{:S(2)}, u32[]{:S(2)}) collective-permute-start(bf16[4,1,64,256]{3,2,1,0:T(8,128)(2,1)S(1)} %get-tuple-element.6), channel_id=1, source_target_pairs={{4,0},{8,4},{12,8},{16,12},{20,16},{24,20},{28,24},{5,1},{9,5},{13... | collective-permute-start | bytes 393224 | tf_op jit(solution)/shard_map/ppermute | solution.py:23
  84.0 2.3 %copy-start.11 = (bf16[1,1,3,256,128]{4,3,2,1,0:T(8,128)(2,1)S(1)}, bf16[1,1,3,256,128]{4,3,2,1,0:T(8,128)(2,1)}, u32[]{:S(2)}) copy-start(bf16[1,1,3,256,128]{4,3,2,1,0:T(8,128)(2,1)} %get-tuple-element.35) | copy-start | bytes 589828
  86.4 0.9 %copy-start.10 = (bf16[1,1,3,256,128]{4,3,2,1,0:T(8,128)(2,1)S(1)}, bf16[1,1,3,256,128]{4,3,2,1,0:T(8,128)(2,1)}, u32[]{:S(2)}) copy-start(bf16[1,1,3,256,128]{4,3,2,1,0:T(8,128)(2,1)} %get-tuple-element.34) | copy-start | bytes 589828
  90.8 0.7 copy-start.16
where the time goes:
time: 93.6 us; the launch traced here: 92.7 us
  starting transfers between devices  26.3 us (28%)
  waiting for transfers between devices  24.5 us (26%)
  local copies, waits for them, and re-layouts  23.4 us (25%)
  matrix products  11.5 us (12%)
  other arithmetic  6.45 us (7%)
    dot_general x27, matrix products, conv_taps(): jnp.einsum('abcd,de->abce', stacked, matrix, preferred_element_type=jnp.f...  11.5 us
    ppermute x3, waiting for transfers between devices, passed_along(): return lax.ppermute(array, axis, pairs)  11 us
    ppermute x3, starting transfers between devices, padded_2(): before = lax.ppermute(last, axis, up)  9.41 us
    ppermute x3, waiting for transfers between devices, padded_2(): before = lax.ppermute(last, axis, up)  8.94 us
    slice x3, local copies, waits for them, and re-layouts, conv_taps(): matrix = kernel[time_tap, row_tap].reshape(3 * in_channels, out_channels)  7.8 us
    ppermute x3, starting transfers between devices, padded_2(): after = lax.ppermute(first, axis, down)  7.31 us
    unnamed x34, local copies, waits for them, and re-layouts  6.51 us
    ppermute x3, starting transfers between devices, passed_along(): return lax.ppermute(array, axis, pairs)  5.89 us
  transfers between devices with their start and end apart: 10, of which 7 were waited for; matrix products, arithmetic and copies ran while one was open for 9% of the time, Pallas kernels for 0%

commit v1 on v0

v1 whole, which is shorter than its diff:
```python
import functools

import jax
import jax.numpy as jnp
from jax import lax
from jax.experimental import pallas as pl
from jax.experimental.pallas import tpu as pltpu
from jax.sharding import PartitionSpec as P

F32, BF16 = jnp.float32, jnp.bfloat16
AXES = ("seq", "tm")


def hop(array, partner, seq, tm):
    pairs = []
    for s in range(seq):
        for t in range(tm):
            s2, t2 = partner(s, t)
            pairs.append((s * tm + t, s2 * tm + t2))
    return lax.ppermute(array, AXES, pairs)


def gathered_pieces(latent):
    seq, tm = lax.axis_size("seq"), lax.axis_size("tm")
    assert seq % 2 == 0 and tm == 4

    def z_partner(first):
        def partner(s, t):
            z = s // 2
            other = z + 1 if (z - first) % 2 == 0 else z - 1
            return (s + 2 * (other - z), t ^ 1) if 0 <= other < seq // 2 else (s, t ^ 1)

        return partner

    held = latent[None]
    held = jnp.concatenate([held, hop(held, lambda s, t: (s, t ^ 3), seq, tm)])
    held = jnp.concatenate([held, hop(held, lambda s, t: (s ^ 1, t ^ 1), seq, tm)])
    even = hop(held, z_partner(0), seq, tm)
    odd = hop(held, z_partner(1), seq, tm)
    held = jnp.concatenate([held, even, odd])
    return jnp.concatenate([held, hop(held, lambda s, t: (s, t ^ 1), seq, tm)])


def silu(v):
    return 0.5 * v * (1.0 + jnp.tanh(0.5 * v))


def normed(hidden, gain):
    factor = lax.rsqrt(jnp.mean(hidden * hidden, axis=-1, keepdims=True) + 1e-06)
    return silu(hidden * factor * gain).astype(BF16)


def decode_kernel(
    rows_total,
    pieces,
    w1,
    b1,
    g1,
    w2,
    b2,
    g2,
    w3,
    b3,
    out,
    rolled,
    rolled_far,
    patches,
    first_act,
    partial,
    second_act,
    final,
    line,
):
    s = lax.axis_index("seq")
    t = lax.axis_index("tm")
    z, x, y, c = s // 2, s % 2, t // 2, t % 2
    n_frames = pieces.shape[1]

    def piece_of(row, chunk):
        dz, dx = row // 2 - z, row % 2 ^ x
        dy, dc = chunk // 2 ^ y, chunk % 2 ^ c
        group = jnp.where(dz == 0, 0, jnp.where((dz == 1) == (z % 2 == 0), 1, 2))
        half = (dx + dy + dc + jnp.where(dz == 0, 0, 1)) % 2
        return half * 12 + group * 4 + 2 * dx + dy

    lane = lax.broadcasted_iota(jnp.int32, (n_frames, 128), 1)

    def one_row(d, _):
        row = jnp.clip(s - 2 + d, 0, rows_total - 1)
        chunks = [pieces[piece_of(row, chunk)].astype(F32) for chunk in range(4)]
        for chunk in range(4):
            for q in range(8):
                shift = (16 - 16 * q) % 128
                near = pltpu.roll(chunks[chunk], shift, 1) if shift else chunks[chunk]
                if q == 0:
                    before = pltpu.roll(chunks[chunk - 1], 16, 1) if chunk else chunks[0]
                    near = jnp.where(lane < 16, before, near)
                if q == 7:
                    after = chunks[chunk + 1] if chunk < 3 else chunks[3]
                    after = pltpu.roll(after, 32 if chunk < 3 else 48, 1)
                    near = jnp.where((lane >= 32) & (lane < 48), after, near)
                at = pl.ds(d * n_frames * 32 + 8 * chunk + q, n_frames, stride=32)
                rolled[at, :] = near
                rolled_far[at, :] = pltpu.roll(near, 64, 1)
        return 0

    lax.fori_loop(0, 5, one_row, 0)

    left = lax.broadcasted_iota(jnp.int32, (32, 128), 1) < 64

    def one_patch(r, _):
        mine = jnp.clip(s - 1 + r, 0, rows_total - 1)
        d = [jnp.clip(mine - 1 + j, 0, rows_total - 1) - (s - 2) for j in range(3)]
        for w in range(8):
            frame = jnp.maximum(2 * t - 6 + w, 0)
            at = [pl.ds(pl.multiple_of((d[j] * n_frames + frame) * 32, 32), 32) for j in range(3)]
            pair = jnp.where(left, rolled[at[0], :], rolled_far[at[1], :])
            patches[r, w, :, :128] = pair.astype(BF16)
            patches[r, w, :, 128:] = rolled[at[2], :].astype(BF16)
        return 0

    lax.fori_loop(0, 3, one_patch, 0)

    def first(r, _):
        lhs = jnp.concatenate([patches[r, i : i + 6].reshape(192, 256) for i in range(3)], axis=1)
        hidden = jnp.dot(lhs, w1[...], preferred_element_type=F32) + b1[...]
        first_act[r] = normed(hidden, g1[...]).reshape(6, 32, 512)
        return 0

    lax.fori_loop(0, 3, first, 0)

    def second(k, _):
        def lhs(rows):
            m = (rows.stop - rows.start) * 128
            return [first_act[rows, i : i + 4].reshape(m, 512) for i in range(3)]

        edge = jnp.dot(
            jnp.concatenate(lhs(slice(0, 2)) + lhs(slice(1, 3)), axis=1),
            jnp.concatenate([w2[i, j, k] for j in (0, 2) for i in range(3)], axis=0),
            preferred_element_type=F32,
        )
        middle = jnp.dot(
            jnp.concatenate(lhs(slice(0, 3)), axis=1),
            jnp.concatenate([w2[i, 1, k] for i in range(3)], axis=0),
            preferred_element_type=F32,
        )
        for p in range(4):
            e, m = p // 2, (p + 1) // 2
            partial[k, p] = edge[e * 128 : (e + 1) * 128] + middle[m * 128 : (m + 1) * 128]
        return 0

    lax.fori_loop(0, 3, second, 0)

    column = lax.broadcasted_iota(jnp.int32, (4, 32, 256), 1)

    def second_norm(p, _):
        a, b, d = [partial[k, p].reshape(4, 32, 256) for k in range(3)]
        a_left = jnp.where(column == 0, a, pltpu.roll(a, 1, 1))
        d_right = jnp.where(column == 31, d, pltpu.roll(d, 31, 1))
        second_act[p, 0] = normed(a_left + b + d + b2[...], g2[...])
        second_act[p, 1] = normed(a + b + d_right + b2[...], g2[...])
        return 0

    lax.fori_loop(0, 4, second_norm, 0)

    def lhs3(rows):
        m = (rows.stop - rows.start) * 128
        return [second_act[rows, :, i : i + 2].reshape(m, 256) for i in range(3)]

    def taps(j):
        return jnp.concatenate(
            [jnp.concatenate([w3[i, j, k] for k in range(3)], axis=1) for i in range(3)], axis=0
        )

    edge = jnp.dot(
        jnp.concatenate(lhs3(slice(0, 3)) + lhs3(slice(1, 4)), axis=1),
        jnp.concatenate([taps(0), taps(2)], axis=0),
        preferred_element_type=F32,
    )
    middle = jnp.dot(
        jnp.concatenate(lhs3(slice(1, 3)), axis=1), taps(1), preferred_element_type=F32
    )
    for r in range(4):
        e, m = (r + 1) // 2, r // 2
        final[r] = edge[e * 128 : (e + 1) * 128] + middle[m * 128 : (m + 1) * 128]

    narrow = lax.broadcasted_iota(jnp.int32, (32, 128), 0)

    def last(r, _):
        def part(q, g, k):
            return final[r, pl.ds((q * 2 + g) * 32, 32), k * 128 : (k + 1) * 128]

        for g in range(2):
            a0, a1, b0, b1_, d0, d1 = [part(q, g, k) for k in range(3) for q in range(2)]
            a_left = jnp.where(narrow == 0, a0, pltpu.roll(a1, 1, 0))
            d_right = jnp.where(narrow == 31, d1, pltpu.roll(d0, 31, 0))
            columns = (a_left + b0 + d0, a0 + b0 + d1, a0 + b1_ + d1, a1 + b1_ + d_right)
            for u, value in enumerate(columns):
                line[g, pl.ds(u, 32, stride=4), :] = value + b3[...]
            out[g, r] = line[g].astype(BF16)
        return 0

    lax.fori_loop(0, 4, last, 0)


def per_device(latent, k1, b1, g1, k2, b2, g2, k3, b3):
    frames, lanes = latent.shape
    tm = lax.axis_size("tm")
    rows_total = lax.axis_size("seq")
    c1, c2, c3 = k1.shape[4], k2.shape[4], k3.shape[4]
    pieces = gathered_pieces(latent)
    w1 = jnp.pad(k1.reshape(3, 3, 48, c1), ((0, 0), (0, 0), (0, 16), (0, 0)))
    w1 = jnp.pad(w1.reshape(3, 192, c1), ((0, 0), (0, 64), (0, 0))).reshape(768, c1)
    vmem = pl.BlockSpec(memory_space=pltpu.VMEM)
    out_frames = frames // tm
    return pl.pallas_call(
        functools.partial(decode_kernel, rows_total),
        out_shape=jax.ShapeDtypeStruct((out_frames, 4, 128, c3), BF16),
        in_specs=[vmem] * 9,
        out_specs=vmem,
        scratch_shapes=[
            pltpu.VMEM((5 * frames * 32, 128), F32),
            pltpu.VMEM((5 * frames * 32, 128), F32),
            pltpu.VMEM((3, 8, 32, 256), BF16),
            pltpu.VMEM((3, 6, 32, c1), BF16),
            pltpu.VMEM((3, 4, 128, c2), F32),
            pltpu.VMEM((4, 2, 4, 32, c2), BF16),
            pltpu.VMEM((4, 128, 3 * c3), F32),
            pltpu.VMEM((2, 128, c3), F32),
        ],
        compiler_params=pltpu.CompilerParams(vmem_limit_bytes=32 * 1024 * 1024),
        cost_estimate=pl.CostEstimate(
            flops=4_000_000_000, bytes_accessed=10_000_000, transcendentals=600_000
        ),
    )(
        pieces,
        w1,
        b1.reshape(1, c1),
        g1.reshape(1, c1),
        pltpu.with_memory_space_constraint(k2, pltpu.VMEM),
        b2.reshape(1, c2),
        g2.reshape(1, c2),
        pltpu.with_memory_space_constraint(k3, pltpu.VMEM),
        b3.reshape(1, c3),
    )


def solution(mesh):
    placed = (P(None, AXES), P(), P(), P(), P(), P(), P(), P(), P())
    return jax.shard_map(
        per_device,
        mesh=mesh,
        in_specs=placed,
        out_specs=P("tm", "seq", None, None),
        check_vma=False,
    )
```

time: 93.6 us -> 30.8 us (0.33)
  the two profiles are of different devices: /device:TPU:12 before, /device:TPU:0 now
where the time goes in v1:
time: 30.8 us; the launch traced here: 30.4 us
  local copies, waits for them, and re-layouts  9.72 us (32%)
  Pallas kernels  7.9 us (26%)
  starting transfers between devices  7.88 us (26%)
  waiting for transfers between devices  3.5 us (11%)
  other arithmetic  1.37 us (4%)
    unnamed x18, local copies, waits for them, and re-layouts  8.59 us
    pallas_call x1, Pallas kernels, per_device(): pl.pallas_call(functools.partial(decode_kernel, rows_total), out_shape=ja...  7.9 us
    ppermute x5, starting transfers between devices, hop(): return lax.ppermute(array, AXES, pairs)  7.88 us
    ppermute x5, waiting for transfers between devices, hop(): return lax.ppermute(array, AXES, pairs)  3.5 us
    pad x1, local copies, waits for them, and re-layouts, per_device(): w1 = jnp.pad(k1.reshape(3, 3, 48, c1), ((0, 0), (0, 0), (0, 16), (0, 0)))  1.06 us
    concatenate x1, other arithmetic, gathered_pieces(): jnp.concatenate([held, hop(held, lambda s, t: (s ^ 1, t ^ 1), seq, tm)])  0.69 us
    concatenate x1, other arithmetic, gathered_pieces(): held = jnp.concatenate([held, hop(held, lambda s, t: (s, t ^ 3), seq, tm)])  0.69 us
  transfers between devices with their start and end apart: 5, of which 3 were waited for; matrix products, arithmetic and copies ran while one was open for 6% of the time, Pallas kernels for 0%

profile of v1, /device:TPU:0, one launch (start us, length us, event | category | flops | bytes accessed | tf_op | source)
XLA Modules:
  0.0 30.4 jit_solution(5124566058605104951)
XLA Ops:
  0.0 2.4 %collective-permute-start = (bf16[1,8,128]{2,1,0:T(8,128)(2,1)}, bf16[1,8,128]{2,1,0:T(8,128)(2,1)S(1)}, u32[]{:S(2)}, u32[]{:S(2)}) collective-permute-start(bf16[1,8,128]{2,1,0:T(8,128)(2,1)} %bitcast.19), channel_id=1, source_target_pairs={{0,3},{1,2},{2,1},{3,0},{4,7},{5,6},{6,5},{7,4},{8,11},{9,10},{10,... | collective-permute-start | bytes 6152 | tf_op jit(solution)/shard_map/ppermute | solution.py:20
  2.4 0.7 %constant_dynamic-update-slice_fusion.4 = (bf16[12,8,128]{2,1,0:T(8,128)(2,1)S(1)}, bf16[24,8,128]{2,1,0:T(8,128)(2,1)S(1)}) fusion(bf16[8,128]{1,0:T(8,128)(2,1)} %param.9), kind=kLoop, calls=%fused_computation.4 | loop fusion | bytes 6144
  3.1 0.8 %collective-permute-done = bf16[1,8,128]{2,1,0:T(8,128)(2,1)S(1)} collective-permute-done((bf16[1,8,128]{2,1,0:T(8,128)(2,1)}, bf16[1,8,128]{2,1,0:T(8,128)(2,1)S(1)}, u32[]{:S(2)}, u32[]{:S(2)}) %collective-permute-start) | collective-permute-done | bytes 2080 | tf_op jit(solution)/shard_map/ppermute | solution.py:20
  3.9 0.7 %pad_maximum_fusion.1 = bf16[2,8,128]{2,1,0:T(8,128)(2,1)S(1)} fusion(bf16[1,8,128]{2,1,0:T(8,128)(2,1)S(1)} %collective-permute-done, bf16[1,8,128]{2,1,0:T(8,128)(2,1)} %bitcast.20), kind=kLoop, calls=%fused_computation.12 | loop fusion | flops 2048 | bytes 8192 | tf_op jit(solution)/shard_map/concatenate | solution.py:36
  4.6 2.0 %collective-permute-start.1 = (bf16[2,8,128]{2,1,0:T(8,128)(2,1)S(1)}, bf16[2,8,128]{2,1,0:T(8,128)(2,1)S(1)}, u32[]{:S(2)}, u32[]{:S(2)}) collective-permute-start(bf16[2,8,128]{2,1,0:T(8,128)(2,1)S(1)} %pad_maximum_fusion.1), channel_id=1, source_target_pairs={{0,5},{1,4},{2,7},{3,6},{4,1},{5,0},{6,3},{7,2},{8,13},{9,12},{10,... | collective-permute-start | bytes 12296 | tf_op jit(solution)/shard_map/ppermute | solution.py:20
  6.6 1.3 %collective-permute-done.1 = bf16[2,8,128]{2,1,0:T(8,128)(2,1)S(1)} collective-permute-done((bf16[2,8,128]{2,1,0:T(8,128)(2,1)S(1)}, bf16[2,8,128]{2,1,0:T(8,128)(2,1)S(1)}, u32[]{:S(2)}, u32[]{:S(2)}) %collective-permute-start.1) | collective-permute-done | bytes 4128 | tf_op jit(solution)/shard_map/ppermute | solution.py:20
  7.9 0.7 %pad_maximum_fusion = bf16[4,8,128]{2,1,0:T(8,128)(2,1)S(1)} fusion(bf16[2,8,128]{2,1,0:T(8,128)(2,1)S(1)} %collective-permute-done.1, bf16[1,8,128]{2,1,0:T(8,128)(2,1)S(1)} %collective-permute-done, bf16[1,8,128]{2,1,0:T(8,128)(2,1)} %bitcast.21), kind=kLoop, calls=%fused_computation.11 | loop fusion | flops 8192 | bytes 16384 | tf_op jit(solution)/shard_map/concatenate | solution.py:37
  8.6 0.4 %collective-permute-start.3 = (bf16[4,8,128]{2,1,0:T(8,128)(2,1)S(1)}, bf16[4,8,128]{2,1,0:T(8,128)(2,1)S(1)}, u32[]{:S(2)}, u32[]{:S(2)}) collective-permute-start(bf16[4,8,128]{2,1,0:T(8,128)(2,1)S(1)} %pad_maximum_fusion), channel_id=1, source_target_pairs={{0,1},{1,0},{2,3},{3,2},{4,5},{5,4},{6,7},{7,6},{8,17},{9,16},{10,... | collective-permute-start | bytes 24584 | tf_op jit(solution)/shard_map/ppermute | solution.py:20
  9.0 3.0 %collective-permute-start.2 = (bf16[4,8,128]{2,1,0:T(8,128)(2,1)S(1)}, bf16[4,8,128]{2,1,0:T(8,128)(2,1)S(1)}, u32[]{:S(2)}, u32[]{:S(2)}) collective-permute-start(bf16[4,8,128]{2,1,0:T(8,128)(2,1)S(1)} %pad_maximum_fusion), channel_id=1, source_target_pairs={{0,9},{1,8},{2,11},{3,10},{4,13},{5,12},{6,15},{7,14},{8,1},{9,0},... | collective-permute-start | bytes 24584 | tf_op jit(solution)/shard_map/ppermute | solution.py:20
  12.0 1.4 %collective-permute-done.2 = bf16[4,8,128]{2,1,0:T(8,128)(2,1)S(1)} collective-permute-done((bf16[4,8,128]{2,1,0:T(8,128)(2,1)S(1)}, bf16[4,8,128]{2,1,0:T(8,128)(2,1)S(1)}, u32[]{:S(2)}, u32[]{:S(2)}) %collective-permute-start.2) | collective-permute-done | bytes 8224 | tf_op jit(solution)/shard_map/ppermute | solution.py:20
  13.4 0.0 collective-permute-done.3
  13.4 0.1 collective-permute-start.4
  13.5 1.1 %pad.8 = bf16[3,3,64,512]{3,2,1,0:T(8,128)(2,1)S(1)} pad(bf16[3,3,48,512]{3,2,1,0:T(8,128)(2,1)} %bitcast.18, bf16[]{:T(256)} %constant.2.clone.1), padding=0_0x0_0x0_16x0_0 | pad | bytes 1032194 | tf_op jit(solution)/shard_map/jit(_pad)/pad | solution.py:212
  14.6 0.1 pad.9
  14.6 0.0 collective-permute-done.4
  14.6 0.0 copy-start
  14.7 3.0 %copy-done = bf16[3,3,3,512,256]{4,3,2,1,0:T(8,128)(2,1)S(1)} copy-done((bf16[3,3,3,512,256]{4,3,2,1,0:T(8,128)(2,1)S(1)}, bf16[3,3,3,512,256]{4,3,2,1,0:T(8,128)(2,1)}, u32[]{:S(2)}) %copy-start) | copy-done | bytes 7077912
  17.7 0.0 copy-start.1
  17.7 1.5 %copy-done.1 = bf16[3,3,3,256,128]{4,3,2,1,0:T(8,128)(2,1)S(1)} copy-done((bf16[3,3,3,256,128]{4,3,2,1,0:T(8,128)(2,1)S(1)}, bf16[3,3,3,256,128]{4,3,2,1,0:T(8,128)(2,1)}, u32[]{:S(2)}) %copy-start.1) | copy-done | bytes 1769496
  19.1 0.0 copy-start.2
  19.1 0.7 %copy-done.2 = f32[512]{0:T(512)S(1)} copy-done((f32[512]{0:T(512)S(1)}, f32[512]{0:T(512)}, u32[]{:S(2)}) %copy-start.2) | copy-done | bytes 2072
  19.8 0.0 copy-start.3
  19.8 0.7 %copy-done.3 = f32[512]{0:T(512)S(1)} copy-done((f32[512]{0:T(512)S(1)}, f32[512]{0:T(512)}, u32[]{:S(2)}) %copy-start.3) | copy-done | bytes 2072
  20.5 0.0 copy-start.4
  20.5 0.7 %copy-done.4 = f32[256]{0:T(256)S(1)} copy-done((f32[256]{0:T(256)S(1)}, f32[256]{0:T(256)}, u32[]{:S(2)}) %copy-start.4) | copy-done | bytes 1048
  21.2 0.0 copy-start.5
  21.2 0.7 %copy-done.5 = f32[256]{0:T(256)S(1)} copy-done((f32[256]{0:T(256)S(1)}, f32[256]{0:T(256)}, u32[]{:S(2)}) %copy-start.5) | copy-done | bytes 1048
  21.9 0.0 copy-start.6
  21.9 0.7 %copy-done.6 = f32[128]{0:T(128)S(1)} copy-done((f32[128]{0:T(128)S(1)}, f32[128]{0:T(128)}, u32[]{:S(2)}) %copy-start.6) | copy-done | bytes 536
  22.5 7.9 %shard_map.91 = bf16[2,4,128,128]{3,2,1,0:T(8,128)(2,1)} custom-call(bf16[24,8,128]{2,1,0:T(8,128)(2,1)S(1)} %constant_dynamic-update-slice_fusion.5.pieces, bf16[768,512]{1,0:T(8,128)(2,1)S(1)} %bitcast.11, f32[1,512]{1,0:T(1,128)S(1)} %bitcast.12, f32[1,512]{1,0:T(1,128)S(1)} %bitcast.13, bf16[3,3,3,512,256]{4,3,2,1,0:T(8,128)(2,1)S(1)} %copy-done, ...), custom_call_target="tpu_custom_call" | custom-call | flops 4000000000 | bytes 10000000 | tf_op jit(solution)/shard_map/pallas_call | solution.py:216
  (5 shorter events, 0.0 us)
Async XLA Ops:
  0.0 3.9 %collective-permute-start = (bf16[1,8,128]{2,1,0:T(8,128)(2,1)}, bf16[1,8,128]{2,1,0:T(8,128)(2,1)S(1)}, u32[]{:S(2)}, u32[]{:S(2)}) collective-permute-start(bf16[1,8,128]{2,1,0:T(8,128)(2,1)} %bitcast.19), channel_id=1, source_target_pairs={{0,3},{1,2},{2,1},{3,0},{4,7},{5,6},{6,5},{7,4},{8,11},{9,10},{10,... | collective-permute-start | bytes 6152 | tf_op jit(solution)/shard_map/ppermute | solution.py:20
  4.6 3.3 %collective-permute-start.1 = (bf16[2,8,128]{2,1,0:T(8,128)(2,1)S(1)}, bf16[2,8,128]{2,1,0:T(8,128)(2,1)S(1)}, u32[]{:S(2)}, u32[]{:S(2)}) collective-permute-start(bf16[2,8,128]{2,1,0:T(8,128)(2,1)S(1)} %pad_maximum_fusion.1), channel_id=1, source_target_pairs={{0,5},{1,4},{2,7},{3,6},{4,1},{5,0},{6,3},{7,2},{8,13},{9,12},{10,... | collective-permute-start | bytes 12296 | tf_op jit(solution)/shard_map/ppermute | solution.py:20
  8.6 4.8 %collective-permute-start.3 = (bf16[4,8,128]{2,1,0:T(8,128)(2,1)S(1)}, bf16[4,8,128]{2,1,0:T(8,128)(2,1)S(1)}, u32[]{:S(2)}, u32[]{:S(2)}) collective-permute-start(bf16[4,8,128]{2,1,0:T(8,128)(2,1)S(1)} %pad_maximum_fusion), channel_id=1, source_target_pairs={{0,1},{1,0},{2,3},{3,2},{4,5},{5,4},{6,7},{7,6},{8,17},{9,16},{10,... | collective-permute-start | bytes 24584 | tf_op jit(solution)/shard_map/ppermute | solution.py:20
  9.0 4.4 %collective-permute-start.2 = (bf16[4,8,128]{2,1,0:T(8,128)(2,1)S(1)}, bf16[4,8,128]{2,1,0:T(8,128)(2,1)S(1)}, u32[]{:S(2)}, u32[]{:S(2)}) collective-permute-start(bf16[4,8,128]{2,1,0:T(8,128)(2,1)S(1)} %pad_maximum_fusion), channel_id=1, source_target_pairs={{0,9},{1,8},{2,11},{3,10},{4,13},{5,12},{6,15},{7,14},{8,1},{9,0},... | collective-permute-start | bytes 24584 | tf_op jit(solution)/shard_map/ppermute | solution.py:20
  13.4 1.3 %collective-permute-start.4 = (bf16[12,8,128]{2,1,0:T(8,128)(2,1)S(1)}, bf16[12,8,128]{2,1,0:T(8,128)(2,1)S(1)}, u32[]{:S(2)}, u32[]{:S(2)}) collective-permute-start(bf16[12,8,128]{2,1,0:T(8,128)(2,1)S(1)} %get-tuple-element.5), channel_id=1, source_target_pairs={{0,1},{1,0},{2,3},{3,2},{4,5},{5,4},{6,7},{7,6},{8,9},{9,8},{10,11... | collective-permute-start | bytes 73736 | tf_op jit(solution)/shard_map/ppermute | solution.py:20
  14.6 3.0 %copy-start = (bf16[3,3,3,512,256]{4,3,2,1,0:T(8,128)(2,1)S(1)}, bf16[3,3,3,512,256]{4,3,2,1,0:T(8,128)(2,1)}, u32[]{:S(2)}) copy-start(bf16[3,3,3,512,256]{4,3,2,1,0:T(8,128)(2,1)} %w2.1) | copy-start | bytes 21233668
  17.7 1.5 %copy-start.1 = (bf16[3,3,3,256,128]{4,3,2,1,0:T(8,128)(2,1)S(1)}, bf16[3,3,3,256,128]{4,3,2,1,0:T(8,128)(2,1)}, u32[]{:S(2)}) copy-start(bf16[3,3,3,256,128]{4,3,2,1,0:T(8,128)(2,1)} %w3.1) | copy-start | bytes 5308420
  19.1 0.7 %copy-start.2 = (f32[512]{0:T(512)S(1)}, f32[512]{0:T(512)}, u32[]{:S(2)}) copy-start(f32[512]{0:T(512)} %param.11) | copy-start | bytes 6148
  19.8 0.7 %copy-start.3 = (f32[512]{0:T(512)S(1)}, f32[512]{0:T(512)}, u32[]{:S(2)}) copy-start(f32[512]{0:T(512)} %param.12) | copy-start | bytes 6148
  20.5 0.7 %copy-start.4 = (f32[256]{0:T(256)S(1)}, f32[256]{0:T(256)}, u32[]{:S(2)}) copy-start(f32[256]{0:T(256)} %param.14) | copy-start | bytes 3076
  21.2 0.7 %copy-start.5 = (f32[256]{0:T(256)S(1)}, f32[256]{0:T(256)}, u32[]{:S(2)}) copy-start(f32[256]{0:T(256)} %param.15) | copy-start | bytes 3076
  21.9 0.7 %copy-start.6 = (f32[128]{0:T(128)S(1)}, f32[128]{0:T(128)}, u32[]{:S(2)}) copy-start(f32[128]{0:T(128)} %param.17) | copy-start | bytes 1540

commit v2 on v1

--- a/solution.py
+++ b/solution.py
@@ -32,13 +32,14 @@
 
         return partner
 
-    held = latent[None]
-    held = jnp.concatenate([held, hop(held, lambda s, t: (s, t ^ 3), seq, tm)])
+    beside = hop(latent[None], lambda s, t: (s, t ^ 3), seq, tm)
+    own = lax.optimization_barrier(jnp.concatenate([latent[None], jnp.zeros_like(latent)[None]]))
+    held = lax.dynamic_update_slice_in_dim(own, beside, 1, 0)
     held = jnp.concatenate([held, hop(held, lambda s, t: (s ^ 1, t ^ 1), seq, tm)])
     even = hop(held, z_partner(0), seq, tm)
     odd = hop(held, z_partner(1), seq, tm)
     held = jnp.concatenate([held, even, odd])
-    return jnp.concatenate([held, hop(held, lambda s, t: (s, t ^ 1), seq, tm)])
+    return held, hop(held, lambda s, t: (s, t ^ 1), seq, tm)
 
 
 def silu(v):
@@ -52,16 +53,18 @@
 
 def decode_kernel(
     rows_total,
+    held,
+    received,
+    k1,
+    b1_in,
+    g1_in,
+    k2,
+    b2_in,
+    g2_in,
+    k3,
+    b3_in,
+    out_hbm,
     pieces,
-    w1,
-    b1,
-    g1,
-    w2,
-    b2,
-    g2,
-    w3,
-    b3,
-    out,
     rolled,
     rolled_far,
     patches,
@@ -70,11 +73,48 @@
     second_act,
     final,
     line,
+    out,
+    w1,
+    w2,
+    w3,
+    b1,
+    g1,
+    b2,
+    g2,
+    b3,
+    sem1,
+    sem2,
+    sem3,
+    sem_small,
+    sem_out,
 ):
+    loads1 = []
+    for i in range(3):
+        for j in range(3):
+            target = w1.at[pl.ds(i * 256 + j * 64, 48)]
+            loads1.append(pltpu.make_async_copy(k1.at[i, j], target, sem1.at[i * 3 + j]))
+    small = [
+        pltpu.make_async_copy(a, b, sem_small.at[n])
+        for n, (a, b) in enumerate(
+            [(b1_in, b1), (g1_in, g1), (b2_in, b2), (g2_in, g2), (b3_in, b3)]
+        )
+    ]
+    loads2 = [
+        pltpu.make_async_copy(k2.at[:, :, k], w2.at[k], sem2.at[k]) for k in range(3)
+    ]
+    load3 = pltpu.make_async_copy(k3, w3, sem3)
+    for copy in loads1 + small + loads2 + [load3]:
+        copy.start()
+    for i in range(3):
+        for start, size in ((48, 16), (112, 16), (176, 80)):
+            w1[pl.ds(i * 256 + start, size), :] = jnp.zeros((size, w1.shape[1]), BF16)
+
     s = lax.axis_index("seq")
     t = lax.axis_index("tm")
     z, x, y, c = s // 2, s % 2, t // 2, t % 2
-    n_frames = pieces.shape[1]
+    n_frames = held.shape[1]
+    pieces[:12] = held[...].astype(F32)
+    pieces[12:] = received[...].astype(F32)
 
     def piece_of(row, chunk):
         dz, dx = row // 2 - z, row % 2 ^ x
@@ -87,7 +127,7 @@
 
     def one_row(d, _):
         row = jnp.clip(s - 2 + d, 0, rows_total - 1)
-        chunks = [pieces[piece_of(row, chunk)].astype(F32) for chunk in range(4)]
+        chunks = [pieces[piece_of(row, chunk)] for chunk in range(4)]
         for chunk in range(4):
             for q in range(8):
                 shift = (16 - 16 * q) % 128
@@ -121,6 +161,9 @@
 
     lax.fori_loop(0, 3, one_patch, 0)
 
+    for copy in loads1 + small:
+        copy.wait()
+
     def first(r, _):
         lhs = jnp.concatenate([patches[r, i : i + 6].reshape(192, 256) for i in range(3)], axis=1)
         hidden = jnp.dot(lhs, w1[...], preferred_element_type=F32) + b1[...]
@@ -130,18 +173,20 @@
     lax.fori_loop(0, 3, first, 0)
 
     def second(k, _):
+        pltpu.make_async_copy(k2.at[:, :, k], w2.at[k], sem2.at[k]).wait()
+
         def lhs(rows):
             m = (rows.stop - rows.start) * 128
             return [first_act[rows, i : i + 4].reshape(m, 512) for i in range(3)]
 
         edge = jnp.dot(
             jnp.concatenate(lhs(slice(0, 2)) + lhs(slice(1, 3)), axis=1),
-            jnp.concatenate([w2[i, j, k] for j in (0, 2) for i in range(3)], axis=0),
+            jnp.concatenate([w2[k, i, j] for j in (0, 2) for i in range(3)], axis=0),
             preferred_element_type=F32,
         )
         middle = jnp.dot(
             jnp.concatenate(lhs(slice(0, 3)), axis=1),
-            jnp.concatenate([w2[i, 1, k] for i in range(3)], axis=0),
+            jnp.concatenate([w2[k, i, 1] for i in range(3)], axis=0),
             preferred_element_type=F32,
         )
         for p in range(4):
@@ -162,6 +207,8 @@
         return 0
 
     lax.fori_loop(0, 4, second_norm, 0)
+
+    load3.wait()
 
     def lhs3(rows):
         m = (rows.stop - rows.start) * 128
@@ -198,9 +245,12 @@
             for u, value in enumerate(columns):
                 line[g, pl.ds(u, 32, stride=4), :] = value + b3[...]
             out[g, r] = line[g].astype(BF16)
+        pltpu.make_async_copy(out.at[:, r], out_hbm.at[:, r], sem_out.at[r]).start()
         return 0
 
     lax.fori_loop(0, 4, last, 0)
+    for r in range(4):
+        pltpu.make_async_copy(out.at[:, r], out_hbm.at[:, r], sem_out.at[r]).wait()
 
 
 def per_device(latent, k1, b1, g1, k2, b2, g2, k3, b3):
@@ -208,17 +258,17 @@
     tm = lax.axis_size("tm")
     rows_total = lax.axis_size("seq")
     c1, c2, c3 = k1.shape[4], k2.shape[4], k3.shape[4]
-    pieces = gathered_pieces(latent)
-    w1 = jnp.pad(k1.reshape(3, 3, 48, c1), ((0, 0), (0, 0), (0, 16), (0, 0)))
-    w1 = jnp.pad(w1.reshape(3, 192, c1), ((0, 0), (0, 64), (0, 0))).reshape(768, c1)
+    held, received = gathered_pieces(latent)
     vmem = pl.BlockSpec(memory_space=pltpu.VMEM)
+    hbm = pl.BlockSpec(memory_space=pltpu.HBM)
     out_frames = frames // tm
     return pl.pallas_call(
         functools.partial(decode_kernel, rows_total),
         out_shape=jax.ShapeDtypeStruct((out_frames, 4, 128, c3), BF16),
-        in_specs=[vmem] * 9,
-        out_specs=vmem,
+        in_specs=[vmem] * 2 + [hbm] * 8,
+        out_specs=hbm,
         scratch_shapes=[
+            pltpu.VMEM((24, frames, 128), F32),
             pltpu.VMEM((5 * frames * 32, 128), F32),
             pltpu.VMEM((5 * frames * 32, 128), F32),
             pltpu.VMEM((3, 8, 32, 256), BF16),
@@ -227,21 +277,41 @@
             pltpu.VMEM((4, 2, 4, 32, c2), BF16),
             pltpu.VMEM((4, 128, 3 * c3), F32),
             pltpu.VMEM((2, 128, c3), F32),
+            pltpu.VMEM((out_frames, 4, 128, c3), BF16),
+            pltpu.VMEM((768, c1), BF16),
+            pltpu.VMEM((3, 3, 3, c1, c2), BF16),
+            pltpu.VMEM((3, 3, 3, c2, c3), BF16),
+            pltpu.VMEM((1, c1), F32),
+            pltpu.VMEM((1, c1), F32),
+            pltpu.VMEM((1, c2), F32),
+            pltpu.VMEM((1, c2), F32),
+            pltpu.VMEM((1, c3), F32),
+            pltpu.SemaphoreType.DMA((9,)),
+            pltpu.SemaphoreType.DMA((3,)),
+            pltpu.SemaphoreType.DMA,
+            pltpu.SemaphoreType.DMA((5,)),
+            pltpu.SemaphoreType.DMA((4,)),
         ],
         compiler_params=pltpu.CompilerParams(vmem_limit_bytes=32 * 1024 * 1024),
         cost_estimate=pl.CostEstimate(
             flops=4_000_000_000, bytes_accessed=10_000_000, transcendentals=600_000
         ),
     )(
-        pieces,
-        w1,
-        b1.reshape(1, c1),
-        g1.reshape(1, c1),
-        pltpu.with_memory_space_constraint(k2, pltpu.VMEM),
-        b2.reshape(1, c2),
-        g2.reshape(1, c2),
-        pltpu.with_memory_space_constraint(k3, pltpu.VMEM),
-        b3.reshape(1, c3),
+        held,
+        received,
+        *[
+            pltpu.with_memory_space_constraint(array, pltpu.HBM)
+            for array in (
+                k1.reshape(3, 3, 48, c1),
+                b1.reshape(1, c1),
+                g1.reshape(1, c1),
+                k2,
+                b2.reshape(1, c2),
+                g2.reshape(1, c2),
+                k3,
+                b3.reshape(1, c3),
+            )
+        ],
     )
 
 

time: 30.8 us -> 22.4 us (0.73)
  local copies, waits for them, and re-layouts: 9.72 us -> 0.72 us
  other arithmetic: 1.37 us -> 0.01 us
  waiting for transfers between devices: 3.5 us -> 4.64 us
  Pallas kernels: 7.9 us -> 9.03 us
    unnamed x18 -> x0, local copies, waits for them, and re-layouts: 8.59 us -> none
    ppermute x5, waiting for transfers between devices: 3.5 us -> 4.64 us  [hop(): return lax.ppermute(array, AXES, pairs)]
    pallas_call x1, Pallas kernels: 7.9 us -> 9.03 us  [per_device(): pl.pallas_call(functools.partial(decode_kernel, rows_total), out_shape=ja...]
    pad x2 -> x0, local copies, waits for them, and re-layouts: 1.11 us -> none  [the longest x1 1.06 us: per_device(): w1 = jnp.pad(k1.reshape(3, 3, 48, c1), ((0, 0), (0, 0), (0, 16), (0, 0)))]
    concatenate x2 -> x1, local copies, waits for them, and re-layouts: 0.02 us -> 0.72 us  [gathered_pieces(): jnp.concatenate([latent[None], jnp.zeros_like(latent)[None]])]
    concatenate x1, other arithmetic: 0.69 us -> 0.01 us  [gathered_pieces(): jnp.concatenate([held, hop(held, lambda s, t: (s ^ 1, t ^ 1), seq, tm)])]
    concatenate x1, other arithmetic: 0.69 us -> 0.01 us  [gathered_pieces(): held = jnp.concatenate([held, even, odd])]
  transfers between devices with their start and end apart: 5 -> 5, of which waited for: 3 -> 4; matrix products, arithmetic and copies ran while one was open for 6% -> 3% of each run, Pallas kernels for 0% -> 0%
where the time goes in v2:
time: 22.4 us; the launch traced here: 22.2 us
  Pallas kernels  9.03 us (40%)
  starting transfers between devices  7.81 us (35%)
  waiting for transfers between devices  4.64 us (21%)
  local copies, waits for them, and re-layouts  0.72 us (3%)
    pallas_call x1, Pallas kernels, per_device(): pl.pallas_call(functools.partial(decode_kernel, rows_total), out_shape=ja...  9.03 us
    ppermute x5, starting transfers between devices, hop(): return lax.ppermute(array, AXES, pairs)  7.81 us
    ppermute x5, waiting for transfers between devices, hop(): return lax.ppermute(array, AXES, pairs)  4.64 us
    concatenate x1, local copies, waits for them, and re-layouts, gathered_pieces(): jnp.concatenate([latent[None], jnp.zeros_like(latent)[None]])  0.72 us
  transfers between devices with their start and end apart: 5, of which 4 were waited for; matrix products, arithmetic and copies ran while one was open for 3% of the time, Pallas kernels for 0%

profile of v2, /device:TPU:0, one launch (start us, length us, event | category | flops | bytes accessed | tf_op | source)
XLA Modules:
  0.0 22.2 jit_solution(13678508601987419321)
XLA Ops:
  0.0 2.4 %collective-permute-start = (bf16[1,8,128]{2,1,0:T(8,128)(2,1)}, bf16[1,8,128]{2,1,0:T(8,128)(2,1)S(1)}, u32[]{:S(2)}, u32[]{:S(2)}) collective-permute-start(bf16[1,8,128]{2,1,0:T(8,128)(2,1)} %bitcast.7), channel_id=1, source_target_pairs={{0,3},{1,2},{2,1},{3,0},{4,7},{5,6},{6,5},{7,4},{8,11},{9,10},{10,... | collective-permute-start | bytes 6152 | tf_op jit(solution)/shard_map/ppermute | solution.py:20
  2.4 0.7 %concatenate.10 = bf16[2,8,128]{2,1,0:T(8,128)(2,1)S(1)} pad(bf16[1,8,128]{2,1,0:T(8,128)(2,1)} %bitcast.8, bf16[]{:T(256)} %constant.0.clone.1), padding=0_1x0_0x0_0 | pad | bytes 6146 | tf_op jit(solution)/shard_map/concatenate | solution.py:36
  3.1 0.8 %collective-permute-done = bf16[1,8,128]{2,1,0:T(8,128)(2,1)S(1)} collective-permute-done((bf16[1,8,128]{2,1,0:T(8,128)(2,1)}, bf16[1,8,128]{2,1,0:T(8,128)(2,1)S(1)}, u32[]{:S(2)}, u32[]{:S(2)}) %collective-permute-start) | collective-permute-done | bytes 2080 | tf_op jit(solution)/shard_map/ppermute | solution.py:20
  3.9 2.0 %collective-permute-start.1 = (bf16[2,8,128]{2,1,0:T(8,128)(2,1)S(1)}, bf16[2,8,128]{2,1,0:T(8,128)(2,1)S(1)}, u32[]{:S(2)}, u32[]{:S(2)}) collective-permute-start(bf16[2,8,128]{2,1,0:T(8,128)(2,1)S(1)} %constant_dynamic-update-slice_fusion), channel_id=1, source_target_pairs={{0,5},{1,4},{2,7},{3,6},{4,1},{5,0},{6,3},{7,2},{8,13},{9,12},{10,... | collective-permute-start | bytes 12296 | tf_op jit(solution)/shard_map/ppermute | solution.py:20
  5.9 1.3 %collective-permute-done.1 = bf16[2,8,128]{2,1,0:T(8,128)(2,1)S(1)} collective-permute-done((bf16[2,8,128]{2,1,0:T(8,128)(2,1)S(1)}, bf16[2,8,128]{2,1,0:T(8,128)(2,1)S(1)}, u32[]{:S(2)}, u32[]{:S(2)}) %collective-permute-start.1) | collective-permute-done | bytes 4128 | tf_op jit(solution)/shard_map/ppermute | solution.py:20
  7.2 0.4 %collective-permute-start.3 = (bf16[4,8,128]{2,1,0:T(8,128)(2,1)S(1)}, bf16[4,8,128]{2,1,0:T(8,128)(2,1)S(1)}, u32[]{:S(2)}, u32[]{:S(2)}) collective-permute-start(bf16[4,8,128]{2,1,0:T(8,128)(2,1)S(1)} %pad_maximum_fusion.1), channel_id=1, source_target_pairs={{0,1},{1,0},{2,3},{3,2},{4,5},{5,4},{6,7},{7,6},{8,17},{9,16},{10,... | collective-permute-start | bytes 24584 | tf_op jit(solution)/shard_map/ppermute | solution.py:20
  7.6 3.0 %collective-permute-start.2 = (bf16[4,8,128]{2,1,0:T(8,128)(2,1)S(1)}, bf16[4,8,128]{2,1,0:T(8,128)(2,1)S(1)}, u32[]{:S(2)}, u32[]{:S(2)}) collective-permute-start(bf16[4,8,128]{2,1,0:T(8,128)(2,1)S(1)} %pad_maximum_fusion.1), channel_id=1, source_target_pairs={{0,9},{1,8},{2,11},{3,10},{4,13},{5,12},{6,15},{7,14},{8,1},{9,0},... | collective-permute-start | bytes 24584 | tf_op jit(solution)/shard_map/ppermute | solution.py:20
  10.6 0.0 collective-permute-done.3
  10.6 1.4 %collective-permute-done.2 = bf16[4,8,128]{2,1,0:T(8,128)(2,1)S(1)} collective-permute-done((bf16[4,8,128]{2,1,0:T(8,128)(2,1)S(1)}, bf16[4,8,128]{2,1,0:T(8,128)(2,1)S(1)}, u32[]{:S(2)}, u32[]{:S(2)}) %collective-permute-start.2) | collective-permute-done | bytes 8224 | tf_op jit(solution)/shard_map/ppermute | solution.py:20
  12.0 0.0 collective-permute-start.4
  12.0 1.1 %collective-permute-done.4.received = bf16[12,8,128]{2,1,0:T(8,128)(2,1)S(1)} collective-permute-done((bf16[12,8,128]{2,1,0:T(8,128)(2,1)S(1)}, bf16[12,8,128]{2,1,0:T(8,128)(2,1)S(1)}, u32[]{:S(2)}, u32[]{:S(2)}) %collective-permute-start.4) | collective-permute-done | bytes 24608 | tf_op jit(solution)/shard_map/ppermute | solution.py:20
  13.2 9.0 %shard_map.91 = bf16[2,4,128,128]{3,2,1,0:T(8,128)(2,1)} custom-call(bf16[12,8,128]{2,1,0:T(8,128)(2,1)S(1)} %pad_maximum_fusion.held, bf16[12,8,128]{2,1,0:T(8,128)(2,1)S(1)} %collective-permute-done.4.received, bf16[3,3,48,512]{3,2,1,0:T(8,128)(2,1)} %bitcast.9, f32[1,512]{1,0:T(1,128)} %bitcast.10, f32[1,512]{1,0:T(1,128)} %bitcast.11, ...), custom_call_target="tpu_custom_call" | custom-call | flops 4000000000 | bytes 10000000 | tf_op jit(solution)/shard_map/pallas_call | solution.py:265
  (3 shorter events, 0.0 us)
Async XLA Ops:
  0.0 3.9 %collective-permute-start = (bf16[1,8,128]{2,1,0:T(8,128)(2,1)}, bf16[1,8,128]{2,1,0:T(8,128)(2,1)S(1)}, u32[]{:S(2)}, u32[]{:S(2)}) collective-permute-start(bf16[1,8,128]{2,1,0:T(8,128)(2,1)} %bitcast.7), channel_id=1, source_target_pairs={{0,3},{1,2},{2,1},{3,0},{4,7},{5,6},{6,5},{7,4},{8,11},{9,10},{10,... | collective-permute-start | bytes 6152 | tf_op jit(solution)/shard_map/ppermute | solution.py:20
  3.9 3.3 %collective-permute-start.1 = (bf16[2,8,128]{2,1,0:T(8,128)(2,1)S(1)}, bf16[2,8,128]{2,1,0:T(8,128)(2,1)S(1)}, u32[]{:S(2)}, u32[]{:S(2)}) collective-permute-start(bf16[2,8,128]{2,1,0:T(8,128)(2,1)S(1)} %constant_dynamic-update-slice_fusion), channel_id=1, source_target_pairs={{0,5},{1,4},{2,7},{3,6},{4,1},{5,0},{6,3},{7,2},{8,13},{9,12},{10,... | collective-permute-start | bytes 12296 | tf_op jit(solution)/shard_map/ppermute | solution.py:20
  7.2 3.4 %collective-permute-start.3 = (bf16[4,8,128]{2,1,0:T(8,128)(2,1)S(1)}, bf16[4,8,128]{2,1,0:T(8,128)(2,1)S(1)}, u32[]{:S(2)}, u32[]{:S(2)}) collective-permute-start(bf16[4,8,128]{2,1,0:T(8,128)(2,1)S(1)} %pad_maximum_fusion.1), channel_id=1, source_target_pairs={{0,1},{1,0},{2,3},{3,2},{4,5},{5,4},{6,7},{7,6},{8,17},{9,16},{10,... | collective-permute-start | bytes 24584 | tf_op jit(solution)/shard_map/ppermute | solution.py:20
  7.6 4.4 %collective-permute-start.2 = (bf16[4,8,128]{2,1,0:T(8,128)(2,1)S(1)}, bf16[4,8,128]{2,1,0:T(8,128)(2,1)S(1)}, u32[]{:S(2)}, u32[]{:S(2)}) collective-permute-start(bf16[4,8,128]{2,1,0:T(8,128)(2,1)S(1)} %pad_maximum_fusion.1), channel_id=1, source_target_pairs={{0,9},{1,8},{2,11},{3,10},{4,13},{5,12},{6,15},{7,14},{8,1},{9,0},... | collective-permute-start | bytes 24584 | tf_op jit(solution)/shard_map/ppermute | solution.py:20
  12.0 1.2 %collective-permute-start.4 = (bf16[12,8,128]{2,1,0:T(8,128)(2,1)S(1)}, bf16[12,8,128]{2,1,0:T(8,128)(2,1)S(1)}, u32[]{:S(2)}, u32[]{:S(2)}) collective-permute-start(bf16[12,8,128]{2,1,0:T(8,128)(2,1)S(1)} %pad_maximum_fusion.held), channel_id=1, source_target_pairs={{0,1},{1,0},{2,3},{3,2},{4,5},{5,4},{6,7},{7,6},{8,9},{9,8},{10,11... | collective-permute-start | bytes 73736 | tf_op jit(solution)/shard_map/ppermute | solution.py:20

commit v3 on v1

--- a/solution.py
+++ b/solution.py
@@ -20,7 +20,7 @@
     return lax.ppermute(array, AXES, pairs)
 
 
-def gathered_pieces(latent):
+def gathered_pieces(latent, k1, b1, g1, k2, b2, g2, b3):
     seq, tm = lax.axis_size("seq"), lax.axis_size("tm")
     assert seq % 2 == 0 and tm == 4
 
@@ -32,36 +32,126 @@
 
         return partner
 
-    held = latent[None]
-    held = jnp.concatenate([held, hop(held, lambda s, t: (s, t ^ 3), seq, tm)])
-    held = jnp.concatenate([held, hop(held, lambda s, t: (s ^ 1, t ^ 1), seq, tm)])
+    beside = hop(latent[None], lambda s, t: (s, t ^ 3), seq, tm)
+    tap0, own = fetched_tap_and_latent(k2, 0, latent)
+    beside, tap0, own = lax.optimization_barrier((beside, tap0, own))
+    held = jnp.concatenate([own, beside])
+
+    k2, _ = lax.optimization_barrier((k2, beside))
+    across = hop(held, lambda s, t: (s ^ 1, t ^ 1), seq, tm)
+    tap1 = fetched_tap(k2, 1)
+    across, tap1 = lax.optimization_barrier((across, tap1))
+    held = jnp.concatenate([held, across])
+
+    k2, _ = lax.optimization_barrier((k2, across))
     even = hop(held, z_partner(0), seq, tm)
     odd = hop(held, z_partner(1), seq, tm)
+    tap2 = fetched_tap(k2, 2)
+    even, odd, tap2 = lax.optimization_barrier((even, odd, tap2))
     held = jnp.concatenate([held, even, odd])
-    return jnp.concatenate([held, hop(held, lambda s, t: (s, t ^ 1), seq, tm)])
-
-
-def silu(v):
-    return 0.5 * v * (1.0 + jnp.tanh(0.5 * v))
+
+    k1, _ = lax.optimization_barrier((k1, even))
+    received = hop(held, lambda s, t: (s, t ^ 1), seq, tm)
+    first = fetched_first(k1, b1, g1, b2, g2, b3)
+    return held, received, first, (tap0, tap1, tap2)
 
 
 def normed(hidden, gain):
     factor = lax.rsqrt(jnp.mean(hidden * hidden, axis=-1, keepdims=True) + 1e-06)
-    return silu(hidden * factor * gain).astype(BF16)
+    half = hidden * (0.5 * factor) * gain
+    return (half + half * jnp.tanh(half)).astype(BF16)
+
+
+def first_weights_kernel(k1, b1_in, g1_in, b2_in, g2_in, b3_in, w1, b1, g1, b2, g2, b3, sem):
+    pairs = [(b1_in, b1), (g1_in, g1), (b2_in, b2), (g2_in, g2), (b3_in, b3)]
+    for i in range(3):
+        for j in range(3):
+            pairs.append((k1.at[i, j], w1.at[pl.ds(i * 256 + j * 64, 48)]))
+    copies = [pltpu.make_async_copy(a, b, sem.at[n]) for n, (a, b) in enumerate(pairs)]
+    for copy in copies:
+        copy.start()
+    for i in range(3):
+        for start, size in ((48, 16), (112, 16), (176, 80)):
+            w1[pl.ds(i * 256 + start, size), :] = jnp.zeros((size, w1.shape[1]), BF16)
+    for copy in copies:
+        copy.wait()
+
+
+def column_tap_kernel(k, k2, w2, sem):
+    copy = pltpu.make_async_copy(k2.at[:, :, k], w2, sem)
+    copy.start()
+    copy.wait()
+
+
+def column_tap_and_latent_kernel(k, k2, latent, w2, own, sem):
+    copies = [
+        pltpu.make_async_copy(latent, own.at[0], sem.at[0]),
+        pltpu.make_async_copy(k2.at[:, :, k], w2, sem.at[1]),
+    ]
+    for copy in copies:
+        copy.start()
+    for copy in copies:
+        copy.wait()
+
+
+def in_hbm(*arrays):
+    return [pltpu.with_memory_space_constraint(array, pltpu.HBM) for array in arrays]
+
+
+def fetched_first(k1, b1, g1, b2, g2, b3):
+    c1 = k1.shape[4]
+    shapes = [(768, c1)] + [(1, v.shape[0]) for v in (b1, g1, b2, g2, b3)]
+    rows = [v.reshape(1, -1) for v in (b1, g1, b2, g2, b3)]
+    return pl.pallas_call(
+        first_weights_kernel,
+        out_shape=[pltpu.VMEM(shapes[0], BF16)] + [pltpu.VMEM(v, F32) for v in shapes[1:]],
+        in_specs=[pl.BlockSpec(memory_space=pltpu.HBM)] * 6,
+        out_specs=[pl.BlockSpec(memory_space=pltpu.VMEM)] * 6,
+        scratch_shapes=[pltpu.SemaphoreType.DMA((14,))],
+        cost_estimate=pl.CostEstimate(flops=0, bytes_accessed=3_000_000, transcendentals=0),
+    )(*in_hbm(k1.reshape(3, 3, 48, c1), *rows))
+
+
+def fetched_tap(k2, k):
+    shape = k2.shape[:2] + k2.shape[3:]
+    return pl.pallas_call(
+        functools.partial(column_tap_kernel, k),
+        out_shape=pltpu.VMEM(shape, BF16),
+        in_specs=[pl.BlockSpec(memory_space=pltpu.HBM)],
+        out_specs=pl.BlockSpec(memory_space=pltpu.VMEM),
+        scratch_shapes=[pltpu.SemaphoreType.DMA],
+        cost_estimate=pl.CostEstimate(flops=0, bytes_accessed=4_500_000, transcendentals=0),
+    )(*in_hbm(k2))
+
+
+def fetched_tap_and_latent(k2, k, latent):
+    shape = k2.shape[:2] + k2.shape[3:]
+    return pl.pallas_call(
+        functools.partial(column_tap_and_latent_kernel, k),
+        out_shape=[pltpu.VMEM(shape, BF16), pltpu.VMEM((1,) + latent.shape, BF16)],
+        in_specs=[pl.BlockSpec(memory_space=pltpu.HBM)] * 2,
+        out_specs=[pl.BlockSpec(memory_space=pltpu.VMEM)] * 2,
+        scratch_shapes=[pltpu.SemaphoreType.DMA((2,))],
+        cost_estimate=pl.CostEstimate(flops=0, bytes_accessed=4_500_000, transcendentals=0),
+    )(*in_hbm(k2, latent))
 
 
 def decode_kernel(
     rows_total,
-    pieces,
+    held,
+    received,
     w1,
     b1,
     g1,
-    w2,
     b2,
     g2,
-    w3,
     b3,
-    out,
+    w2_0,
+    w2_1,
+    w2_2,
+    k3,
+    out_hbm,
+    pieces,
     rolled,
     rolled_far,
     patches,
@@ -70,11 +160,19 @@
     second_act,
     final,
     line,
+    out,
+    w3,
+    sem3,
+    sem_out,
 ):
+    load3 = pltpu.make_async_copy(k3, w3, sem3)
+    load3.start()
     s = lax.axis_index("seq")
     t = lax.axis_index("tm")
     z, x, y, c = s // 2, s % 2, t // 2, t % 2
-    n_frames = pieces.shape[1]
+    n_frames = held.shape[1]
+    pieces[:12] = held[...].astype(F32)
+    pieces[12:] = received[...].astype(F32)
 
     def piece_of(row, chunk):
         dz, dx = row // 2 - z, row % 2 ^ x
@@ -87,7 +185,7 @@
 
     def one_row(d, _):
         row = jnp.clip(s - 2 + d, 0, rows_total - 1)
-        chunks = [pieces[piece_of(row, chunk)].astype(F32) for chunk in range(4)]
+        chunks = [pieces[piece_of(row, chunk)] for chunk in range(4)]
         for chunk in range(4):
             for q in range(8):
                 shift = (16 - 16 * q) % 128
@@ -121,47 +219,49 @@
 
     lax.fori_loop(0, 3, one_patch, 0)
 
-    def first(r, _):
+    def first(r):
         lhs = jnp.concatenate([patches[r, i : i + 6].reshape(192, 256) for i in range(3)], axis=1)
         hidden = jnp.dot(lhs, w1[...], preferred_element_type=F32) + b1[...]
         first_act[r] = normed(hidden, g1[...]).reshape(6, 32, 512)
-        return 0
-
-    lax.fori_loop(0, 3, first, 0)
-
-    def second(k, _):
+
+    for r in range(3):
+        first(r)
+
+    def second(k, w2):
         def lhs(rows):
             m = (rows.stop - rows.start) * 128
             return [first_act[rows, i : i + 4].reshape(m, 512) for i in range(3)]
 
         edge = jnp.dot(
             jnp.concatenate(lhs(slice(0, 2)) + lhs(slice(1, 3)), axis=1),
-            jnp.concatenate([w2[i, j, k] for j in (0, 2) for i in range(3)], axis=0),
+            jnp.concatenate([w2[i, j] for j in (0, 2) for i in range(3)], axis=0),
             preferred_element_type=F32,
         )
         middle = jnp.dot(
             jnp.concatenate(lhs(slice(0, 3)), axis=1),
-            jnp.concatenate([w2[i, 1, k] for i in range(3)], axis=0),
+            jnp.concatenate([w2[i, 1] for i in range(3)], axis=0),
             preferred_element_type=F32,
         )
         for p in range(4):
             e, m = p // 2, (p + 1) // 2
             partial[k, p] = edge[e * 128 : (e + 1) * 128] + middle[m * 128 : (m + 1) * 128]
-        return 0
-
-    lax.fori_loop(0, 3, second, 0)
+
+    for k, w2 in enumerate((w2_0, w2_1, w2_2)):
+        second(k, w2)
 
     column = lax.broadcasted_iota(jnp.int32, (4, 32, 256), 1)
 
-    def second_norm(p, _):
+    def second_norm(p):
         a, b, d = [partial[k, p].reshape(4, 32, 256) for k in range(3)]
         a_left = jnp.where(column == 0, a, pltpu.roll(a, 1, 1))
         d_right = jnp.where(column == 31, d, pltpu.roll(d, 31, 1))
         second_act[p, 0] = normed(a_left + b + d + b2[...], g2[...])
         second_act[p, 1] = normed(a + b + d_right + b2[...], g2[...])
-        return 0
-
-    lax.fori_loop(0, 4, second_norm, 0)
+
+    for p in range(4):
+        second_norm(p)
+
+    load3.wait()
 
     def lhs3(rows):
         m = (rows.stop - rows.start) * 128
@@ -186,7 +286,7 @@
 
     narrow = lax.broadcasted_iota(jnp.int32, (32, 128), 0)
 
-    def last(r, _):
+    def last(r):
         def part(q, g, k):
             return final[r, pl.ds((q * 2 + g) * 32, 32), k * 128 : (k + 1) * 128]
 
@@ -198,9 +298,12 @@
             for u, value in enumerate(columns):
                 line[g, pl.ds(u, 32, stride=4), :] = value + b3[...]
             out[g, r] = line[g].astype(BF16)
-        return 0
-
-    lax.fori_loop(0, 4, last, 0)
+        pltpu.make_async_copy(out.at[:, r], out_hbm.at[:, r], sem_out.at[r]).start()
+
+    for r in range(4):
+        last(r)
+    for r in range(4):
+        pltpu.make_async_copy(out.at[:, r], out_hbm.at[:, r], sem_out.at[r]).wait()
 
 
 def per_device(latent, k1, b1, g1, k2, b2, g2, k3, b3):
@@ -208,17 +311,17 @@
     tm = lax.axis_size("tm")
     rows_total = lax.axis_size("seq")
     c1, c2, c3 = k1.shape[4], k2.shape[4], k3.shape[4]
-    pieces = gathered_pieces(latent)
-    w1 = jnp.pad(k1.reshape(3, 3, 48, c1), ((0, 0), (0, 0), (0, 16), (0, 0)))
-    w1 = jnp.pad(w1.reshape(3, 192, c1), ((0, 0), (0, 64), (0, 0))).reshape(768, c1)
+    held, received, first, taps = gathered_pieces(latent, k1, b1, g1, k2, b2, g2, b3)
     vmem = pl.BlockSpec(memory_space=pltpu.VMEM)
+    hbm = pl.BlockSpec(memory_space=pltpu.HBM)
     out_frames = frames // tm
     return pl.pallas_call(
         functools.partial(decode_kernel, rows_total),
         out_shape=jax.ShapeDtypeStruct((out_frames, 4, 128, c3), BF16),
-        in_specs=[vmem] * 9,
-        out_specs=vmem,
+        in_specs=[vmem] * 11 + [hbm],
+        out_specs=hbm,
         scratch_shapes=[
+            pltpu.VMEM((24, frames, 128), F32),
             pltpu.VMEM((5 * frames * 32, 128), F32),
             pltpu.VMEM((5 * frames * 32, 128), F32),
             pltpu.VMEM((3, 8, 32, 256), BF16),
@@ -227,22 +330,16 @@
             pltpu.VMEM((4, 2, 4, 32, c2), BF16),
             pltpu.VMEM((4, 128, 3 * c3), F32),
             pltpu.VMEM((2, 128, c3), F32),
+            pltpu.VMEM((out_frames, 4, 128, c3), BF16),
+            pltpu.VMEM((3, 3, 3, c2, c3), BF16),
+            pltpu.SemaphoreType.DMA,
+            pltpu.SemaphoreType.DMA((4,)),
         ],
-        compiler_params=pltpu.CompilerParams(vmem_limit_bytes=32 * 1024 * 1024),
+        compiler_params=pltpu.CompilerParams(vmem_limit_bytes=24 * 1024 * 1024),
         cost_estimate=pl.CostEstimate(
             flops=4_000_000_000, bytes_accessed=10_000_000, transcendentals=600_000
         ),
-    )(
-        pieces,
-        w1,
-        b1.reshape(1, c1),
-        g1.reshape(1, c1),
-        pltpu.with_memory_space_constraint(k2, pltpu.VMEM),
-        b2.reshape(1, c2),
-        g2.reshape(1, c2),
-        pltpu.with_memory_space_constraint(k3, pltpu.VMEM),
-        b3.reshape(1, c3),
-    )
+    )(held, received, *first, *taps, *in_hbm(k3))
 
 
 def solution(mesh):

time: 30.8 us -> 26.6 us (0.86)
  Pallas kernels: 7.9 us -> 12.7 us
  local copies, waits for them, and re-layouts: 9.72 us -> 6.17 us
  waiting for transfers between devices: 3.5 us -> 0.01 us
  other arithmetic: 1.37 us -> 0.01 us
  starting transfers between devices: 7.88 us -> 7.19 us
    pallas_call x0 -> x4, Pallas kernels: none -> 6.24 us  [the longest x2 3.35 us: fetched_tap(): pl.pallas_call(functools.partial(column_tap_kernel, k), out_shape=pltpu.V...]
    ppermute x5, waiting for transfers between devices: 3.5 us -> 0.01 us  [hop(): return lax.ppermute(array, AXES, pairs)]
    unnamed x18 -> x11, local copies, waits for them, and re-layouts: 8.59 us -> 6.16 us
    pallas_call x1, Pallas kernels: 7.9 us -> 6.46 us  [per_device(): pl.pallas_call(functools.partial(decode_kernel, rows_total), out_shape=ja...]
    concatenate x2 -> x1, other arithmetic: 1.37 us -> 0.01 us  [gathered_pieces(): held = jnp.concatenate([own, beside])]
    pad x2 -> x0, local copies, waits for them, and re-layouts: 1.11 us -> none  [the longest x1 1.06 us: per_device(): w1 = jnp.pad(k1.reshape(3, 3, 48, c1), ((0, 0), (0, 0), (0, 16), (0, 0)))]
    ppermute x5, starting transfers between devices: 7.88 us -> 7.19 us  [hop(): return lax.ppermute(array, AXES, pairs)]
  transfers between devices with their start and end apart: 5 -> 5, of which waited for: 3 -> 0; matrix products, arithmetic and copies ran while one was open for 6% -> 0% of each run, Pallas kernels for 0% -> 24%
where the time goes in v3:
time: 26.6 us; the launch traced here: 26.2 us
  Pallas kernels  12.7 us (48%)
  starting transfers between devices  7.19 us (27%)
  local copies, waits for them, and re-layouts  6.17 us (23%)
    ppermute x5, starting transfers between devices, hop(): return lax.ppermute(array, AXES, pairs)  7.19 us
    pallas_call x1, Pallas kernels, per_device(): pl.pallas_call(functools.partial(decode_kernel, rows_total), out_shape=ja...  6.46 us
    unnamed x11, local copies, waits for them, and re-layouts  6.16 us
    pallas_call x2, Pallas kernels, fetched_tap(): pl.pallas_call(functools.partial(column_tap_kernel, k), out_shape=pltpu.V...  3.35 us
    pallas_call x1, Pallas kernels, fetched_tap_and_latent(): pl.pallas_call(functools.partial(column_tap_and_latent_kernel, k), out_sh...  1.7 us
    pallas_call x1, Pallas kernels, fetched_first(): pl.pallas_call(first_weights_kernel, out_shape=[pltpu.VMEM(shapes[0], BF1...  1.19 us
  transfers between devices with their start and end apart: 5, of which 0 were waited for; matrix products, arithmetic and copies ran while one was open for 0% of the time, Pallas kernels for 24%

profile of v3, /device:TPU:0, one launch (start us, length us, event | category | flops | bytes accessed | tf_op | source)
XLA Modules:
  0.0 26.2 jit_solution(12369962644847717787)
XLA Ops:
  0.0 2.4 %collective-permute-start = (bf16[1,8,128]{2,1,0:T(8,128)(2,1)}, bf16[1,8,128]{2,1,0:T(8,128)(2,1)S(1)}, u32[]{:S(2)}, u32[]{:S(2)}) collective-permute-start(bf16[1,8,128]{2,1,0:T(8,128)(2,1)} %bitcast.10), channel_id=1, source_target_pairs={{0,3},{1,2},{2,1},{3,0},{4,7},{5,6},{6,5},{7,4},{8,11},{9,10},{10,... | collective-permute-start | bytes 6152 | tf_op jit(solution)/shard_map/ppermute | solution.py:20
  2.4 1.7 %shard_map.91 = (bf16[3,3,512,256]{3,2,1,0:T(8,128)(2,1)S(1)}, bf16[1,8,128]{2,1,0:T(8,128)(2,1)S(1)}) custom-call(bf16[3,3,3,512,256]{4,3,2,1,0:T(8,128)(2,1)} %k2.3, bf16[8,128]{1,0:T(8,128)(2,1)} %latent.1), custom_call_target="tpu_custom_call" | custom-call | bytes 4500000 | tf_op jit(solution)/shard_map/pallas_call | solution.py:129
  4.1 0.0 copy-start.2
  4.1 1.4 %copy-done.2 = bf16[3,3,512,256]{3,2,1,0:T(8,128)(2,1)} copy-done((bf16[3,3,512,256]{3,2,1,0:T(8,128)(2,1)}, bf16[3,3,512,256]{3,2,1,0:T(8,128)(2,1)S(1)}, u32[]{:S(2)}) %copy-start.2) | copy-done | bytes 2359320
  5.5 0.0 collective-permute-done
  5.5 1.8 %collective-permute-start.1 = (bf16[2,8,128]{2,1,0:T(8,128)(2,1)S(1)}, bf16[2,8,128]{2,1,0:T(8,128)(2,1)S(1)}, u32[]{:S(2)}, u32[]{:S(2)}) collective-permute-start(bf16[2,8,128]{2,1,0:T(8,128)(2,1)S(1)} %pad_maximum_fusion), channel_id=1, source_target_pairs={{0,5},{1,4},{2,7},{3,6},{4,1},{5,0},{6,3},{7,2},{8,13},{9,12},{10,... | collective-permute-start | bytes 12296 | tf_op jit(solution)/shard_map/ppermute | solution.py:20
  7.4 1.7 %shard_map.92.w2_1 = bf16[3,3,512,256]{3,2,1,0:T(8,128)(2,1)S(1)} custom-call(bf16[3,3,3,512,256]{4,3,2,1,0:T(8,128)(2,1)} %k2.3), custom_call_target="tpu_custom_call" | custom-call | bytes 4500000 | tf_op jit(solution)/shard_map/pallas_call | solution.py:117
  9.1 0.0 copy-start
  9.1 1.4 %copy-done = bf16[3,3,512,256]{3,2,1,0:T(8,128)(2,1)} copy-done((bf16[3,3,512,256]{3,2,1,0:T(8,128)(2,1)}, bf16[3,3,512,256]{3,2,1,0:T(8,128)(2,1)S(1)}, u32[]{:S(2)}) %copy-start) | copy-done | bytes 2359320
  10.5 0.0 collective-permute-done.1
  10.5 0.0 collective-permute-start.3
  10.5 2.9 %collective-permute-start.2 = (bf16[4,8,128]{2,1,0:T(8,128)(2,1)S(1)}, bf16[4,8,128]{2,1,0:T(8,128)(2,1)S(1)}, u32[]{:S(2)}, u32[]{:S(2)}) collective-permute-start(bf16[4,8,128]{2,1,0:T(8,128)(2,1)S(1)} %get-tuple-element.43), channel_id=1, source_target_pairs={{0,9},{1,8},{2,11},{3,10},{4,13},{5,12},{6,15},{7,14},{8,1},{9,0},... | collective-permute-start | bytes 24584 | tf_op jit(solution)/shard_map/ppermute | solution.py:20
  13.4 1.7 %shard_map.93.w2_2 = bf16[3,3,512,256]{3,2,1,0:T(8,128)(2,1)S(1)} custom-call(bf16[3,3,3,512,256]{4,3,2,1,0:T(8,128)(2,1)} %k2.3), custom_call_target="tpu_custom_call" | custom-call | bytes 4500000 | tf_op jit(solution)/shard_map/pallas_call | solution.py:117
  15.0 0.0 collective-permute-done.3
  15.1 0.0 collective-permute-done.2
  15.1 0.1 collective-permute-start.4
  15.2 1.2 %shard_map.94 = (bf16[768,512]{1,0:T(8,128)(2,1)S(1)}, f32[1,512]{1,0:T(1,128)S(1)}, f32[1,512]{1,0:T(1,128)S(1)}, f32[1,256]{1,0:T(1,128)S(1)}, f32[1,256]{1,0:T(1,128)S(1)}, /*index=5*/f32[1,128]{1,0:T(1,128)S(1)}) custom-call(bf16[3,3,48,512]{3,2,1,0:T(8,128)(2,1)} %bitcast.7, f32[1,512]{1,0:T(1,128)} %bitcast.8, f32[1,512]{1,0:T(1,128)} %bitcast.9, ...), custom_call_target="tpu_custom_call" | custom-call | bytes 3000000 | tf_op jit(solution)/shard_map/pallas_call | solution.py:105
  16.4 0.0 collective-permute-done.4.received
  16.4 0.0 copy-start.1
  16.4 1.7 %copy-done.1 = bf16[3,3,512,256]{3,2,1,0:T(8,128)(2,1)S(1)} copy-done((bf16[3,3,512,256]{3,2,1,0:T(8,128)(2,1)S(1)}, bf16[3,3,512,256]{3,2,1,0:T(8,128)(2,1)}, u32[]{:S(2)}) %copy-start.1) | copy-done | bytes 2359320
  18.1 0.0 copy-start.3
  18.1 1.7 %copy-done.3 = bf16[3,3,512,256]{3,2,1,0:T(8,128)(2,1)S(1)} copy-done((bf16[3,3,512,256]{3,2,1,0:T(8,128)(2,1)S(1)}, bf16[3,3,512,256]{3,2,1,0:T(8,128)(2,1)}, u32[]{:S(2)}) %copy-start.3) | copy-done | bytes 2359320
  19.7 6.5 %shard_map.95 = bf16[2,4,128,128]{3,2,1,0:T(8,128)(2,1)} custom-call(bf16[12,8,128]{2,1,0:T(8,128)(2,1)S(1)} %constant_dynamic-update-slice_fusion.3.held, bf16[12,8,128]{2,1,0:T(8,128)(2,1)S(1)} %collective-permute-done.4.received, bf16[768,512]{1,0:T(8,128)(2,1)S(1)} %get-tuple-element.34.w1, f32[1,512]{1,0:T(1,128)S(1)} %get-tuple-element.35.b1, ...), custom_call_target="tpu_custom_call" | custom-call | flops 4000000000 | bytes 10000000 | tf_op jit(solution)/shard_map/pallas_call | solution.py:318
  (6 shorter events, 0.0 us)
Async XLA Ops:
  0.0 5.5 %collective-permute-start = (bf16[1,8,128]{2,1,0:T(8,128)(2,1)}, bf16[1,8,128]{2,1,0:T(8,128)(2,1)S(1)}, u32[]{:S(2)}, u32[]{:S(2)}) collective-permute-start(bf16[1,8,128]{2,1,0:T(8,128)(2,1)} %bitcast.10), channel_id=1, source_target_pairs={{0,3},{1,2},{2,1},{3,0},{4,7},{5,6},{6,5},{7,4},{8,11},{9,10},{10,... | collective-permute-start | bytes 6152 | tf_op jit(solution)/shard_map/ppermute | solution.py:20
  4.1 1.4 %copy-start.2 = (bf16[3,3,512,256]{3,2,1,0:T(8,128)(2,1)}, bf16[3,3,512,256]{3,2,1,0:T(8,128)(2,1)S(1)}, u32[]{:S(2)}) copy-start(bf16[3,3,512,256]{3,2,1,0:T(8,128)(2,1)S(1)} %get-tuple-element.40.w2_0) | copy-start | bytes 7077892
  5.5 4.9 %collective-permute-start.1 = (bf16[2,8,128]{2,1,0:T(8,128)(2,1)S(1)}, bf16[2,8,128]{2,1,0:T(8,128)(2,1)S(1)}, u32[]{:S(2)}, u32[]{:S(2)}) collective-permute-start(bf16[2,8,128]{2,1,0:T(8,128)(2,1)S(1)} %pad_maximum_fusion), channel_id=1, source_target_pairs={{0,5},{1,4},{2,7},{3,6},{4,1},{5,0},{6,3},{7,2},{8,13},{9,12},{10,... | collective-permute-start | bytes 12296 | tf_op jit(solution)/shard_map/ppermute | solution.py:20
  9.1 1.4 %copy-start = (bf16[3,3,512,256]{3,2,1,0:T(8,128)(2,1)}, bf16[3,3,512,256]{3,2,1,0:T(8,128)(2,1)S(1)}, u32[]{:S(2)}) copy-start(bf16[3,3,512,256]{3,2,1,0:T(8,128)(2,1)S(1)} %shard_map.92.w2_1) | copy-start | bytes 7077892
  10.5 4.6 %collective-permute-start.3 = (bf16[4,8,128]{2,1,0:T(8,128)(2,1)S(1)}, bf16[4,8,128]{2,1,0:T(8,128)(2,1)S(1)}, u32[]{:S(2)}, u32[]{:S(2)}) collective-permute-start(bf16[4,8,128]{2,1,0:T(8,128)(2,1)S(1)} %get-tuple-element.43), channel_id=1, source_target_pairs={{0,1},{1,0},{2,3},{3,2},{4,5},{5,4},{6,7},{7,6},{8,17},{9,16},{10,... | collective-permute-start | bytes 24584 | tf_op jit(solution)/shard_map/ppermute | solution.py:20
  10.5 4.6 %collective-permute-start.2 = (bf16[4,8,128]{2,1,0:T(8,128)(2,1)S(1)}, bf16[4,8,128]{2,1,0:T(8,128)(2,1)S(1)}, u32[]{:S(2)}, u32[]{:S(2)}) collective-permute-start(bf16[4,8,128]{2,1,0:T(8,128)(2,1)S(1)} %get-tuple-element.43), channel_id=1, source_target_pairs={{0,9},{1,8},{2,11},{3,10},{4,13},{5,12},{6,15},{7,14},{8,1},{9,0},... | collective-permute-start | bytes 24584 | tf_op jit(solution)/shard_map/ppermute | solution.py:20
  15.1 1.3 %collective-permute-start.4 = (bf16[12,8,128]{2,1,0:T(8,128)(2,1)S(1)}, bf16[12,8,128]{2,1,0:T(8,128)(2,1)S(1)}, u32[]{:S(2)}, u32[]{:S(2)}) collective-permute-start(bf16[12,8,128]{2,1,0:T(8,128)(2,1)S(1)} %constant_dynamic-update-slice_fusion.3.held), channel_id=1, source_target_pairs={{0,1},{1,0},{2,3},{3,2},{4,5},{5,4},{6,7},{7,6},{8,9},{9,8},{10,11... | collective-permute-start | bytes 73736 | tf_op jit(solution)/shard_map/ppermute | solution.py:20
  16.4 1.7 %copy-start.1 = (bf16[3,3,512,256]{3,2,1,0:T(8,128)(2,1)S(1)}, bf16[3,3,512,256]{3,2,1,0:T(8,128)(2,1)}, u32[]{:S(2)}) copy-start(bf16[3,3,512,256]{3,2,1,0:T(8,128)(2,1)} %copy-done) | copy-start | bytes 7077892
  18.1 1.7 %copy-start.3 = (bf16[3,3,512,256]{3,2,1,0:T(8,128)(2,1)S(1)}, bf16[3,3,512,256]{3,2,1,0:T(8,128)(2,1)}, u32[]{:S(2)}) copy-start(bf16[3,3,512,256]{3,2,1,0:T(8,128)(2,1)} %copy-done.2) | copy-start | bytes 7077892

commit v4 on v3

--- a/solution.py
+++ b/solution.py
@@ -108,6 +108,7 @@
         in_specs=[pl.BlockSpec(memory_space=pltpu.HBM)] * 6,
         out_specs=[pl.BlockSpec(memory_space=pltpu.VMEM)] * 6,
         scratch_shapes=[pltpu.SemaphoreType.DMA((14,))],
+        compiler_params=pltpu.CompilerParams(vmem_limit_bytes=1024 * 1024),
         cost_estimate=pl.CostEstimate(flops=0, bytes_accessed=3_000_000, transcendentals=0),
     )(*in_hbm(k1.reshape(3, 3, 48, c1), *rows))
 
@@ -120,6 +121,7 @@
         in_specs=[pl.BlockSpec(memory_space=pltpu.HBM)],
         out_specs=pl.BlockSpec(memory_space=pltpu.VMEM),
         scratch_shapes=[pltpu.SemaphoreType.DMA],
+        compiler_params=pltpu.CompilerParams(vmem_limit_bytes=1024 * 1024),
         cost_estimate=pl.CostEstimate(flops=0, bytes_accessed=4_500_000, transcendentals=0),
     )(*in_hbm(k2))
 
@@ -132,6 +134,7 @@
         in_specs=[pl.BlockSpec(memory_space=pltpu.HBM)] * 2,
         out_specs=[pl.BlockSpec(memory_space=pltpu.VMEM)] * 2,
         scratch_shapes=[pltpu.SemaphoreType.DMA((2,))],
+        compiler_params=pltpu.CompilerParams(vmem_limit_bytes=1024 * 1024),
         cost_estimate=pl.CostEstimate(flops=0, bytes_accessed=4_500_000, transcendentals=0),
     )(*in_hbm(k2, latent))
 
@@ -335,7 +338,7 @@
             pltpu.SemaphoreType.DMA,
             pltpu.SemaphoreType.DMA((4,)),
         ],
-        compiler_params=pltpu.CompilerParams(vmem_limit_bytes=24 * 1024 * 1024),
+        compiler_params=pltpu.CompilerParams(vmem_limit_bytes=16 * 1024 * 1024),
         cost_estimate=pl.CostEstimate(
             flops=4_000_000_000, bytes_accessed=10_000_000, transcendentals=600_000
         ),

time: 26.6 us -> 20.7 us (0.78)
  local copies, waits for them, and re-layouts: 6.17 us -> 0.04 us
  starting transfers between devices: 7.19 us -> 7.61 us
    unnamed x11 -> x3, local copies, waits for them, and re-layouts: 6.16 us -> 0.02 us
    ppermute x5, starting transfers between devices: 7.19 us -> 7.61 us  [hop(): return lax.ppermute(array, AXES, pairs)]
  transfers between devices with their start and end apart: 5 -> 5, of which waited for: 0 -> 0; matrix products, arithmetic and copies ran while one was open for 0% -> 0% of each run, Pallas kernels for 24% -> 30%
where the time goes in v4:
time: 20.7 us; the launch traced here: 20.5 us
  Pallas kernels  12.7 us (61%)
  starting transfers between devices  7.61 us (37%)
    ppermute x5, starting transfers between devices, hop(): return lax.ppermute(array, AXES, pairs)  7.61 us
    pallas_call x1, Pallas kernels, per_device(): pl.pallas_call(functools.partial(decode_kernel, rows_total), out_shape=ja...  6.47 us
    pallas_call x2, Pallas kernels, fetched_tap(): pl.pallas_call(functools.partial(column_tap_kernel, k), out_shape=pltpu.V...  3.35 us
    pallas_call x1, Pallas kernels, fetched_tap_and_latent(): pl.pallas_call(functools.partial(column_tap_and_latent_kernel, k), out_sh...  1.7 us
    pallas_call x1, Pallas kernels, fetched_first(): pl.pallas_call(first_weights_kernel, out_shape=[pltpu.VMEM(shapes[0], BF1...  1.19 us
  transfers between devices with their start and end apart: 5, of which 0 were waited for; matrix products, arithmetic and copies ran while one was open for 0% of the time, Pallas kernels for 30%

profile of v4, /device:TPU:0, one launch (start us, length us, event | category | flops | bytes accessed | tf_op | source)
XLA Modules:
  0.0 20.5 jit_solution(16405828246228852780)
XLA Ops:
  0.0 2.4 %collective-permute-start = (bf16[1,8,128]{2,1,0:T(8,128)(2,1)}, bf16[1,8,128]{2,1,0:T(8,128)(2,1)S(1)}, u32[]{:S(2)}, u32[]{:S(2)}) collective-permute-start(bf16[1,8,128]{2,1,0:T(8,128)(2,1)} %bitcast.10), channel_id=1, source_target_pairs={{0,3},{1,2},{2,1},{3,0},{4,7},{5,6},{6,5},{7,4},{8,11},{9,10},{10,... | collective-permute-start | bytes 6152 | tf_op jit(solution)/shard_map/ppermute | solution.py:20
  2.4 1.7 %shard_map.91 = (bf16[3,3,512,256]{3,2,1,0:T(8,128)(2,1)S(1)}, bf16[1,8,128]{2,1,0:T(8,128)(2,1)S(1)}) custom-call(bf16[3,3,3,512,256]{4,3,2,1,0:T(8,128)(2,1)} %k2.3, bf16[8,128]{1,0:T(8,128)(2,1)} %latent.1), custom_call_target="tpu_custom_call" | custom-call | bytes 4500000 | tf_op jit(solution)/shard_map/pallas_call | solution.py:131
  4.1 0.0 collective-permute-done
  4.1 1.8 %collective-permute-start.1 = (bf16[2,8,128]{2,1,0:T(8,128)(2,1)S(1)}, bf16[2,8,128]{2,1,0:T(8,128)(2,1)S(1)}, u32[]{:S(2)}, u32[]{:S(2)}) collective-permute-start(bf16[2,8,128]{2,1,0:T(8,128)(2,1)S(1)} %pad_maximum_fusion), channel_id=1, source_target_pairs={{0,5},{1,4},{2,7},{3,6},{4,1},{5,0},{6,3},{7,2},{8,13},{9,12},{10,... | collective-permute-start | bytes 12296 | tf_op jit(solution)/shard_map/ppermute | solution.py:20
  6.0 1.7 %shard_map.92.w2_1 = bf16[3,3,512,256]{3,2,1,0:T(8,128)(2,1)S(1)} custom-call(bf16[3,3,3,512,256]{4,3,2,1,0:T(8,128)(2,1)} %k2.3), custom_call_target="tpu_custom_call" | custom-call | bytes 4500000 | tf_op jit(solution)/shard_map/pallas_call | solution.py:118
  7.7 0.0 collective-permute-done.1
  7.7 0.4 %collective-permute-start.3 = (bf16[4,8,128]{2,1,0:T(8,128)(2,1)S(1)}, bf16[4,8,128]{2,1,0:T(8,128)(2,1)S(1)}, u32[]{:S(2)}, u32[]{:S(2)}) collective-permute-start(bf16[4,8,128]{2,1,0:T(8,128)(2,1)S(1)} %get-tuple-element.43), channel_id=1, source_target_pairs={{0,1},{1,0},{2,3},{3,2},{4,5},{5,4},{6,7},{7,6},{8,17},{9,16},{10,... | collective-permute-start | bytes 24584 | tf_op jit(solution)/shard_map/ppermute | solution.py:20
  8.1 2.5 %collective-permute-start.2 = (bf16[4,8,128]{2,1,0:T(8,128)(2,1)S(1)}, bf16[4,8,128]{2,1,0:T(8,128)(2,1)S(1)}, u32[]{:S(2)}, u32[]{:S(2)}) collective-permute-start(bf16[4,8,128]{2,1,0:T(8,128)(2,1)S(1)} %get-tuple-element.43), channel_id=1, source_target_pairs={{0,9},{1,8},{2,11},{3,10},{4,13},{5,12},{6,15},{7,14},{8,1},{9,0},... | collective-permute-start | bytes 24584 | tf_op jit(solution)/shard_map/ppermute | solution.py:20
  10.7 1.7 %shard_map.93.w2_2 = bf16[3,3,512,256]{3,2,1,0:T(8,128)(2,1)S(1)} custom-call(bf16[3,3,3,512,256]{4,3,2,1,0:T(8,128)(2,1)} %k2.3), custom_call_target="tpu_custom_call" | custom-call | bytes 4500000 | tf_op jit(solution)/shard_map/pallas_call | solution.py:118
  12.3 0.0 collective-permute-done.3
  12.3 0.0 collective-permute-done.2
  12.4 0.4 %collective-permute-start.4 = (bf16[12,8,128]{2,1,0:T(8,128)(2,1)S(1)}, bf16[12,8,128]{2,1,0:T(8,128)(2,1)S(1)}, u32[]{:S(2)}, u32[]{:S(2)}) collective-permute-start(bf16[12,8,128]{2,1,0:T(8,128)(2,1)S(1)} %constant_dynamic-update-slice_fusion.3.held), channel_id=1, source_target_pairs={{0,1},{1,0},{2,3},{3,2},{4,5},{5,4},{6,7},{7,6},{8,9},{9,8},{10,11... | collective-permute-start | bytes 73736 | tf_op jit(solution)/shard_map/ppermute | solution.py:20
  12.8 1.2 %shard_map.94 = (bf16[768,512]{1,0:T(8,128)(2,1)S(1)}, f32[1,512]{1,0:T(1,128)S(1)}, f32[1,512]{1,0:T(1,128)S(1)}, f32[1,256]{1,0:T(1,128)S(1)}, f32[1,256]{1,0:T(1,128)S(1)}, /*index=5*/f32[1,128]{1,0:T(1,128)S(1)}) custom-call(bf16[3,3,48,512]{3,2,1,0:T(8,128)(2,1)} %bitcast.7, f32[1,512]{1,0:T(1,128)} %bitcast.8, f32[1,512]{1,0:T(1,128)} %bitcast.9, ...), custom_call_target="tpu_custom_call" | custom-call | bytes 3000000 | tf_op jit(solution)/shard_map/pallas_call | solution.py:105
  14.0 0.0 collective-permute-done.4.received
  14.0 6.5 %shard_map.95 = bf16[2,4,128,128]{3,2,1,0:T(8,128)(2,1)} custom-call(bf16[12,8,128]{2,1,0:T(8,128)(2,1)S(1)} %constant_dynamic-update-slice_fusion.3.held, bf16[12,8,128]{2,1,0:T(8,128)(2,1)S(1)} %collective-permute-done.4.received, bf16[768,512]{1,0:T(8,128)(2,1)S(1)} %get-tuple-element.34.w1, f32[1,512]{1,0:T(1,128)S(1)} %get-tuple-element.35.b1, ...), custom_call_target="tpu_custom_call" | custom-call | flops 4000000000 | bytes 10000000 | tf_op jit(solution)/shard_map/pallas_call | solution.py:321
  (6 shorter events, 0.0 us)
Async XLA Ops:
  0.0 4.1 %collective-permute-start = (bf16[1,8,128]{2,1,0:T(8,128)(2,1)}, bf16[1,8,128]{2,1,0:T(8,128)(2,1)S(1)}, u32[]{:S(2)}, u32[]{:S(2)}) collective-permute-start(bf16[1,8,128]{2,1,0:T(8,128)(2,1)} %bitcast.10), channel_id=1, source_target_pairs={{0,3},{1,2},{2,1},{3,0},{4,7},{5,6},{6,5},{7,4},{8,11},{9,10},{10,... | collective-permute-start | bytes 6152 | tf_op jit(solution)/shard_map/ppermute | solution.py:20
  4.1 3.5 %collective-permute-start.1 = (bf16[2,8,128]{2,1,0:T(8,128)(2,1)S(1)}, bf16[2,8,128]{2,1,0:T(8,128)(2,1)S(1)}, u32[]{:S(2)}, u32[]{:S(2)}) collective-permute-start(bf16[2,8,128]{2,1,0:T(8,128)(2,1)S(1)} %pad_maximum_fusion), channel_id=1, source_target_pairs={{0,5},{1,4},{2,7},{3,6},{4,1},{5,0},{6,3},{7,2},{8,13},{9,12},{10,... | collective-permute-start | bytes 12296 | tf_op jit(solution)/shard_map/ppermute | solution.py:20
  7.7 4.6 %collective-permute-start.3 = (bf16[4,8,128]{2,1,0:T(8,128)(2,1)S(1)}, bf16[4,8,128]{2,1,0:T(8,128)(2,1)S(1)}, u32[]{:S(2)}, u32[]{:S(2)}) collective-permute-start(bf16[4,8,128]{2,1,0:T(8,128)(2,1)S(1)} %get-tuple-element.43), channel_id=1, source_target_pairs={{0,1},{1,0},{2,3},{3,2},{4,5},{5,4},{6,7},{7,6},{8,17},{9,16},{10,... | collective-permute-start | bytes 24584 | tf_op jit(solution)/shard_map/ppermute | solution.py:20
  8.1 4.2 %collective-permute-start.2 = (bf16[4,8,128]{2,1,0:T(8,128)(2,1)S(1)}, bf16[4,8,128]{2,1,0:T(8,128)(2,1)S(1)}, u32[]{:S(2)}, u32[]{:S(2)}) collective-permute-start(bf16[4,8,128]{2,1,0:T(8,128)(2,1)S(1)} %get-tuple-element.43), channel_id=1, source_target_pairs={{0,9},{1,8},{2,11},{3,10},{4,13},{5,12},{6,15},{7,14},{8,1},{9,0},... | collective-permute-start | bytes 24584 | tf_op jit(solution)/shard_map/ppermute | solution.py:20
  12.4 1.6 %collective-permute-start.4 = (bf16[12,8,128]{2,1,0:T(8,128)(2,1)S(1)}, bf16[12,8,128]{2,1,0:T(8,128)(2,1)S(1)}, u32[]{:S(2)}, u32[]{:S(2)}) collective-permute-start(bf16[12,8,128]{2,1,0:T(8,128)(2,1)S(1)} %constant_dynamic-update-slice_fusion.3.held), channel_id=1, source_target_pairs={{0,1},{1,0},{2,3},{3,2},{4,5},{5,4},{6,7},{7,6},{8,9},{9,8},{10,11... | collective-permute-start | bytes 73736 | tf_op jit(solution)/shard_map/ppermute | solution.py:20

commit v5 on v3

--- a/solution.py
+++ b/solution.py
@@ -20,7 +20,7 @@
     return lax.ppermute(array, AXES, pairs)
 
 
-def gathered_pieces(latent, k1, b1, g1, k2, b2, g2, b3):
+def gathered_pieces(latent, k1, b1, g1, b2, g2, b3):
     seq, tm = lax.axis_size("seq"), lax.axis_size("tm")
     assert seq % 2 == 0 and tm == 4
 
@@ -33,27 +33,14 @@
         return partner
 
     beside = hop(latent[None], lambda s, t: (s, t ^ 3), seq, tm)
-    tap0, own = fetched_tap_and_latent(k2, 0, latent)
-    beside, tap0, own = lax.optimization_barrier((beside, tap0, own))
+    *first, own = fetched_first(k1, b1, g1, b2, g2, b3, latent)
+    beside, own, *first = lax.optimization_barrier((beside, own, *first))
     held = jnp.concatenate([own, beside])
-
-    k2, _ = lax.optimization_barrier((k2, beside))
-    across = hop(held, lambda s, t: (s ^ 1, t ^ 1), seq, tm)
-    tap1 = fetched_tap(k2, 1)
-    across, tap1 = lax.optimization_barrier((across, tap1))
-    held = jnp.concatenate([held, across])
-
-    k2, _ = lax.optimization_barrier((k2, across))
+    held = jnp.concatenate([held, hop(held, lambda s, t: (s ^ 1, t ^ 1), seq, tm)])
     even = hop(held, z_partner(0), seq, tm)
     odd = hop(held, z_partner(1), seq, tm)
-    tap2 = fetched_tap(k2, 2)
-    even, odd, tap2 = lax.optimization_barrier((even, odd, tap2))
     held = jnp.concatenate([held, even, odd])
-
-    k1, _ = lax.optimization_barrier((k1, even))
-    received = hop(held, lambda s, t: (s, t ^ 1), seq, tm)
-    first = fetched_first(k1, b1, g1, b2, g2, b3)
-    return held, received, first, (tap0, tap1, tap2)
+    return held, hop(held, lambda s, t: (s, t ^ 1), seq, tm), first
 
 
 def normed(hidden, gain):
@@ -62,8 +49,11 @@
     return (half + half * jnp.tanh(half)).astype(BF16)
 
 
-def first_weights_kernel(k1, b1_in, g1_in, b2_in, g2_in, b3_in, w1, b1, g1, b2, g2, b3, sem):
+def first_weights_kernel(
+    k1, b1_in, g1_in, b2_in, g2_in, b3_in, latent, w1, b1, g1, b2, g2, b3, own, sem
+):
     pairs = [(b1_in, b1), (g1_in, g1), (b2_in, b2), (g2_in, g2), (b3_in, b3)]
+    pairs.append((latent, own.at[0]))
     for i in range(3):
         for j in range(3):
             pairs.append((k1.at[i, j], w1.at[pl.ds(i * 256 + j * 64, 48)]))
@@ -77,63 +67,23 @@
         copy.wait()
 
 
-def column_tap_kernel(k, k2, w2, sem):
-    copy = pltpu.make_async_copy(k2.at[:, :, k], w2, sem)
-    copy.start()
-    copy.wait()
-
-
-def column_tap_and_latent_kernel(k, k2, latent, w2, own, sem):
-    copies = [
-        pltpu.make_async_copy(latent, own.at[0], sem.at[0]),
-        pltpu.make_async_copy(k2.at[:, :, k], w2, sem.at[1]),
-    ]
-    for copy in copies:
-        copy.start()
-    for copy in copies:
-        copy.wait()
-
-
 def in_hbm(*arrays):
     return [pltpu.with_memory_space_constraint(array, pltpu.HBM) for array in arrays]
 
 
-def fetched_first(k1, b1, g1, b2, g2, b3):
+def fetched_first(k1, b1, g1, b2, g2, b3, latent):
     c1 = k1.shape[4]
-    shapes = [(768, c1)] + [(1, v.shape[0]) for v in (b1, g1, b2, g2, b3)]
     rows = [v.reshape(1, -1) for v in (b1, g1, b2, g2, b3)]
+    shapes = [pltpu.VMEM((768, c1), BF16)] + [pltpu.VMEM(v.shape, F32) for v in rows]
     return pl.pallas_call(
         first_weights_kernel,
-        out_shape=[pltpu.VMEM(shapes[0], BF16)] + [pltpu.VMEM(v, F32) for v in shapes[1:]],
-        in_specs=[pl.BlockSpec(memory_space=pltpu.HBM)] * 6,
-        out_specs=[pl.BlockSpec(memory_space=pltpu.VMEM)] * 6,
-        scratch_shapes=[pltpu.SemaphoreType.DMA((14,))],
-        cost_estimate=pl.CostEstimate(flops=0, bytes_accessed=3_000_000, transcendentals=0),
-    )(*in_hbm(k1.reshape(3, 3, 48, c1), *rows))
-
-
-def fetched_tap(k2, k):
-    shape = k2.shape[:2] + k2.shape[3:]
-    return pl.pallas_call(
-        functools.partial(column_tap_kernel, k),
-        out_shape=pltpu.VMEM(shape, BF16),
-        in_specs=[pl.BlockSpec(memory_space=pltpu.HBM)],
-        out_specs=pl.BlockSpec(memory_space=pltpu.VMEM),
-        scratch_shapes=[pltpu.SemaphoreType.DMA],
-        cost_estimate=pl.CostEstimate(flops=0, bytes_accessed=4_500_000, transcendentals=0),
-    )(*in_hbm(k2))
-
-
-def fetched_tap_and_latent(k2, k, latent):
-    shape = k2.shape[:2] + k2.shape[3:]
-    return pl.pallas_call(
-        functools.partial(column_tap_and_latent_kernel, k),
-        out_shape=[pltpu.VMEM(shape, BF16), pltpu.VMEM((1,) + latent.shape, BF16)],
-        in_specs=[pl.BlockSpec(memory_space=pltpu.HBM)] * 2,
-        out_specs=[pl.BlockSpec(memory_space=pltpu.VMEM)] * 2,
-        scratch_shapes=[pltpu.SemaphoreType.DMA((2,))],
-        cost_estimate=pl.CostEstimate(flops=0, bytes_accessed=4_500_000, transcendentals=0),
-    )(*in_hbm(k2, latent))
+        out_shape=shapes + [pltpu.VMEM((1,) + latent.shape, BF16)],
+        in_specs=[pl.BlockSpec(memory_space=pltpu.HBM)] * 7,
+        out_specs=[pl.BlockSpec(memory_space=pltpu.VMEM)] * 7,
+        scratch_shapes=[pltpu.SemaphoreType.DMA((15,))],
+        compiler_params=pltpu.CompilerParams(vmem_limit_bytes=1024 * 1024),
+        cost_estimate=pl.CostEstimate(flops=10000000000, bytes_accessed=40000000, transcendentals=0),
+    )(*in_hbm(k1.reshape(3, 3, 48, c1), *rows, latent))
 
 
 def decode_kernel(
@@ -146,27 +96,22 @@
     b2,
     g2,
     b3,
-    w2_0,
-    w2_1,
-    w2_2,
-    k3,
+    w2,
+    w3,
     out_hbm,
     pieces,
     rolled,
     rolled_far,
     patches,
     first_act,
-    partial,
+    edge,
+    middle_sums,
     second_act,
     final,
     line,
     out,
-    w3,
-    sem3,
     sem_out,
 ):
-    load3 = pltpu.make_async_copy(k3, w3, sem3)
-    load3.start()
     s = lax.axis_index("seq")
     t = lax.axis_index("tm")
     z, x, y, c = s // 2, s % 2, t // 2, t % 2
@@ -227,41 +172,40 @@
     for r in range(3):
         first(r)
 
-    def second(k, w2):
-        def lhs(rows):
-            m = (rows.stop - rows.start) * 128
-            return [first_act[rows, i : i + 4].reshape(m, 512) for i in range(3)]
-
-        edge = jnp.dot(
+    def lhs(rows):
+        m = (rows.stop - rows.start) * 128
+        return [first_act[rows, i : i + 4].reshape(m, 512) for i in range(3)]
+
+    for k in range(3):
+        edge[k] = jnp.dot(
             jnp.concatenate(lhs(slice(0, 2)) + lhs(slice(1, 3)), axis=1),
-            jnp.concatenate([w2[i, j] for j in (0, 2) for i in range(3)], axis=0),
+            jnp.concatenate([w2[i, j, k] for j in (0, 2) for i in range(3)], axis=0),
             preferred_element_type=F32,
         )
+    for k in range(3):
         middle = jnp.dot(
             jnp.concatenate(lhs(slice(0, 3)), axis=1),
-            jnp.concatenate([w2[i, 1] for i in range(3)], axis=0),
+            jnp.concatenate([w2[i, 1, k] for i in range(3)], axis=0),
             preferred_element_type=F32,
         )
-        for p in range(4):
-            e, m = p // 2, (p + 1) // 2
-            partial[k, p] = edge[e * 128 : (e + 1) * 128] + middle[m * 128 : (m + 1) * 128]
-
-    for k, w2 in enumerate((w2_0, w2_1, w2_2)):
-        second(k, w2)
+        middle_sums[k] = middle
 
     column = lax.broadcasted_iota(jnp.int32, (4, 32, 256), 1)
 
     def second_norm(p):
-        a, b, d = [partial[k, p].reshape(4, 32, 256) for k in range(3)]
+        e, m = p // 2 * 128, (p + 1) // 2 * 128
+        a, b, d = [
+            (edge[k, e : e + 128] + middle_sums[k, m : m + 128]).reshape(4, 32, 256)
+            for k in range(3)
+        ]
         a_left = jnp.where(column == 0, a, pltpu.roll(a, 1, 1))
         d_right = jnp.where(column == 31, d, pltpu.roll(d, 31, 1))
-        second_act[p, 0] = normed(a_left + b + d + b2[...], g2[...])
-        second_act[p, 1] = normed(a + b + d_right + b2[...], g2[...])
+        second_act[p, 0] = normed(a_left + (b + b2[...]) + d, g2[...])
+        second_act[p, 1] = normed(a + (b + b2[...]) + d_right, g2[...])
 
     for p in range(4):
         second_norm(p)
 
-    load3.wait()
 
     def lhs3(rows):
         m = (rows.stop - rows.start) * 128
@@ -272,7 +216,7 @@
             [jnp.concatenate([w3[i, j, k] for k in range(3)], axis=1) for i in range(3)], axis=0
         )
 
-    edge = jnp.dot(
+    outer3 = jnp.dot(
         jnp.concatenate(lhs3(slice(0, 3)) + lhs3(slice(1, 4)), axis=1),
         jnp.concatenate([taps(0), taps(2)], axis=0),
         preferred_element_type=F32,
@@ -282,7 +226,7 @@
     )
     for r in range(4):
         e, m = (r + 1) // 2, r // 2
-        final[r] = edge[e * 128 : (e + 1) * 128] + middle[m * 128 : (m + 1) * 128]
+        final[r] = outer3[e * 128 : (e + 1) * 128] + middle[m * 128 : (m + 1) * 128]
 
     narrow = lax.broadcasted_iota(jnp.int32, (32, 128), 0)
 
@@ -311,14 +255,14 @@
     tm = lax.axis_size("tm")
     rows_total = lax.axis_size("seq")
     c1, c2, c3 = k1.shape[4], k2.shape[4], k3.shape[4]
-    held, received, first, taps = gathered_pieces(latent, k1, b1, g1, k2, b2, g2, b3)
+    held, received, first = gathered_pieces(latent, k1, b1, g1, b2, g2, b3)
     vmem = pl.BlockSpec(memory_space=pltpu.VMEM)
     hbm = pl.BlockSpec(memory_space=pltpu.HBM)
     out_frames = frames // tm
     return pl.pallas_call(
         functools.partial(decode_kernel, rows_total),
         out_shape=jax.ShapeDtypeStruct((out_frames, 4, 128, c3), BF16),
-        in_specs=[vmem] * 11 + [hbm],
+        in_specs=[vmem] * 10,
         out_specs=hbm,
         scratch_shapes=[
             pltpu.VMEM((24, frames, 128), F32),
@@ -326,20 +270,19 @@
             pltpu.VMEM((5 * frames * 32, 128), F32),
             pltpu.VMEM((3, 8, 32, 256), BF16),
             pltpu.VMEM((3, 6, 32, c1), BF16),
-            pltpu.VMEM((3, 4, 128, c2), F32),
+            pltpu.VMEM((3, 256, c2), F32),
+            pltpu.VMEM((3, 384, c2), F32),
             pltpu.VMEM((4, 2, 4, 32, c2), BF16),
             pltpu.VMEM((4, 128, 3 * c3), F32),
             pltpu.VMEM((2, 128, c3), F32),
             pltpu.VMEM((out_frames, 4, 128, c3), BF16),
-            pltpu.VMEM((3, 3, 3, c2, c3), BF16),
-            pltpu.SemaphoreType.DMA,
             pltpu.SemaphoreType.DMA((4,)),
         ],
-        compiler_params=pltpu.CompilerParams(vmem_limit_bytes=24 * 1024 * 1024),
+        compiler_params=pltpu.CompilerParams(vmem_limit_bytes=12 * 1024 * 1024),
         cost_estimate=pl.CostEstimate(
             flops=4_000_000_000, bytes_accessed=10_000_000, transcendentals=600_000
         ),
-    )(held, received, *first, *taps, *in_hbm(k3))
+    )(held, received, *first, k2, k3)
 
 
 def solution(mesh):

time: 26.6 us -> 18.8 us (0.71)
  the two profiles are of different devices: /device:TPU:0 before, /device:TPU:21 now
where the time goes in v5:
time: 18.8 us; the launch traced here: 18.7 us
  Pallas kernels  7.53 us (40%)
  waiting for transfers between devices  7.09 us (38%)
  starting transfers between devices  4 us (21%)
    ppermute x5, waiting for transfers between devices, hop(): return lax.ppermute(array, AXES, pairs)  7.09 us
    pallas_call x1, Pallas kernels, per_device(): pl.pallas_call(functools.partial(decode_kernel, rows_total), out_shape=ja...  6.17 us
    ppermute x5, starting transfers between devices, hop(): return lax.ppermute(array, AXES, pairs)  4 us
    pallas_call x1, Pallas kernels, fetched_first(): pl.pallas_call(first_weights_kernel, out_shape=shapes + [pltpu.VMEM((1,)...  1.36 us
  transfers between devices with their start and end apart: 5, of which 5 were waited for; matrix products, arithmetic and copies ran while one was open for 0% of the time, Pallas kernels for 7%

profile of v5, /device:TPU:21, one launch (start us, length us, event | category | flops | bytes accessed | tf_op | source)
XLA Modules:
  0.0 18.7 jit_solution(11553013018842946105)
XLA Ops:
  0.0 0.8 %collective-permute-start = (bf16[1,8,128]{2,1,0:T(8,128)(2,1)}, bf16[1,8,128]{2,1,0:T(8,128)(2,1)S(1)}, u32[]{:S(2)}, u32[]{:S(2)}) collective-permute-start(bf16[1,8,128]{2,1,0:T(8,128)(2,1)} %bitcast.10), channel_id=1, source_target_pairs={{0,3},{1,2},{2,1},{3,0},{4,7},{5,6},{6,5},{7,4},{8,11},{9,10},{10,... | collective-permute-start | bytes 6152 | tf_op jit(solution)/shard_map/ppermute | solution.py:20
  0.8 0.0 copy-start
  0.8 0.0 copy-start.1
  0.8 1.4 %shard_map.91 = (bf16[768,512]{1,0:T(8,128)(2,1)S(1)}, f32[1,512]{1,0:T(1,128)S(1)}, f32[1,512]{1,0:T(1,128)S(1)}, f32[1,256]{1,0:T(1,128)S(1)}, f32[1,256]{1,0:...) custom-call(bf16[3,3,48,512]{3,2,1,0:T(8,128)(2,1)} %bitcast.7, f32[1,512]{1,0:T(1,128)} %bitcast.8, ...), custom_call_target="tpu_custom_call" | custom-call | flops 10000000000 | bytes 40000000 | tf_op jit(solution)/shard_map/pallas_call | solution.py:78
  2.2 1.3 %collective-permute-done = bf16[1,8,128]{2,1,0:T(8,128)(2,1)S(1)} collective-permute-done((bf16[1,8,128]{2,1,0:T(8,128)(2,1)}, bf16[1,8,128]{2,1,0:T(8,128)(2,1)S(1)}, u32[]{:S(2)}, u32[]{:S(2)}) %collective-permute-start) | collective-permute-done | bytes 2080 | tf_op jit(solution)/shard_map/ppermute | solution.py:20
  3.5 1.6 %collective-permute-start.1 = (bf16[2,8,128]{2,1,0:T(8,128)(2,1)S(1)}, bf16[2,8,128]{2,1,0:T(8,128)(2,1)S(1)}, u32[]{:S(2)}, u32[]{:S(2)}) collective-permute-start(bf16[2,8,128]{2,1,0:T(8,128)(2,1)S(1)} %pad_maximum_fusion), channel_id=1, source_target_pairs={{0,5},{1,4},{2,7},{3,6},{4,1},{5,0},{6,3},{7,2},{8,13},{9,12},{10,... | collective-permute-start | bytes 12296 | tf_op jit(solution)/shard_map/ppermute | solution.py:20
  5.1 1.5 %collective-permute-done.1 = bf16[2,8,128]{2,1,0:T(8,128)(2,1)S(1)} collective-permute-done((bf16[2,8,128]{2,1,0:T(8,128)(2,1)S(1)}, bf16[2,8,128]{2,1,0:T(8,128)(2,1)S(1)}, u32[]{:S(2)}, u32[]{:S(2)}) %collective-permute-start.1) | collective-permute-done | bytes 4128 | tf_op jit(solution)/shard_map/ppermute | solution.py:20
  6.6 1.6 %collective-permute-start.2 = (bf16[4,8,128]{2,1,0:T(8,128)(2,1)S(1)}, bf16[4,8,128]{2,1,0:T(8,128)(2,1)S(1)}, u32[]{:S(2)}, u32[]{:S(2)}) collective-permute-start(bf16[4,8,128]{2,1,0:T(8,128)(2,1)S(1)} %get-tuple-element.35), channel_id=1, source_target_pairs={{0,9},{1,8},{2,11},{3,10},{4,13},{5,12},{6,15},{7,14},{8,1},{9,0},... | collective-permute-start | bytes 24584 | tf_op jit(solution)/shard_map/ppermute | solution.py:20
  8.2 0.0 collective-permute-start.3
  8.2 1.5 %collective-permute-done.2 = bf16[4,8,128]{2,1,0:T(8,128)(2,1)S(1)} collective-permute-done((bf16[4,8,128]{2,1,0:T(8,128)(2,1)S(1)}, bf16[4,8,128]{2,1,0:T(8,128)(2,1)S(1)}, u32[]{:S(2)}, u32[]{:S(2)}) %collective-permute-start.2) | collective-permute-done | bytes 8224 | tf_op jit(solution)/shard_map/ppermute | solution.py:20
  9.7 1.6 %collective-permute-done.3 = bf16[4,8,128]{2,1,0:T(8,128)(2,1)S(1)} collective-permute-done((bf16[4,8,128]{2,1,0:T(8,128)(2,1)S(1)}, bf16[4,8,128]{2,1,0:T(8,128)(2,1)S(1)}, u32[]{:S(2)}, u32[]{:S(2)}) %collective-permute-start.3) | collective-permute-done | bytes 8224 | tf_op jit(solution)/shard_map/ppermute | solution.py:20
  11.3 0.1 collective-permute-start.4
  11.4 1.1 %collective-permute-done.4.received = bf16[12,8,128]{2,1,0:T(8,128)(2,1)S(1)} collective-permute-done((bf16[12,8,128]{2,1,0:T(8,128)(2,1)S(1)}, bf16[12,8,128]{2,1,0:T(8,128)(2,1)S(1)}, u32[]{:S(2)}, u32[]{:S(2)}) %collective-permute-start.4) | collective-permute-done | bytes 24608 | tf_op jit(solution)/shard_map/ppermute | solution.py:20
  12.5 0.0 copy-done
  12.5 0.0 copy-done.1
  12.5 6.2 %shard_map.92 = bf16[2,4,128,128]{3,2,1,0:T(8,128)(2,1)} custom-call(bf16[12,8,128]{2,1,0:T(8,128)(2,1)S(1)} %constant_dynamic-update-slice_fusion.3.held, bf16[12,8,128]{2,1,0:T(8,128)(2,1)S(1)} %collective-permute-done.4.received, bf16[768,512]{1,0:T(8,128)(2,1)S(1)} %get-tuple-element.29.w1, f32[1,512]{1,0:T(1,128)S(1)} %get-tuple-element.30.b1, ...), custom_call_target="tpu_custom_call" | custom-call | flops 4000000000 | bytes 10000000 | tf_op jit(solution)/shard_map/pallas_call | solution.py:262
  (6 shorter events, 0.0 us)
Async XLA Ops:
  0.0 3.5 %collective-permute-start = (bf16[1,8,128]{2,1,0:T(8,128)(2,1)}, bf16[1,8,128]{2,1,0:T(8,128)(2,1)S(1)}, u32[]{:S(2)}, u32[]{:S(2)}) collective-permute-start(bf16[1,8,128]{2,1,0:T(8,128)(2,1)} %bitcast.10), channel_id=1, source_target_pairs={{0,3},{1,2},{2,1},{3,0},{4,7},{5,6},{6,5},{7,4},{8,11},{9,10},{10,... | collective-permute-start | bytes 6152 | tf_op jit(solution)/shard_map/ppermute | solution.py:20
  0.8 11.7 %copy-start = (bf16[3,3,3,512,256]{4,3,2,1,0:T(8,128)(2,1)S(1)}, bf16[3,3,3,512,256]{4,3,2,1,0:T(8,128)(2,1)}, u32[]{:S(2)}) copy-start(bf16[3,3,3,512,256]{4,3,2,1,0:T(8,128)(2,1)} %w2.1) | copy-start | bytes 21233668
  0.8 11.7 %copy-start.1 = (bf16[3,3,3,256,128]{4,3,2,1,0:T(8,128)(2,1)S(1)}, bf16[3,3,3,256,128]{4,3,2,1,0:T(8,128)(2,1)}, u32[]{:S(2)}) copy-start(bf16[3,3,3,256,128]{4,3,2,1,0:T(8,128)(2,1)} %w3.1) | copy-start | bytes 5308420
  3.5 3.1 %collective-permute-start.1 = (bf16[2,8,128]{2,1,0:T(8,128)(2,1)S(1)}, bf16[2,8,128]{2,1,0:T(8,128)(2,1)S(1)}, u32[]{:S(2)}, u32[]{:S(2)}) collective-permute-start(bf16[2,8,128]{2,1,0:T(8,128)(2,1)S(1)} %pad_maximum_fusion), channel_id=1, source_target_pairs={{0,5},{1,4},{2,7},{3,6},{4,1},{5,0},{6,3},{7,2},{8,13},{9,12},{10,... | collective-permute-start | bytes 12296 | tf_op jit(solution)/shard_map/ppermute | solution.py:20
  6.6 3.1 %collective-permute-start.2 = (bf16[4,8,128]{2,1,0:T(8,128)(2,1)S(1)}, bf16[4,8,128]{2,1,0:T(8,128)(2,1)S(1)}, u32[]{:S(2)}, u32[]{:S(2)}) collective-permute-start(bf16[4,8,128]{2,1,0:T(8,128)(2,1)S(1)} %get-tuple-element.35), channel_id=1, source_target_pairs={{0,9},{1,8},{2,11},{3,10},{4,13},{5,12},{6,15},{7,14},{8,1},{9,0},... | collective-permute-start | bytes 24584 | tf_op jit(solution)/shard_map/ppermute | solution.py:20
  8.2 3.1 %collective-permute-start.3 = (bf16[4,8,128]{2,1,0:T(8,128)(2,1)S(1)}, bf16[4,8,128]{2,1,0:T(8,128)(2,1)S(1)}, u32[]{:S(2)}, u32[]{:S(2)}) collective-permute-start(bf16[4,8,128]{2,1,0:T(8,128)(2,1)S(1)} %get-tuple-element.35), channel_id=1, source_target_pairs={{0,1},{1,0},{2,3},{3,2},{4,5},{5,4},{6,7},{7,6},{8,17},{9,16},{10,... | collective-permute-start | bytes 24584 | tf_op jit(solution)/shard_map/ppermute | solution.py:20
  11.3 1.2 %collective-permute-start.4 = (bf16[12,8,128]{2,1,0:T(8,128)(2,1)S(1)}, bf16[12,8,128]{2,1,0:T(8,128)(2,1)S(1)}, u32[]{:S(2)}, u32[]{:S(2)}) collective-permute-start(bf16[12,8,128]{2,1,0:T(8,128)(2,1)S(1)} %constant_dynamic-update-slice_fusion.3.held), channel_id=1, source_target_pairs={{0,1},{1,0},{2,3},{3,2},{4,5},{5,4},{6,7},{7,6},{8,9},{9,8},{10,11... | collective-permute-start | bytes 73736 | tf_op jit(solution)/shard_map/ppermute | solution.py:20

commit v6 on v5

--- a/solution.py
+++ b/solution.py
@@ -55,14 +55,14 @@
     pairs = [(b1_in, b1), (g1_in, g1), (b2_in, b2), (g2_in, g2), (b3_in, b3)]
     pairs.append((latent, own.at[0]))
     for i in range(3):
-        for j in range(3):
-            pairs.append((k1.at[i, j], w1.at[pl.ds(i * 256 + j * 64, 48)]))
+        pairs.append((k1.at[i], w1.at[pl.ds(0, 9), pl.ds(16 * (1 + i), 16)]))
     copies = [pltpu.make_async_copy(a, b, sem.at[n]) for n, (a, b) in enumerate(pairs)]
     for copy in copies:
         copy.start()
-    for i in range(3):
-        for start, size in ((48, 16), (112, 16), (176, 80)):
-            w1[pl.ds(i * 256 + start, size), :] = jnp.zeros((size, w1.shape[1]), BF16)
+    zeros = jnp.zeros((9, 16, w1.shape[2]), BF16)
+    w1[:9, :16] = zeros
+    w1[:9, 64:] = zeros
+    w1[9] = jnp.zeros(w1.shape[1:], BF16)
     for copy in copies:
         copy.wait()
 
@@ -74,16 +74,16 @@
 def fetched_first(k1, b1, g1, b2, g2, b3, latent):
     c1 = k1.shape[4]
     rows = [v.reshape(1, -1) for v in (b1, g1, b2, g2, b3)]
-    shapes = [pltpu.VMEM((768, c1), BF16)] + [pltpu.VMEM(v.shape, F32) for v in rows]
+    shapes = [pltpu.VMEM((10, 80, c1), BF16)] + [pltpu.VMEM(v.shape, F32) for v in rows]
     return pl.pallas_call(
         first_weights_kernel,
         out_shape=shapes + [pltpu.VMEM((1,) + latent.shape, BF16)],
         in_specs=[pl.BlockSpec(memory_space=pltpu.HBM)] * 7,
         out_specs=[pl.BlockSpec(memory_space=pltpu.VMEM)] * 7,
-        scratch_shapes=[pltpu.SemaphoreType.DMA((15,))],
+        scratch_shapes=[pltpu.SemaphoreType.DMA((9,))],
         compiler_params=pltpu.CompilerParams(vmem_limit_bytes=1024 * 1024),
         cost_estimate=pl.CostEstimate(flops=10000000000, bytes_accessed=40000000, transcendentals=0),
-    )(*in_hbm(k1.reshape(3, 3, 48, c1), *rows, latent))
+    )(*in_hbm(k1.reshape(3, 9, 16, c1), *rows, latent))
 
 
 def decode_kernel(
@@ -100,14 +100,14 @@
     w3,
     out_hbm,
     pieces,
-    rolled,
-    rolled_far,
+    shifted,
     patches,
     first_act,
     edge,
     middle_sums,
     second_act,
-    final,
+    outer3,
+    middle3,
     line,
     out,
     sem_out,
@@ -126,77 +126,74 @@
         half = (dx + dy + dc + jnp.where(dz == 0, 0, 1)) % 2
         return half * 12 + group * 4 + 2 * dx + dy
 
-    lane = lax.broadcasted_iota(jnp.int32, (n_frames, 128), 1)
-
-    def one_row(d, _):
+    before = n_frames - 2 - 2 * t
+    frame = lax.broadcasted_iota(jnp.int32, (4, n_frames, 128), 1)
+    group = lax.broadcasted_iota(jnp.int32, (4, n_frames, 128), 2) // 16
+    column32 = lax.broadcasted_iota(jnp.int32, (32, 128), 0)
+    for d in range(5):
         row = jnp.clip(s - 2 + d, 0, rows_total - 1)
-        chunks = [pieces[piece_of(row, chunk)] for chunk in range(4)]
-        for chunk in range(4):
-            for q in range(8):
-                shift = (16 - 16 * q) % 128
-                near = pltpu.roll(chunks[chunk], shift, 1) if shift else chunks[chunk]
-                if q == 0:
-                    before = pltpu.roll(chunks[chunk - 1], 16, 1) if chunk else chunks[0]
-                    near = jnp.where(lane < 16, before, near)
-                if q == 7:
-                    after = chunks[chunk + 1] if chunk < 3 else chunks[3]
-                    after = pltpu.roll(after, 32 if chunk < 3 else 48, 1)
-                    near = jnp.where((lane >= 32) & (lane < 48), after, near)
-                at = pl.ds(d * n_frames * 32 + 8 * chunk + q, n_frames, stride=32)
-                rolled[at, :] = near
-                rolled_far[at, :] = pltpu.roll(near, 64, 1)
-        return 0
-
-    lax.fori_loop(0, 5, one_row, 0)
-
-    left = lax.broadcasted_iota(jnp.int32, (32, 128), 1) < 64
-
-    def one_patch(r, _):
+        block = jnp.stack([pieces[piece_of(row, chunk)] for chunk in range(4)])
+        block = jnp.where(frame < before, block[:, :1], pltpu.roll(block, before, 1))
+        for bit in (4, 2, 1):
+            upper = pltpu.roll(pltpu.roll(block, 8 - bit, 1), 16 * bit, 2)
+            lower = upper if bit == 4 else pltpu.roll(pltpu.roll(block, bit, 1), 128 - 16 * bit, 2)
+            f, g = (frame & bit) != 0, (group & bit) != 0
+            block = jnp.where(f == g, block, jnp.where(f, lower, upper))
+        middle = block.reshape(32, 128)
+        left = jnp.where(column32 == 0, middle, pltpu.roll(middle, 1, 0))
+        right = jnp.where(column32 == 31, middle, pltpu.roll(middle, 31, 0))
+        for k, value in enumerate((left, middle, right)):
+            for n, turn in enumerate((0, 96, 64, 32)):
+                turned = pltpu.roll(value, turn, 1) if turn else value
+                shifted[n, d, k] = turned.astype(BF16)
+
+    low = lax.broadcasted_iota(jnp.int32, (32, 128), 1) < 64
+    for r in range(3):
         mine = jnp.clip(s - 1 + r, 0, rows_total - 1)
         d = [jnp.clip(mine - 1 + j, 0, rows_total - 1) - (s - 2) for j in range(3)]
-        for w in range(8):
-            frame = jnp.maximum(2 * t - 6 + w, 0)
-            at = [pl.ds(pl.multiple_of((d[j] * n_frames + frame) * 32, 32), 32) for j in range(3)]
-            pair = jnp.where(left, rolled[at[0], :], rolled_far[at[1], :])
-            patches[r, w, :, :128] = pair.astype(BF16)
-            patches[r, w, :, 128:] = rolled[at[2], :].astype(BF16)
-        return 0
-
-    lax.fori_loop(0, 3, one_patch, 0)
-
-    def first(r):
-        lhs = jnp.concatenate([patches[r, i : i + 6].reshape(192, 256) for i in range(3)], axis=1)
-        hidden = jnp.dot(lhs, w1[...], preferred_element_type=F32) + b1[...]
-        first_act[r] = normed(hidden, g1[...]).reshape(6, 32, 512)
-
-    for r in range(3):
-        first(r)
+        for n in range(5):
+            first, second = 2 * n, min(2 * n + 1, 8)
+            for v in range(3):
+                one = shifted[v, d[first // 3], first % 3]
+                two = shifted[(v + 2) % 4, d[second // 3], second % 3]
+                patches[v, r, :, n * 128 : (n + 1) * 128] = jnp.where(low, one, two)
+
+    for b in range(2):
+        window = slice(16 - 16 * b, 80 - 16 * b)
+        hidden = jnp.dot(
+            patches[...].reshape(288, 640),
+            jnp.concatenate([w1[n, window] for n in range(10)], axis=0),
+            preferred_element_type=F32,
+        )
+        act = normed(hidden + b1[...], g1[...]).reshape(3, 3, 32, 512)
+        for v in range(3):
+            first_act[:, 2 * v + b] = act[v]
 
     def lhs(rows):
         m = (rows.stop - rows.start) * 128
         return [first_act[rows, i : i + 4].reshape(m, 512) for i in range(3)]
 
-    for k in range(3):
-        edge[k] = jnp.dot(
-            jnp.concatenate(lhs(slice(0, 2)) + lhs(slice(1, 3)), axis=1),
-            jnp.concatenate([w2[i, j, k] for j in (0, 2) for i in range(3)], axis=0),
-            preferred_element_type=F32,
-        )
-    for k in range(3):
-        middle = jnp.dot(
-            jnp.concatenate(lhs(slice(0, 3)), axis=1),
-            jnp.concatenate([w2[i, 1, k] for i in range(3)], axis=0),
-            preferred_element_type=F32,
-        )
-        middle_sums[k] = middle
+    def taps2(i, j):
+        return jnp.concatenate([w2[i, j, k] for k in range(3)], axis=1)
+
+    edge[...] = jnp.dot(
+        jnp.concatenate(lhs(slice(0, 2)) + lhs(slice(1, 3)), axis=1),
+        jnp.concatenate([taps2(i, j) for j in (0, 2) for i in range(3)], axis=0),
+        preferred_element_type=F32,
+    )
+    middle_sums[...] = jnp.dot(
+        jnp.concatenate(lhs(slice(0, 3)), axis=1),
+        jnp.concatenate([taps2(i, 1) for i in range(3)], axis=0),
+        preferred_element_type=F32,
+    )
 
     column = lax.broadcasted_iota(jnp.int32, (4, 32, 256), 1)
 
     def second_norm(p):
         e, m = p // 2 * 128, (p + 1) // 2 * 128
         a, b, d = [
-            (edge[k, e : e + 128] + middle_sums[k, m : m + 128]).reshape(4, 32, 256)
-            for k in range(3)
+            (edge[e : e + 128, lanes] + middle_sums[m : m + 128, lanes]).reshape(4, 32, 256)
+            for lanes in (slice(k * 256, (k + 1) * 256) for k in range(3))
         ]
         a_left = jnp.where(column == 0, a, pltpu.roll(a, 1, 1))
         d_right = jnp.where(column == 31, d, pltpu.roll(d, 31, 1))
@@ -211,28 +208,31 @@
         m = (rows.stop - rows.start) * 128
         return [second_act[rows, :, i : i + 2].reshape(m, 256) for i in range(3)]
 
-    def taps(j):
+    def block3(j, ks):
         return jnp.concatenate(
-            [jnp.concatenate([w3[i, j, k] for k in range(3)], axis=1) for i in range(3)], axis=0
+            [jnp.concatenate([w3[i, j, k] for k in ks], axis=1) for i in range(3)], axis=0
         )
 
-    outer3 = jnp.dot(
+    none = jnp.zeros((768, 128), BF16)
+    upper = jnp.concatenate([block3(0, (0, 1, 2)), block3(1, (2,))], axis=1)
+    lower = jnp.concatenate([block3(2, (0, 1, 2)), none], axis=1)
+    outer3[...] = jnp.dot(
         jnp.concatenate(lhs3(slice(0, 3)) + lhs3(slice(1, 4)), axis=1),
-        jnp.concatenate([taps(0), taps(2)], axis=0),
+        jnp.concatenate([upper, lower], axis=0),
         preferred_element_type=F32,
     )
-    middle = jnp.dot(
-        jnp.concatenate(lhs3(slice(1, 3)), axis=1), taps(1), preferred_element_type=F32
-    )
-    for r in range(4):
-        e, m = (r + 1) // 2, r // 2
-        final[r] = outer3[e * 128 : (e + 1) * 128] + middle[m * 128 : (m + 1) * 128]
-
+    middle3[...] = jnp.dot(
+        jnp.concatenate(lhs3(slice(1, 3)), axis=1), block3(1, (0, 1)), preferred_element_type=F32
+    )
     narrow = lax.broadcasted_iota(jnp.int32, (32, 128), 0)
 
     def last(r):
         def part(q, g, k):
-            return final[r, pl.ds((q * 2 + g) * 32, 32), k * 128 : (k + 1) * 128]
+            e, m, at = (r + 1) // 2 * 128, r // 2 * 128, (q * 2 + g) * 32
+            outer = outer3[e + at : e + at + 32, k * 128 : (k + 1) * 128]
+            if k == 2:
+                return outer + outer3[m + 128 + at : m + 160 + at, 384:]
+            return outer + middle3[m + at : m + at + 32, k * 128 : (k + 1) * 128]
 
         for g in range(2):
             a0, a1, b0, b1_, d0, d1 = [part(q, g, k) for k in range(3) for q in range(2)]
@@ -266,14 +266,14 @@
         out_specs=hbm,
         scratch_shapes=[
             pltpu.VMEM((24, frames, 128), F32),
-            pltpu.VMEM((5 * frames * 32, 128), F32),
-            pltpu.VMEM((5 * frames * 32, 128), F32),
-            pltpu.VMEM((3, 8, 32, 256), BF16),
+            pltpu.VMEM((4, 5, 3, 32, 128), BF16),
+            pltpu.VMEM((3, 3, 32, 640), BF16),
             pltpu.VMEM((3, 6, 32, c1), BF16),
-            pltpu.VMEM((3, 256, c2), F32),
-            pltpu.VMEM((3, 384, c2), F32),
+            pltpu.VMEM((256, 3 * c2), F32),
+            pltpu.VMEM((384, 3 * c2), F32),
             pltpu.VMEM((4, 2, 4, 32, c2), BF16),
-            pltpu.VMEM((4, 128, 3 * c3), F32),
+            pltpu.VMEM((384, 4 * c3), F32),
+            pltpu.VMEM((256, 2 * c3), F32),
             pltpu.VMEM((2, 128, c3), F32),
             pltpu.VMEM((out_frames, 4, 128, c3), BF16),
             pltpu.SemaphoreType.DMA((4,)),

time: 18.8 us -> 18.3 us (0.973)
  Pallas kernels: 7.53 us -> 6.97 us
    pallas_call x1, Pallas kernels: 6.17 us -> 5.59 us  [per_device(): pl.pallas_call(functools.partial(decode_kernel, rows_total), out_shape=ja...]
  transfers between devices with their start and end apart: 5 -> 5, of which waited for: 5 -> 5; matrix products, arithmetic and copies ran while one was open for 0% -> 0% of each run, Pallas kernels for 7% -> 8%
where the time goes in v6:
time: 18.3 us; the launch traced here: 18.1 us
  waiting for transfers between devices  7.08 us (39%)
  Pallas kernels  6.97 us (38%)
  starting transfers between devices  4 us (22%)
    ppermute x5, waiting for transfers between devices, hop(): return lax.ppermute(array, AXES, pairs)  7.08 us
    pallas_call x1, Pallas kernels, per_device(): pl.pallas_call(functools.partial(decode_kernel, rows_total), out_shape=ja...  5.59 us
    ppermute x5, starting transfers between devices, hop(): return lax.ppermute(array, AXES, pairs)  4 us
    pallas_call x1, Pallas kernels, fetched_first(): pl.pallas_call(first_weights_kernel, out_shape=shapes + [pltpu.VMEM((1,)...  1.38 us
  transfers between devices with their start and end apart: 5, of which 5 were waited for; matrix products, arithmetic and copies ran while one was open for 0% of the time, Pallas kernels for 8%

profile of v6, /device:TPU:21, one launch (start us, length us, event | category | flops | bytes accessed | tf_op | source)
XLA Modules:
  0.0 18.1 jit_solution(8167078625420252969)
XLA Ops:
  0.0 0.8 %collective-permute-start = (bf16[1,8,128]{2,1,0:T(8,128)(2,1)}, bf16[1,8,128]{2,1,0:T(8,128)(2,1)S(1)}, u32[]{:S(2)}, u32[]{:S(2)}) collective-permute-start(bf16[1,8,128]{2,1,0:T(8,128)(2,1)} %bitcast.10), channel_id=1, source_target_pairs={{0,3},{1,2},{2,1},{3,0},{4,7},{5,6},{6,5},{7,4},{8,11},{9,10},{10,... | collective-permute-start | bytes 6152 | tf_op jit(solution)/shard_map/ppermute | solution.py:20
  0.8 0.0 copy-start
  0.8 0.0 copy-start.1
  0.8 1.4 %shard_map.91 = (bf16[10,80,512]{2,1,0:T(8,128)(2,1)S(1)}, f32[1,512]{1,0:T(1,128)S(1)}, f32[1,512]{1,0:T(1,128)S(1)}, f32[1,256]{1,0:T(1,128)S(1)}, f32[1,256]{...) custom-call(bf16[3,9,16,512]{3,2,1,0:T(8,128)(2,1)} %bitcast.7, f32[1,512]{1,0:T(1,128)} %bitcast.8, ...), custom_call_target="tpu_custom_call" | custom-call | flops 10000000000 | bytes 40000000 | tf_op jit(solution)/shard_map/pallas_call | solution.py:78
  2.2 1.3 %collective-permute-done = bf16[1,8,128]{2,1,0:T(8,128)(2,1)S(1)} collective-permute-done((bf16[1,8,128]{2,1,0:T(8,128)(2,1)}, bf16[1,8,128]{2,1,0:T(8,128)(2,1)S(1)}, u32[]{:S(2)}, u32[]{:S(2)}) %collective-permute-start) | collective-permute-done | bytes 2080 | tf_op jit(solution)/shard_map/ppermute | solution.py:20
  3.5 1.6 %collective-permute-start.1 = (bf16[2,8,128]{2,1,0:T(8,128)(2,1)S(1)}, bf16[2,8,128]{2,1,0:T(8,128)(2,1)S(1)}, u32[]{:S(2)}, u32[]{:S(2)}) collective-permute-start(bf16[2,8,128]{2,1,0:T(8,128)(2,1)S(1)} %pad_maximum_fusion), channel_id=1, source_target_pairs={{0,5},{1,4},{2,7},{3,6},{4,1},{5,0},{6,3},{7,2},{8,13},{9,12},{10,... | collective-permute-start | bytes 12296 | tf_op jit(solution)/shard_map/ppermute | solution.py:20
  5.1 1.5 %collective-permute-done.1 = bf16[2,8,128]{2,1,0:T(8,128)(2,1)S(1)} collective-permute-done((bf16[2,8,128]{2,1,0:T(8,128)(2,1)S(1)}, bf16[2,8,128]{2,1,0:T(8,128)(2,1)S(1)}, u32[]{:S(2)}, u32[]{:S(2)}) %collective-permute-start.1) | collective-permute-done | bytes 4128 | tf_op jit(solution)/shard_map/ppermute | solution.py:20
  6.6 1.6 %collective-permute-start.2 = (bf16[4,8,128]{2,1,0:T(8,128)(2,1)S(1)}, bf16[4,8,128]{2,1,0:T(8,128)(2,1)S(1)}, u32[]{:S(2)}, u32[]{:S(2)}) collective-permute-start(bf16[4,8,128]{2,1,0:T(8,128)(2,1)S(1)} %get-tuple-element.35), channel_id=1, source_target_pairs={{0,9},{1,8},{2,11},{3,10},{4,13},{5,12},{6,15},{7,14},{8,1},{9,0},... | collective-permute-start | bytes 24584 | tf_op jit(solution)/shard_map/ppermute | solution.py:20
  8.2 0.0 collective-permute-start.3
  8.2 1.5 %collective-permute-done.2 = bf16[4,8,128]{2,1,0:T(8,128)(2,1)S(1)} collective-permute-done((bf16[4,8,128]{2,1,0:T(8,128)(2,1)S(1)}, bf16[4,8,128]{2,1,0:T(8,128)(2,1)S(1)}, u32[]{:S(2)}, u32[]{:S(2)}) %collective-permute-start.2) | collective-permute-done | bytes 8224 | tf_op jit(solution)/shard_map/ppermute | solution.py:20
  9.7 1.6 %collective-permute-done.3 = bf16[4,8,128]{2,1,0:T(8,128)(2,1)S(1)} collective-permute-done((bf16[4,8,128]{2,1,0:T(8,128)(2,1)S(1)}, bf16[4,8,128]{2,1,0:T(8,128)(2,1)S(1)}, u32[]{:S(2)}, u32[]{:S(2)}) %collective-permute-start.3) | collective-permute-done | bytes 8224 | tf_op jit(solution)/shard_map/ppermute | solution.py:20
  11.3 0.1 collective-permute-start.4
  11.4 1.1 %collective-permute-done.4.received = bf16[12,8,128]{2,1,0:T(8,128)(2,1)S(1)} collective-permute-done((bf16[12,8,128]{2,1,0:T(8,128)(2,1)S(1)}, bf16[12,8,128]{2,1,0:T(8,128)(2,1)S(1)}, u32[]{:S(2)}, u32[]{:S(2)}) %collective-permute-start.4) | collective-permute-done | bytes 24608 | tf_op jit(solution)/shard_map/ppermute | solution.py:20
  12.5 0.0 copy-done
  12.5 0.0 copy-done.1
  12.5 5.6 %shard_map.92 = bf16[2,4,128,128]{3,2,1,0:T(8,128)(2,1)} custom-call(bf16[12,8,128]{2,1,0:T(8,128)(2,1)S(1)} %constant_dynamic-update-slice_fusion.3.held, bf16[12,8,128]{2,1,0:T(8,128)(2,1)S(1)} %collective-permute-done.4.received, bf16[10,80,512]{2,1,0:T(8,128)(2,1)S(1)} %get-tuple-element.29.w1, f32[1,512]{1,0:T(1,128)S(1)} %get-tuple-element.30.b1, ...), custom_call_target="tpu_custom_call" | custom-call | flops 4000000000 | bytes 10000000 | tf_op jit(solution)/shard_map/pallas_call | solution.py:262
  (6 shorter events, 0.0 us)
Async XLA Ops:
  0.0 3.5 %collective-permute-start = (bf16[1,8,128]{2,1,0:T(8,128)(2,1)}, bf16[1,8,128]{2,1,0:T(8,128)(2,1)S(1)}, u32[]{:S(2)}, u32[]{:S(2)}) collective-permute-start(bf16[1,8,128]{2,1,0:T(8,128)(2,1)} %bitcast.10), channel_id=1, source_target_pairs={{0,3},{1,2},{2,1},{3,0},{4,7},{5,6},{6,5},{7,4},{8,11},{9,10},{10,... | collective-permute-start | bytes 6152 | tf_op jit(solution)/shard_map/ppermute | solution.py:20
  0.8 11.7 %copy-start = (bf16[3,3,3,512,256]{4,3,2,1,0:T(8,128)(2,1)S(1)}, bf16[3,3,3,512,256]{4,3,2,1,0:T(8,128)(2,1)}, u32[]{:S(2)}) copy-start(bf16[3,3,3,512,256]{4,3,2,1,0:T(8,128)(2,1)} %w2.1) | copy-start | bytes 21233668
  0.8 11.7 %copy-start.1 = (bf16[3,3,3,256,128]{4,3,2,1,0:T(8,128)(2,1)S(1)}, bf16[3,3,3,256,128]{4,3,2,1,0:T(8,128)(2,1)}, u32[]{:S(2)}) copy-start(bf16[3,3,3,256,128]{4,3,2,1,0:T(8,128)(2,1)} %w3.1) | copy-start | bytes 5308420
  3.5 3.1 %collective-permute-start.1 = (bf16[2,8,128]{2,1,0:T(8,128)(2,1)S(1)}, bf16[2,8,128]{2,1,0:T(8,128)(2,1)S(1)}, u32[]{:S(2)}, u32[]{:S(2)}) collective-permute-start(bf16[2,8,128]{2,1,0:T(8,128)(2,1)S(1)} %pad_maximum_fusion), channel_id=1, source_target_pairs={{0,5},{1,4},{2,7},{3,6},{4,1},{5,0},{6,3},{7,2},{8,13},{9,12},{10,... | collective-permute-start | bytes 12296 | tf_op jit(solution)/shard_map/ppermute | solution.py:20
  6.6 3.1 %collective-permute-start.2 = (bf16[4,8,128]{2,1,0:T(8,128)(2,1)S(1)}, bf16[4,8,128]{2,1,0:T(8,128)(2,1)S(1)}, u32[]{:S(2)}, u32[]{:S(2)}) collective-permute-start(bf16[4,8,128]{2,1,0:T(8,128)(2,1)S(1)} %get-tuple-element.35), channel_id=1, source_target_pairs={{0,9},{1,8},{2,11},{3,10},{4,13},{5,12},{6,15},{7,14},{8,1},{9,0},... | collective-permute-start | bytes 24584 | tf_op jit(solution)/shard_map/ppermute | solution.py:20
  8.2 3.1 %collective-permute-start.3 = (bf16[4,8,128]{2,1,0:T(8,128)(2,1)S(1)}, bf16[4,8,128]{2,1,0:T(8,128)(2,1)S(1)}, u32[]{:S(2)}, u32[]{:S(2)}) collective-permute-start(bf16[4,8,128]{2,1,0:T(8,128)(2,1)S(1)} %get-tuple-element.35), channel_id=1, source_target_pairs={{0,1},{1,0},{2,3},{3,2},{4,5},{5,4},{6,7},{7,6},{8,17},{9,16},{10,... | collective-permute-start | bytes 24584 | tf_op jit(solution)/shard_map/ppermute | solution.py:20
  11.3 1.2 %collective-permute-start.4 = (bf16[12,8,128]{2,1,0:T(8,128)(2,1)S(1)}, bf16[12,8,128]{2,1,0:T(8,128)(2,1)S(1)}, u32[]{:S(2)}, u32[]{:S(2)}) collective-permute-start(bf16[12,8,128]{2,1,0:T(8,128)(2,1)S(1)} %constant_dynamic-update-slice_fusion.3.held), channel_id=1, source_target_pairs={{0,1},{1,0},{2,3},{3,2},{4,5},{5,4},{6,7},{7,6},{8,9},{9,8},{10,11... | collective-permute-start | bytes 73736 | tf_op jit(solution)/shard_map/ppermute | solution.py:20

commit v7 on v6

--- a/solution.py
+++ b/solution.py
@@ -20,7 +20,7 @@
     return lax.ppermute(array, AXES, pairs)
 
 
-def gathered_pieces(latent, k1, b1, g1, b2, g2, b3):
+def gathered_pieces(latent, k1, b1, g1, k2, b2, g2, b3):
     seq, tm = lax.axis_size("seq"), lax.axis_size("tm")
     assert seq % 2 == 0 and tm == 4
 
@@ -36,11 +36,19 @@
     *first, own = fetched_first(k1, b1, g1, b2, g2, b3, latent)
     beside, own, *first = lax.optimization_barrier((beside, own, *first))
     held = jnp.concatenate([own, beside])
-    held = jnp.concatenate([held, hop(held, lambda s, t: (s ^ 1, t ^ 1), seq, tm)])
+    k2, _ = lax.optimization_barrier((k2, beside))
+    across = hop(held, lambda s, t: (s ^ 1, t ^ 1), seq, tm)
+    across, *sums0 = lax.optimization_barrier((across, *tap_sums(k2, 0)))
+    held = jnp.concatenate([held, across])
+    k2, _ = lax.optimization_barrier((k2, across))
     even = hop(held, z_partner(0), seq, tm)
     odd = hop(held, z_partner(1), seq, tm)
+    even, odd, *sums1 = lax.optimization_barrier((even, odd, *tap_sums(k2, 1)))
     held = jnp.concatenate([held, even, odd])
-    return held, hop(held, lambda s, t: (s, t ^ 1), seq, tm), first
+    k2, _ = lax.optimization_barrier((k2, even))
+    received = hop(held, lambda s, t: (s, t ^ 1), seq, tm)
+    sums2 = tap_sums(k2, 2)
+    return held, received, first, [*sums0, *sums1, *sums2], k2
 
 
 def normed(hidden, gain):
@@ -86,6 +94,31 @@
     )(*in_hbm(k1.reshape(3, 9, 16, c1), *rows, latent))
 
 
+def tap_sums_kernel(i, k2, low, high, full):
+    def part(n, _):
+        k, at = n // 8, pl.ds(pl.multiple_of(n % 8 * 64, 64), 64)
+        a, b, c = [k2[i, j, k, at, :].astype(F32) for j in range(3)]
+        ab = a + b
+        low[k, at, :] = ab.astype(BF16)
+        high[k, at, :] = (b + c).astype(BF16)
+        full[k, at, :] = (ab + c).astype(BF16)
+        return 0
+
+    lax.fori_loop(0, 24, part, 0)
+
+
+def tap_sums(k2, i):
+    vmem = pl.BlockSpec(memory_space=pltpu.VMEM)
+    return pl.pallas_call(
+        functools.partial(tap_sums_kernel, i),
+        out_shape=[pltpu.VMEM(k2.shape[2:], BF16)] * 3,
+        in_specs=[vmem],
+        out_specs=[vmem] * 3,
+        compiler_params=pltpu.CompilerParams(vmem_limit_bytes=1024 * 1024),
+        cost_estimate=pl.CostEstimate(flops=0, bytes_accessed=4_000_000, transcendentals=0),
+    )(k2)
+
+
 def decode_kernel(
     rows_total,
     held,
@@ -96,6 +129,15 @@
     b2,
     g2,
     b3,
+    low0,
+    high0,
+    full0,
+    low1,
+    high1,
+    full1,
+    low2,
+    high2,
+    full2,
     w2,
     w3,
     out_hbm,
@@ -103,8 +145,10 @@
     shifted,
     patches,
     first_act,
-    edge,
+    difference,
+    upper_sums,
     middle_sums,
+    lower_sums,
     second_act,
     outer3,
     middle3,
@@ -169,32 +213,48 @@
         for v in range(3):
             first_act[:, 2 * v + b] = act[v]
 
-    def lhs(rows):
-        m = (rows.stop - rows.start) * 128
-        return [first_act[rows, i : i + 4].reshape(m, 512) for i in range(3)]
-
-    def taps2(i, j):
-        return jnp.concatenate([w2[i, j, k] for k in range(3)], axis=1)
-
-    edge[...] = jnp.dot(
-        jnp.concatenate(lhs(slice(0, 2)) + lhs(slice(1, 3)), axis=1),
-        jnp.concatenate([taps2(i, j) for j in (0, 2) for i in range(3)], axis=0),
+    v0, v1, v2 = [first_act[r].astype(F32) for r in range(3)]
+    difference[0] = (v0 - v1).astype(BF16)
+    difference[1] = (v1 - v2).astype(BF16)
+
+    def lhs(ref, r):
+        return jnp.concatenate([ref[r, i : i + 4].reshape(128, 512) for i in range(3)], axis=1)
+
+    def side_by_side(taps):
+        return jnp.concatenate(
+            [jnp.concatenate([tap[k] for tap in of_i for k in range(3)], axis=1) for of_i in taps],
+            axis=0,
+        )
+
+    upper_sums[...] = jnp.dot(
+        lhs(difference, 0),
+        side_by_side([(low, w2.at[i, 0]) for i, low in enumerate((low0, low1, low2))]),
         preferred_element_type=F32,
     )
     middle_sums[...] = jnp.dot(
-        jnp.concatenate(lhs(slice(0, 3)), axis=1),
-        jnp.concatenate([taps2(i, 1) for i in range(3)], axis=0),
+        lhs(first_act, 1),
+        side_by_side([(full,) for full in (full0, full1, full2)]),
         preferred_element_type=F32,
     )
+    lower_sums[...] = jnp.dot(
+        lhs(difference, 1),
+        side_by_side([(w2.at[i, 2], high) for i, high in enumerate((high0, high1, high2))]),
+        preferred_element_type=F32,
+    )
 
     column = lax.broadcasted_iota(jnp.int32, (4, 32, 256), 1)
 
     def second_norm(p):
-        e, m = p // 2 * 128, (p + 1) // 2 * 128
-        a, b, d = [
-            (edge[e : e + 128, lanes] + middle_sums[m : m + 128, lanes]).reshape(4, 32, 256)
-            for lanes in (slice(k * 256, (k + 1) * 256) for k in range(3))
-        ]
+        def sums(k):
+            both, own = k * 256, (p % 2 * 3 + k) * 256
+            shared = middle_sums[:, both : both + 256]
+            if p < 2:
+                total = shared + upper_sums[:, own : own + 256]
+            else:
+                total = shared - lower_sums[:, own : own + 256]
+            return total.reshape(4, 32, 256)
+
+        a, b, d = [sums(k) for k in range(3)]
         a_left = jnp.where(column == 0, a, pltpu.roll(a, 1, 1))
         d_right = jnp.where(column == 31, d, pltpu.roll(d, 31, 1))
         second_act[p, 0] = normed(a_left + (b + b2[...]) + d, g2[...])
@@ -255,22 +315,26 @@
     tm = lax.axis_size("tm")
     rows_total = lax.axis_size("seq")
     c1, c2, c3 = k1.shape[4], k2.shape[4], k3.shape[4]
-    held, received, first = gathered_pieces(latent, k1, b1, g1, b2, g2, b3)
+    held, received, first, sums, k2 = gathered_pieces(
+        latent, k1, b1, g1, k2, b2, g2, b3
+    )
     vmem = pl.BlockSpec(memory_space=pltpu.VMEM)
     hbm = pl.BlockSpec(memory_space=pltpu.HBM)
     out_frames = frames // tm
     return pl.pallas_call(
         functools.partial(decode_kernel, rows_total),
         out_shape=jax.ShapeDtypeStruct((out_frames, 4, 128, c3), BF16),
-        in_specs=[vmem] * 10,
+        in_specs=[vmem] * 19,
         out_specs=hbm,
         scratch_shapes=[
             pltpu.VMEM((24, frames, 128), F32),
             pltpu.VMEM((4, 5, 3, 32, 128), BF16),
             pltpu.VMEM((3, 3, 32, 640), BF16),
             pltpu.VMEM((3, 6, 32, c1), BF16),
-            pltpu.VMEM((256, 3 * c2), F32),
-            pltpu.VMEM((384, 3 * c2), F32),
+            pltpu.VMEM((2, 6, 32, c1), BF16),
+            pltpu.VMEM((128, 6 * c2), F32),
+            pltpu.VMEM((128, 3 * c2), F32),
+            pltpu.VMEM((128, 6 * c2), F32),
             pltpu.VMEM((4, 2, 4, 32, c2), BF16),
             pltpu.VMEM((384, 4 * c3), F32),
             pltpu.VMEM((256, 2 * c3), F32),
@@ -282,7 +346,7 @@
         cost_estimate=pl.CostEstimate(
             flops=4_000_000_000, bytes_accessed=10_000_000, transcendentals=600_000
         ),
-    )(held, received, *first, k2, k3)
+    )(held, received, *first, *sums, k2, k3)
 
 
 def solution(mesh):

time: 18.3 us -> 18.2 us (level)
  the two profiles are of different devices: /device:TPU:21 before, /device:TPU:0 now
where the time goes in v7:
time: 18.2 us; the launch traced here: 18 us
  Pallas kernels  8.01 us (44%)
  starting transfers between devices  7.87 us (43%)
  waiting for transfers between devices  2.04 us (11%)
    ppermute x5, starting transfers between devices, hop(): return lax.ppermute(array, AXES, pairs)  7.87 us
    pallas_call x1, Pallas kernels, per_device(): pl.pallas_call(functools.partial(decode_kernel, rows_total), out_shape=ja...  4.74 us
    ppermute x5, waiting for transfers between devices, hop(): return lax.ppermute(array, AXES, pairs)  2.04 us
    pallas_call x3, Pallas kernels, tap_sums(): pl.pallas_call(functools.partial(tap_sums_kernel, i), out_shape=[pltpu.VM...  1.9 us
    pallas_call x1, Pallas kernels, fetched_first(): pl.pallas_call(first_weights_kernel, out_shape=shapes + [pltpu.VMEM((1,)...  1.38 us
  transfers between devices with their start and end apart: 5, of which 4 were waited for; matrix products, arithmetic and copies ran while one was open for 0% of the time, Pallas kernels for 18%

profile of v7, /device:TPU:0, one launch (start us, length us, event | category | flops | bytes accessed | tf_op | source)
XLA Modules:
  0.0 18.0 jit_solution(17865048165423712097)
XLA Ops:
  0.0 2.4 %collective-permute-start = (bf16[1,8,128]{2,1,0:T(8,128)(2,1)}, bf16[1,8,128]{2,1,0:T(8,128)(2,1)S(1)}, u32[]{:S(2)}, u32[]{:S(2)}) collective-permute-start(bf16[1,8,128]{2,1,0:T(8,128)(2,1)} %bitcast.10), channel_id=1, source_target_pairs={{0,3},{1,2},{2,1},{3,0},{4,7},{5,6},{6,5},{7,4},{8,11},{9,10},{10,... | collective-permute-start | bytes 6152 | tf_op jit(solution)/shard_map/ppermute | solution.py:20
  2.4 0.0 copy-start
  2.4 1.4 %shard_map.91 = (bf16[10,80,512]{2,1,0:T(8,128)(2,1)S(1)}, f32[1,512]{1,0:T(1,128)S(1)}, f32[1,512]{1,0:T(1,128)S(1)}, f32[1,256]{1,0:T(1,128)S(1)}, f32[1,256]{...) custom-call(bf16[3,9,16,512]{3,2,1,0:T(8,128)(2,1)} %bitcast.7, f32[1,512]{1,0:T(1,128)} %bitcast.8, ...), custom_call_target="tpu_custom_call" | custom-call | flops 10000000000 | bytes 40000000 | tf_op jit(solution)/shard_map/pallas_call | solution.py:86
  3.8 0.1 collective-permute-done
  3.9 2.0 %collective-permute-start.1 = (bf16[2,8,128]{2,1,0:T(8,128)(2,1)S(1)}, bf16[2,8,128]{2,1,0:T(8,128)(2,1)S(1)}, u32[]{:S(2)}, u32[]{:S(2)}) collective-permute-start(bf16[2,8,128]{2,1,0:T(8,128)(2,1)S(1)} %pad_maximum_fusion), channel_id=1, source_target_pairs={{0,5},{1,4},{2,7},{3,6},{4,1},{5,0},{6,3},{7,2},{8,13},{9,12},{10,... | collective-permute-start | bytes 12296 | tf_op jit(solution)/shard_map/ppermute | solution.py:20
  6.0 0.0 copy-done
  6.0 0.6 %shard_map.92 = (bf16[3,512,256]{2,1,0:T(8,128)(2,1)S(1)}, bf16[3,512,256]{2,1,0:T(8,128)(2,1)S(1)}, bf16[3,512,256]{2,1,0:T(8,128)(2,1)S(1)}) custom-call(bf16[3,3,3,512,256]{4,3,2,1,0:T(8,128)(2,1)S(1)} %copy-done), custom_call_target="tpu_custom_call" | custom-call | bytes 4000000 | tf_op jit(solution)/shard_map/pallas_call | solution.py:112
  6.6 0.7 %collective-permute-done.1 = bf16[2,8,128]{2,1,0:T(8,128)(2,1)S(1)} collective-permute-done((bf16[2,8,128]{2,1,0:T(8,128)(2,1)S(1)}, bf16[2,8,128]{2,1,0:T(8,128)(2,1)S(1)}, u32[]{:S(2)}, u32[]{:S(2)}) %collective-permute-start.1) | collective-permute-done | bytes 4128 | tf_op jit(solution)/shard_map/ppermute | solution.py:20
  7.3 0.0 copy-start.1
  7.3 0.4 %collective-permute-start.3 = (bf16[4,8,128]{2,1,0:T(8,128)(2,1)S(1)}, bf16[4,8,128]{2,1,0:T(8,128)(2,1)S(1)}, u32[]{:S(2)}, u32[]{:S(2)}) collective-permute-start(bf16[4,8,128]{2,1,0:T(8,128)(2,1)S(1)} %get-tuple-element.77), channel_id=1, source_target_pairs={{0,1},{1,0},{2,3},{3,2},{4,5},{5,4},{6,7},{7,6},{8,17},{9,16},{10,... | collective-permute-start | bytes 24584 | tf_op jit(solution)/shard_map/ppermute | solution.py:20
  7.7 3.0 %collective-permute-start.2 = (bf16[4,8,128]{2,1,0:T(8,128)(2,1)S(1)}, bf16[4,8,128]{2,1,0:T(8,128)(2,1)S(1)}, u32[]{:S(2)}, u32[]{:S(2)}) collective-permute-start(bf16[4,8,128]{2,1,0:T(8,128)(2,1)S(1)} %get-tuple-element.77), channel_id=1, source_target_pairs={{0,9},{1,8},{2,11},{3,10},{4,13},{5,12},{6,15},{7,14},{8,1},{9,0},... | collective-permute-start | bytes 24584 | tf_op jit(solution)/shard_map/ppermute | solution.py:20
  10.7 0.6 %shard_map.93 = (bf16[3,512,256]{2,1,0:T(8,128)(2,1)S(1)}, bf16[3,512,256]{2,1,0:T(8,128)(2,1)S(1)}, bf16[3,512,256]{2,1,0:T(8,128)(2,1)S(1)}) custom-call(bf16[3,3,3,512,256]{4,3,2,1,0:T(8,128)(2,1)S(1)} %copy-done), custom_call_target="tpu_custom_call" | custom-call | bytes 4000000 | tf_op jit(solution)/shard_map/pallas_call | solution.py:112
  11.3 0.0 collective-permute-done.3
  11.3 0.7 %collective-permute-done.2 = bf16[4,8,128]{2,1,0:T(8,128)(2,1)S(1)} collective-permute-done((bf16[4,8,128]{2,1,0:T(8,128)(2,1)S(1)}, bf16[4,8,128]{2,1,0:T(8,128)(2,1)S(1)}, u32[]{:S(2)}, u32[]{:S(2)}) %collective-permute-start.2) | collective-permute-done | bytes 8224 | tf_op jit(solution)/shard_map/ppermute | solution.py:20
  12.1 0.0 collective-permute-start.4
  12.1 0.6 %shard_map.94 = (bf16[3,512,256]{2,1,0:T(8,128)(2,1)S(1)}, bf16[3,512,256]{2,1,0:T(8,128)(2,1)S(1)}, bf16[3,512,256]{2,1,0:T(8,128)(2,1)S(1)}) custom-call(bf16[3,3,3,512,256]{4,3,2,1,0:T(8,128)(2,1)S(1)} %copy-done), custom_call_target="tpu_custom_call" | custom-call | bytes 4000000 | tf_op jit(solution)/shard_map/pallas_call | solution.py:112
  12.8 0.5 %collective-permute-done.4.received = bf16[12,8,128]{2,1,0:T(8,128)(2,1)S(1)} collective-permute-done((bf16[12,8,128]{2,1,0:T(8,128)(2,1)S(1)}, bf16[12,8,128]{2,1,0:T(8,128)(2,1)S(1)}, u32[]{:S(2)}, u32[]{:S(2)}) %collective-permute-start.4) | collective-permute-done | bytes 24608 | tf_op jit(solution)/shard_map/ppermute | solution.py:20
  13.3 0.0 copy-done.1
  13.3 4.7 %shard_map.95 = bf16[2,4,128,128]{3,2,1,0:T(8,128)(2,1)} custom-call(bf16[12,8,128]{2,1,0:T(8,128)(2,1)S(1)} %constant_dynamic-update-slice_fusion.3.held, bf16[12,8,128]{2,1,0:T(8,128)(2,1)S(1)} %collective-permute-done.4.received, bf16[10,80,512]{2,1,0:T(8,128)(2,1)S(1)} %get-tuple-element.61.w1, f32[1,512]{1,0:T(1,128)S(1)} %get-tuple-element.62.b1, ...), custom_call_target="tpu_custom_call" | custom-call | flops 4000000000 | bytes 10000000 | tf_op jit(solution)/shard_map/pallas_call | solution.py:324
  (6 shorter events, 0.0 us)
Async XLA Ops:
  0.0 3.9 %collective-permute-start = (bf16[1,8,128]{2,1,0:T(8,128)(2,1)}, bf16[1,8,128]{2,1,0:T(8,128)(2,1)S(1)}, u32[]{:S(2)}, u32[]{:S(2)}) collective-permute-start(bf16[1,8,128]{2,1,0:T(8,128)(2,1)} %bitcast.10), channel_id=1, source_target_pairs={{0,3},{1,2},{2,1},{3,0},{4,7},{5,6},{6,5},{7,4},{8,11},{9,10},{10,... | collective-permute-start | bytes 6152 | tf_op jit(solution)/shard_map/ppermute | solution.py:20
  2.4 3.6 %copy-start = (bf16[3,3,3,512,256]{4,3,2,1,0:T(8,128)(2,1)S(1)}, bf16[3,3,3,512,256]{4,3,2,1,0:T(8,128)(2,1)}, u32[]{:S(2)}) copy-start(bf16[3,3,3,512,256]{4,3,2,1,0:T(8,128)(2,1)} %w2) | copy-start | bytes 21233668
  3.9 3.3 %collective-permute-start.1 = (bf16[2,8,128]{2,1,0:T(8,128)(2,1)S(1)}, bf16[2,8,128]{2,1,0:T(8,128)(2,1)S(1)}, u32[]{:S(2)}, u32[]{:S(2)}) collective-permute-start(bf16[2,8,128]{2,1,0:T(8,128)(2,1)S(1)} %pad_maximum_fusion), channel_id=1, source_target_pairs={{0,5},{1,4},{2,7},{3,6},{4,1},{5,0},{6,3},{7,2},{8,13},{9,12},{10,... | collective-permute-start | bytes 12296 | tf_op jit(solution)/shard_map/ppermute | solution.py:20
  7.3 6.0 %copy-start.1 = (bf16[3,3,3,256,128]{4,3,2,1,0:T(8,128)(2,1)S(1)}, bf16[3,3,3,256,128]{4,3,2,1,0:T(8,128)(2,1)}, u32[]{:S(2)}) copy-start(bf16[3,3,3,256,128]{4,3,2,1,0:T(8,128)(2,1)} %w3.1) | copy-start | bytes 5308420
  7.3 4.0 %collective-permute-start.3 = (bf16[4,8,128]{2,1,0:T(8,128)(2,1)S(1)}, bf16[4,8,128]{2,1,0:T(8,128)(2,1)S(1)}, u32[]{:S(2)}, u32[]{:S(2)}) collective-permute-start(bf16[4,8,128]{2,1,0:T(8,128)(2,1)S(1)} %get-tuple-element.77), channel_id=1, source_target_pairs={{0,1},{1,0},{2,3},{3,2},{4,5},{5,4},{6,7},{7,6},{8,17},{9,16},{10,... | collective-permute-start | bytes 24584 | tf_op jit(solution)/shard_map/ppermute | solution.py:20
  7.7 4.4 %collective-permute-start.2 = (bf16[4,8,128]{2,1,0:T(8,128)(2,1)S(1)}, bf16[4,8,128]{2,1,0:T(8,128)(2,1)S(1)}, u32[]{:S(2)}, u32[]{:S(2)}) collective-permute-start(bf16[4,8,128]{2,1,0:T(8,128)(2,1)S(1)} %get-tuple-element.77), channel_id=1, source_target_pairs={{0,9},{1,8},{2,11},{3,10},{4,13},{5,12},{6,15},{7,14},{8,1},{9,0},... | collective-permute-start | bytes 24584 | tf_op jit(solution)/shard_map/ppermute | solution.py:20
  12.1 1.2 %collective-permute-start.4 = (bf16[12,8,128]{2,1,0:T(8,128)(2,1)S(1)}, bf16[12,8,128]{2,1,0:T(8,128)(2,1)S(1)}, u32[]{:S(2)}, u32[]{:S(2)}) collective-permute-start(bf16[12,8,128]{2,1,0:T(8,128)(2,1)S(1)} %constant_dynamic-update-slice_fusion.3.held), channel_id=1, source_target_pairs={{0,1},{1,0},{2,3},{3,2},{4,5},{5,4},{6,7},{7,6},{8,9},{9,8},{10,11... | collective-permute-start | bytes 73736 | tf_op jit(solution)/shard_map/ppermute | solution.py:20

commit v8 on v7

--- a/solution.py
+++ b/solution.py
@@ -43,7 +43,7 @@
     k2, _ = lax.optimization_barrier((k2, across))
     even = hop(held, z_partner(0), seq, tm)
     odd = hop(held, z_partner(1), seq, tm)
-    even, odd, *sums1 = lax.optimization_barrier((even, odd, *tap_sums(k2, 1)))
+    odd, even, *sums1 = lax.optimization_barrier((odd, even, *tap_sums(k2, 1)))
     held = jnp.concatenate([held, even, odd])
     k2, _ = lax.optimization_barrier((k2, even))
     received = hop(held, lambda s, t: (s, t ^ 1), seq, tm)

time: 18.2 us -> 17.4 us (0.956)
  the two profiles are of different devices: /device:TPU:0 before, /device:TPU:23 now
where the time goes in v8:
time: 17.4 us; the launch traced here: 17.3 us
  Pallas kernels  8.01 us (46%)
  waiting for transfers between devices  6.12 us (35%)
  starting transfers between devices  3.04 us (17%)
    ppermute x5, waiting for transfers between devices, hop(): return lax.ppermute(array, AXES, pairs)  6.12 us
    pallas_call x1, Pallas kernels, per_device(): pl.pallas_call(functools.partial(decode_kernel, rows_total), out_shape=ja...  4.74 us
    ppermute x5, starting transfers between devices, hop(): return lax.ppermute(array, AXES, pairs)  3.04 us
    pallas_call x3, Pallas kernels, tap_sums(): pl.pallas_call(functools.partial(tap_sums_kernel, i), out_shape=[pltpu.VM...  1.9 us
    pallas_call x1, Pallas kernels, fetched_first(): pl.pallas_call(first_weights_kernel, out_shape=shapes + [pltpu.VMEM((1,)...  1.38 us
  transfers between devices with their start and end apart: 5, of which 5 were waited for; matrix products, arithmetic and copies ran while one was open for 0% of the time, Pallas kernels for 19%

profile of v8, /device:TPU:23, one launch (start us, length us, event | category | flops | bytes accessed | tf_op | source)
XLA Modules:
  0.0 17.3 jit_solution(15349729049220705921)
XLA Ops:
  0.0 0.8 %collective-permute-start = (bf16[1,8,128]{2,1,0:T(8,128)(2,1)}, bf16[1,8,128]{2,1,0:T(8,128)(2,1)S(1)}, u32[]{:S(2)}, u32[]{:S(2)}) collective-permute-start(bf16[1,8,128]{2,1,0:T(8,128)(2,1)} %bitcast.10), channel_id=1, source_target_pairs={{0,3},{1,2},{2,1},{3,0},{4,7},{5,6},{6,5},{7,4},{8,11},{9,10},{10,... | collective-permute-start | bytes 6152 | tf_op jit(solution)/shard_map/ppermute | solution.py:20
  0.8 0.0 copy-start
  0.8 1.4 %shard_map.91 = (bf16[10,80,512]{2,1,0:T(8,128)(2,1)S(1)}, f32[1,512]{1,0:T(1,128)S(1)}, f32[1,512]{1,0:T(1,128)S(1)}, f32[1,256]{1,0:T(1,128)S(1)}, f32[1,256]{...) custom-call(bf16[3,9,16,512]{3,2,1,0:T(8,128)(2,1)} %bitcast.7, f32[1,512]{1,0:T(1,128)} %bitcast.8, ...), custom_call_target="tpu_custom_call" | custom-call | flops 10000000000 | bytes 40000000 | tf_op jit(solution)/shard_map/pallas_call | solution.py:86
  2.2 1.3 %collective-permute-done = bf16[1,8,128]{2,1,0:T(8,128)(2,1)S(1)} collective-permute-done((bf16[1,8,128]{2,1,0:T(8,128)(2,1)}, bf16[1,8,128]{2,1,0:T(8,128)(2,1)S(1)}, u32[]{:S(2)}, u32[]{:S(2)}) %collective-permute-start) | collective-permute-done | bytes 2080 | tf_op jit(solution)/shard_map/ppermute | solution.py:20
  3.5 0.6 %collective-permute-start.1 = (bf16[2,8,128]{2,1,0:T(8,128)(2,1)S(1)}, bf16[2,8,128]{2,1,0:T(8,128)(2,1)S(1)}, u32[]{:S(2)}, u32[]{:S(2)}) collective-permute-start(bf16[2,8,128]{2,1,0:T(8,128)(2,1)S(1)} %pad_maximum_fusion), channel_id=1, source_target_pairs={{0,5},{1,4},{2,7},{3,6},{4,1},{5,0},{6,3},{7,2},{8,13},{9,12},{10,... | collective-permute-start | bytes 12296 | tf_op jit(solution)/shard_map/ppermute | solution.py:20
  4.1 0.0 copy-done
  4.1 0.6 %shard_map.92 = (bf16[3,512,256]{2,1,0:T(8,128)(2,1)S(1)}, bf16[3,512,256]{2,1,0:T(8,128)(2,1)S(1)}, bf16[3,512,256]{2,1,0:T(8,128)(2,1)S(1)}) custom-call(bf16[3,3,3,512,256]{4,3,2,1,0:T(8,128)(2,1)S(1)} %copy-done), custom_call_target="tpu_custom_call" | custom-call | bytes 4000000 | tf_op jit(solution)/shard_map/pallas_call | solution.py:112
  4.8 1.8 %collective-permute-done.1 = bf16[2,8,128]{2,1,0:T(8,128)(2,1)S(1)} collective-permute-done((bf16[2,8,128]{2,1,0:T(8,128)(2,1)S(1)}, bf16[2,8,128]{2,1,0:T(8,128)(2,1)S(1)}, u32[]{:S(2)}, u32[]{:S(2)}) %collective-permute-start.1) | collective-permute-done | bytes 4128 | tf_op jit(solution)/shard_map/ppermute | solution.py:20
  6.6 0.0 copy-start.1
  6.6 1.6 %collective-permute-start.3 = (bf16[4,8,128]{2,1,0:T(8,128)(2,1)S(1)}, bf16[4,8,128]{2,1,0:T(8,128)(2,1)S(1)}, u32[]{:S(2)}, u32[]{:S(2)}) collective-permute-start(bf16[4,8,128]{2,1,0:T(8,128)(2,1)S(1)} %get-tuple-element.77), channel_id=1, source_target_pairs={{0,9},{1,8},{2,11},{3,10},{4,13},{5,12},{6,15},{7,14},{8,1},{9,0},... | collective-permute-start | bytes 24584 | tf_op jit(solution)/shard_map/ppermute | solution.py:20
  8.2 0.0 collective-permute-start.2
  8.2 0.6 %shard_map.93 = (bf16[3,512,256]{2,1,0:T(8,128)(2,1)S(1)}, bf16[3,512,256]{2,1,0:T(8,128)(2,1)S(1)}, bf16[3,512,256]{2,1,0:T(8,128)(2,1)S(1)}) custom-call(bf16[3,3,3,512,256]{4,3,2,1,0:T(8,128)(2,1)S(1)} %copy-done), custom_call_target="tpu_custom_call" | custom-call | bytes 4000000 | tf_op jit(solution)/shard_map/pallas_call | solution.py:112
  8.8 0.9 %collective-permute-done.3 = bf16[4,8,128]{2,1,0:T(8,128)(2,1)S(1)} collective-permute-done((bf16[4,8,128]{2,1,0:T(8,128)(2,1)S(1)}, bf16[4,8,128]{2,1,0:T(8,128)(2,1)S(1)}, u32[]{:S(2)}, u32[]{:S(2)}) %collective-permute-start.3) | collective-permute-done | bytes 8224 | tf_op jit(solution)/shard_map/ppermute | solution.py:20
  9.7 1.6 %collective-permute-done.2 = bf16[4,8,128]{2,1,0:T(8,128)(2,1)S(1)} collective-permute-done((bf16[4,8,128]{2,1,0:T(8,128)(2,1)S(1)}, bf16[4,8,128]{2,1,0:T(8,128)(2,1)S(1)}, u32[]{:S(2)}, u32[]{:S(2)}) %collective-permute-start.2) | collective-permute-done | bytes 8224 | tf_op jit(solution)/shard_map/ppermute | solution.py:20
  11.3 0.1 collective-permute-start.4
  11.4 0.6 %shard_map.94 = (bf16[3,512,256]{2,1,0:T(8,128)(2,1)S(1)}, bf16[3,512,256]{2,1,0:T(8,128)(2,1)S(1)}, bf16[3,512,256]{2,1,0:T(8,128)(2,1)S(1)}) custom-call(bf16[3,3,3,512,256]{4,3,2,1,0:T(8,128)(2,1)S(1)} %copy-done), custom_call_target="tpu_custom_call" | custom-call | bytes 4000000 | tf_op jit(solution)/shard_map/pallas_call | solution.py:112
  12.0 0.5 %collective-permute-done.4.received = bf16[12,8,128]{2,1,0:T(8,128)(2,1)S(1)} collective-permute-done((bf16[12,8,128]{2,1,0:T(8,128)(2,1)S(1)}, bf16[12,8,128]{2,1,0:T(8,128)(2,1)S(1)}, u32[]{:S(2)}, u32[]{:S(2)}) %collective-permute-start.4) | collective-permute-done | bytes 24608 | tf_op jit(solution)/shard_map/ppermute | solution.py:20
  12.5 0.0 copy-done.1
  12.5 4.7 %shard_map.95 = bf16[2,4,128,128]{3,2,1,0:T(8,128)(2,1)} custom-call(bf16[12,8,128]{2,1,0:T(8,128)(2,1)S(1)} %constant_dynamic-update-slice_fusion.3.held, bf16[12,8,128]{2,1,0:T(8,128)(2,1)S(1)} %collective-permute-done.4.received, bf16[10,80,512]{2,1,0:T(8,128)(2,1)S(1)} %get-tuple-element.61.w1, f32[1,512]{1,0:T(1,128)S(1)} %get-tuple-element.62.b1, ...), custom_call_target="tpu_custom_call" | custom-call | flops 4000000000 | bytes 10000000 | tf_op jit(solution)/shard_map/pallas_call | solution.py:324
  (6 shorter events, 0.0 us)
Async XLA Ops:
  0.0 3.5 %collective-permute-start = (bf16[1,8,128]{2,1,0:T(8,128)(2,1)}, bf16[1,8,128]{2,1,0:T(8,128)(2,1)S(1)}, u32[]{:S(2)}, u32[]{:S(2)}) collective-permute-start(bf16[1,8,128]{2,1,0:T(8,128)(2,1)} %bitcast.10), channel_id=1, source_target_pairs={{0,3},{1,2},{2,1},{3,0},{4,7},{5,6},{6,5},{7,4},{8,11},{9,10},{10,... | collective-permute-start | bytes 6152 | tf_op jit(solution)/shard_map/ppermute | solution.py:20
  0.8 3.3 %copy-start = (bf16[3,3,3,512,256]{4,3,2,1,0:T(8,128)(2,1)S(1)}, bf16[3,3,3,512,256]{4,3,2,1,0:T(8,128)(2,1)}, u32[]{:S(2)}) copy-start(bf16[3,3,3,512,256]{4,3,2,1,0:T(8,128)(2,1)} %w2) | copy-start | bytes 21233668
  3.5 3.1 %collective-permute-start.1 = (bf16[2,8,128]{2,1,0:T(8,128)(2,1)S(1)}, bf16[2,8,128]{2,1,0:T(8,128)(2,1)S(1)}, u32[]{:S(2)}, u32[]{:S(2)}) collective-permute-start(bf16[2,8,128]{2,1,0:T(8,128)(2,1)S(1)} %pad_maximum_fusion), channel_id=1, source_target_pairs={{0,5},{1,4},{2,7},{3,6},{4,1},{5,0},{6,3},{7,2},{8,13},{9,12},{10,... | collective-permute-start | bytes 12296 | tf_op jit(solution)/shard_map/ppermute | solution.py:20
  6.6 5.9 %copy-start.1 = (bf16[3,3,3,256,128]{4,3,2,1,0:T(8,128)(2,1)S(1)}, bf16[3,3,3,256,128]{4,3,2,1,0:T(8,128)(2,1)}, u32[]{:S(2)}) copy-start(bf16[3,3,3,256,128]{4,3,2,1,0:T(8,128)(2,1)} %w3.1) | copy-start | bytes 5308420
  6.6 3.1 %collective-permute-start.3 = (bf16[4,8,128]{2,1,0:T(8,128)(2,1)S(1)}, bf16[4,8,128]{2,1,0:T(8,128)(2,1)S(1)}, u32[]{:S(2)}, u32[]{:S(2)}) collective-permute-start(bf16[4,8,128]{2,1,0:T(8,128)(2,1)S(1)} %get-tuple-element.77), channel_id=1, source_target_pairs={{0,9},{1,8},{2,11},{3,10},{4,13},{5,12},{6,15},{7,14},{8,1},{9,0},... | collective-permute-start | bytes 24584 | tf_op jit(solution)/shard_map/ppermute | solution.py:20
  8.2 3.1 %collective-permute-start.2 = (bf16[4,8,128]{2,1,0:T(8,128)(2,1)S(1)}, bf16[4,8,128]{2,1,0:T(8,128)(2,1)S(1)}, u32[]{:S(2)}, u32[]{:S(2)}) collective-permute-start(bf16[4,8,128]{2,1,0:T(8,128)(2,1)S(1)} %get-tuple-element.77), channel_id=1, source_target_pairs={{0,1},{1,0},{2,3},{3,2},{4,5},{5,4},{6,7},{7,6},{8,17},{9,16},{10,... | collective-permute-start | bytes 24584 | tf_op jit(solution)/shard_map/ppermute | solution.py:20
  11.3 1.2 %collective-permute-start.4 = (bf16[12,8,128]{2,1,0:T(8,128)(2,1)S(1)}, bf16[12,8,128]{2,1,0:T(8,128)(2,1)S(1)}, u32[]{:S(2)}, u32[]{:S(2)}) collective-permute-start(bf16[12,8,128]{2,1,0:T(8,128)(2,1)S(1)} %constant_dynamic-update-slice_fusion.3.held), channel_id=1, source_target_pairs={{0,1},{1,0},{2,3},{3,2},{4,5},{5,4},{6,7},{7,6},{8,9},{9,8},{10,11... | collective-permute-start | bytes 73736 | tf_op jit(solution)/shard_map/ppermute | solution.py:20

commit v9 on v8

--- a/solution.py
+++ b/solution.py
@@ -63,14 +63,12 @@
     pairs = [(b1_in, b1), (g1_in, g1), (b2_in, b2), (g2_in, g2), (b3_in, b3)]
     pairs.append((latent, own.at[0]))
     for i in range(3):
-        pairs.append((k1.at[i], w1.at[pl.ds(0, 9), pl.ds(16 * (1 + i), 16)]))
+        for n in range(9):
+            pairs.append((k1.at[i, n], w1.at[pl.ds(48 * n + 16 * i, 16)]))
     copies = [pltpu.make_async_copy(a, b, sem.at[n]) for n, (a, b) in enumerate(pairs)]
     for copy in copies:
         copy.start()
-    zeros = jnp.zeros((9, 16, w1.shape[2]), BF16)
-    w1[:9, :16] = zeros
-    w1[:9, 64:] = zeros
-    w1[9] = jnp.zeros(w1.shape[1:], BF16)
+    w1[432:] = jnp.zeros((80, w1.shape[1]), BF16)
     for copy in copies:
         copy.wait()
 
@@ -82,13 +80,13 @@
 def fetched_first(k1, b1, g1, b2, g2, b3, latent):
     c1 = k1.shape[4]
     rows = [v.reshape(1, -1) for v in (b1, g1, b2, g2, b3)]
-    shapes = [pltpu.VMEM((10, 80, c1), BF16)] + [pltpu.VMEM(v.shape, F32) for v in rows]
+    shapes = [pltpu.VMEM((512, c1), BF16)] + [pltpu.VMEM(v.shape, F32) for v in rows]
     return pl.pallas_call(
         first_weights_kernel,
         out_shape=shapes + [pltpu.VMEM((1,) + latent.shape, BF16)],
         in_specs=[pl.BlockSpec(memory_space=pltpu.HBM)] * 7,
         out_specs=[pl.BlockSpec(memory_space=pltpu.VMEM)] * 7,
-        scratch_shapes=[pltpu.SemaphoreType.DMA((9,))],
+        scratch_shapes=[pltpu.SemaphoreType.DMA((33,))],
         compiler_params=pltpu.CompilerParams(vmem_limit_bytes=1024 * 1024),
         cost_estimate=pl.CostEstimate(flops=10000000000, bytes_accessed=40000000, transcendentals=0),
     )(*in_hbm(k1.reshape(3, 9, 16, c1), *rows, latent))
@@ -143,7 +141,6 @@
     out_hbm,
     pieces,
     shifted,
-    patches,
     first_act,
     difference,
     upper_sums,
@@ -158,16 +155,16 @@
 ):
     s = lax.axis_index("seq")
     t = lax.axis_index("tm")
-    z, x, y, c = s // 2, s % 2, t // 2, t % 2
+    z, x, y, c = s >> 1, s & 1, t >> 1, t & 1
     n_frames = held.shape[1]
     pieces[:12] = held[...].astype(F32)
     pieces[12:] = received[...].astype(F32)
 
     def piece_of(row, chunk):
-        dz, dx = row // 2 - z, row % 2 ^ x
-        dy, dc = chunk // 2 ^ y, chunk % 2 ^ c
-        group = jnp.where(dz == 0, 0, jnp.where((dz == 1) == (z % 2 == 0), 1, 2))
-        half = (dx + dy + dc + jnp.where(dz == 0, 0, 1)) % 2
+        dz, dx = (row >> 1) - z, (row & 1) ^ x
+        dy, dc = (chunk >> 1) ^ y, (chunk & 1) ^ c
+        group = jnp.where(dz == 0, 0, jnp.where((dz == 1) == ((z & 1) == 0), 1, 2))
+        half = (dx + dy + dc + jnp.where(dz == 0, 0, 1)) & 1
         return half * 12 + group * 4 + 2 * dx + dy
 
     before = n_frames - 2 - 2 * t
@@ -187,31 +184,36 @@
         left = jnp.where(column32 == 0, middle, pltpu.roll(middle, 1, 0))
         right = jnp.where(column32 == 31, middle, pltpu.roll(middle, 31, 0))
         for k, value in enumerate((left, middle, right)):
-            for n, turn in enumerate((0, 96, 64, 32)):
-                turned = pltpu.roll(value, turn, 1) if turn else value
+            for n in range(8):
+                turned = pltpu.roll(value, 16 * n, 1) if n else value
                 shifted[n, d, k] = turned.astype(BF16)
 
-    low = lax.broadcasted_iota(jnp.int32, (32, 128), 1) < 64
+    lane = lax.broadcasted_iota(jnp.int32, (32, 128), 1)
+    near = []
     for r in range(3):
         mine = jnp.clip(s - 1 + r, 0, rows_total - 1)
-        d = [jnp.clip(mine - 1 + j, 0, rows_total - 1) - (s - 2) for j in range(3)]
-        for n in range(5):
-            first, second = 2 * n, min(2 * n + 1, 8)
-            for v in range(3):
-                one = shifted[v, d[first // 3], first % 3]
-                two = shifted[(v + 2) % 4, d[second // 3], second % 3]
-                patches[v, r, :, n * 128 : (n + 1) * 128] = jnp.where(low, one, two)
-
-    for b in range(2):
-        window = slice(16 - 16 * b, 80 - 16 * b)
+        near.append([jnp.clip(mine - 1 + j, 0, rows_total - 1) - (s - 2) for j in range(3)])
+
+    def patch(v, r, n):
+        value = None
+        for tap in range(9):
+            if tap * 48 < n * 128 + 128 and tap * 48 + 48 > n * 128:
+                part = shifted[(3 * tap - v) % 8, near[r][tap // 3], tap % 3]
+                value = part if value is None else jnp.where(lane >= tap * 48 - n * 128, part, value)
+        return value
+
+    for v in range(0, 6, 2):
+        patches = [
+            jnp.concatenate([patch(u, r, n) for n in range(4)], axis=1)
+            for u in (v, v + 1)
+            for r in range(3)
+        ]
         hidden = jnp.dot(
-            patches[...].reshape(288, 640),
-            jnp.concatenate([w1[n, window] for n in range(10)], axis=0),
-            preferred_element_type=F32,
+            jnp.concatenate(patches, axis=0), w1[...], preferred_element_type=F32
         )
-        act = normed(hidden + b1[...], g1[...]).reshape(3, 3, 32, 512)
-        for v in range(3):
-            first_act[:, 2 * v + b] = act[v]
+        act = normed(hidden + b1[...], g1[...]).reshape(2, 3, 32, 512)
+        for u in range(2):
+            first_act[:, v + u] = act[u]
 
     v0, v1, v2 = [first_act[r].astype(F32) for r in range(3)]
     difference[0] = (v0 - v1).astype(BF16)
@@ -226,14 +228,14 @@
             axis=0,
         )
 
+    middle_sums[...] = jnp.dot(
+        lhs(first_act, 1),
+        side_by_side([(full,) for full in (full0, full1, full2)]),
+        preferred_element_type=F32,
+    )
     upper_sums[...] = jnp.dot(
         lhs(difference, 0),
         side_by_side([(low, w2.at[i, 0]) for i, low in enumerate((low0, low1, low2))]),
-        preferred_element_type=F32,
-    )
-    middle_sums[...] = jnp.dot(
-        lhs(first_act, 1),
-        side_by_side([(full,) for full in (full0, full1, full2)]),
         preferred_element_type=F32,
     )
     lower_sums[...] = jnp.dot(
@@ -328,8 +330,7 @@
         out_specs=hbm,
         scratch_shapes=[
             pltpu.VMEM((24, frames, 128), F32),
-            pltpu.VMEM((4, 5, 3, 32, 128), BF16),
-            pltpu.VMEM((3, 3, 32, 640), BF16),
+            pltpu.VMEM((8, 5, 3, 32, 128), BF16),
             pltpu.VMEM((3, 6, 32, c1), BF16),
             pltpu.VMEM((2, 6, 32, c1), BF16),
             pltpu.VMEM((128, 6 * c2), F32),

time: 17.4 us -> 17.4 us (level)
  no operation moved by 1% of the time
where the time goes in v9:
time: 17.4 us; the launch traced here: 17.2 us
  Pallas kernels  7.95 us (46%)
  waiting for transfers between devices  6.1 us (35%)
  starting transfers between devices  3.04 us (17%)
    ppermute x5, waiting for transfers between devices, hop(): return lax.ppermute(array, AXES, pairs)  6.1 us
    pallas_call x1, Pallas kernels, per_device(): pl.pallas_call(functools.partial(decode_kernel, rows_total), out_shape=ja...  4.66 us
    ppermute x5, starting transfers between devices, hop(): return lax.ppermute(array, AXES, pairs)  3.04 us
    pallas_call x3, Pallas kernels, tap_sums(): pl.pallas_call(functools.partial(tap_sums_kernel, i), out_shape=[pltpu.VM...  1.9 us
    pallas_call x1, Pallas kernels, fetched_first(): pl.pallas_call(first_weights_kernel, out_shape=shapes + [pltpu.VMEM((1,)...  1.39 us
  transfers between devices with their start and end apart: 5, of which 5 were waited for; matrix products, arithmetic and copies ran while one was open for 0% of the time, Pallas kernels for 19%

profile of v9, /device:TPU:23, one launch (start us, length us, event | category | flops | bytes accessed | tf_op | source)
XLA Modules:
  0.0 17.2 jit_solution(8747053268368697026)
XLA Ops:
  0.0 0.8 %collective-permute-start = (bf16[1,8,128]{2,1,0:T(8,128)(2,1)}, bf16[1,8,128]{2,1,0:T(8,128)(2,1)S(1)}, u32[]{:S(2)}, u32[]{:S(2)}) collective-permute-start(bf16[1,8,128]{2,1,0:T(8,128)(2,1)} %bitcast.10), channel_id=1, source_target_pairs={{0,3},{1,2},{2,1},{3,0},{4,7},{5,6},{6,5},{7,4},{8,11},{9,10},{10,... | collective-permute-start | bytes 6152 | tf_op jit(solution)/shard_map/ppermute | solution.py:20
  0.8 0.0 copy-start
  0.8 1.4 %shard_map.91 = (bf16[512,512]{1,0:T(8,128)(2,1)S(1)}, f32[1,512]{1,0:T(1,128)S(1)}, f32[1,512]{1,0:T(1,128)S(1)}, f32[1,256]{1,0:T(1,128)S(1)}, f32[1,256]{1,0:...) custom-call(bf16[3,9,16,512]{3,2,1,0:T(8,128)(2,1)} %bitcast.7, f32[1,512]{1,0:T(1,128)} %bitcast.8, ...), custom_call_target="tpu_custom_call" | custom-call | flops 10000000000 | bytes 40000000 | tf_op jit(solution)/shard_map/pallas_call | solution.py:84
  2.2 1.3 %collective-permute-done = bf16[1,8,128]{2,1,0:T(8,128)(2,1)S(1)} collective-permute-done((bf16[1,8,128]{2,1,0:T(8,128)(2,1)}, bf16[1,8,128]{2,1,0:T(8,128)(2,1)S(1)}, u32[]{:S(2)}, u32[]{:S(2)}) %collective-permute-start) | collective-permute-done | bytes 2080 | tf_op jit(solution)/shard_map/ppermute | solution.py:20
  3.5 0.6 %collective-permute-start.1 = (bf16[2,8,128]{2,1,0:T(8,128)(2,1)S(1)}, bf16[2,8,128]{2,1,0:T(8,128)(2,1)S(1)}, u32[]{:S(2)}, u32[]{:S(2)}) collective-permute-start(bf16[2,8,128]{2,1,0:T(8,128)(2,1)S(1)} %pad_maximum_fusion), channel_id=1, source_target_pairs={{0,5},{1,4},{2,7},{3,6},{4,1},{5,0},{6,3},{7,2},{8,13},{9,12},{10,... | collective-permute-start | bytes 12296 | tf_op jit(solution)/shard_map/ppermute | solution.py:20
  4.1 0.0 copy-done
  4.1 0.6 %shard_map.92 = (bf16[3,512,256]{2,1,0:T(8,128)(2,1)S(1)}, bf16[3,512,256]{2,1,0:T(8,128)(2,1)S(1)}, bf16[3,512,256]{2,1,0:T(8,128)(2,1)S(1)}) custom-call(bf16[3,3,3,512,256]{4,3,2,1,0:T(8,128)(2,1)S(1)} %copy-done), custom_call_target="tpu_custom_call" | custom-call | bytes 4000000 | tf_op jit(solution)/shard_map/pallas_call | solution.py:110
  4.8 1.8 %collective-permute-done.1 = bf16[2,8,128]{2,1,0:T(8,128)(2,1)S(1)} collective-permute-done((bf16[2,8,128]{2,1,0:T(8,128)(2,1)S(1)}, bf16[2,8,128]{2,1,0:T(8,128)(2,1)S(1)}, u32[]{:S(2)}, u32[]{:S(2)}) %collective-permute-start.1) | collective-permute-done | bytes 4128 | tf_op jit(solution)/shard_map/ppermute | solution.py:20
  6.6 0.0 copy-start.1
  6.6 1.6 %collective-permute-start.3 = (bf16[4,8,128]{2,1,0:T(8,128)(2,1)S(1)}, bf16[4,8,128]{2,1,0:T(8,128)(2,1)S(1)}, u32[]{:S(2)}, u32[]{:S(2)}) collective-permute-start(bf16[4,8,128]{2,1,0:T(8,128)(2,1)S(1)} %get-tuple-element.77), channel_id=1, source_target_pairs={{0,9},{1,8},{2,11},{3,10},{4,13},{5,12},{6,15},{7,14},{8,1},{9,0},... | collective-permute-start | bytes 24584 | tf_op jit(solution)/shard_map/ppermute | solution.py:20
  8.2 0.0 collective-permute-start.2
  8.2 0.6 %shard_map.93 = (bf16[3,512,256]{2,1,0:T(8,128)(2,1)S(1)}, bf16[3,512,256]{2,1,0:T(8,128)(2,1)S(1)}, bf16[3,512,256]{2,1,0:T(8,128)(2,1)S(1)}) custom-call(bf16[3,3,3,512,256]{4,3,2,1,0:T(8,128)(2,1)S(1)} %copy-done), custom_call_target="tpu_custom_call" | custom-call | bytes 4000000 | tf_op jit(solution)/shard_map/pallas_call | solution.py:110
  8.8 0.9 %collective-permute-done.3 = bf16[4,8,128]{2,1,0:T(8,128)(2,1)S(1)} collective-permute-done((bf16[4,8,128]{2,1,0:T(8,128)(2,1)S(1)}, bf16[4,8,128]{2,1,0:T(8,128)(2,1)S(1)}, u32[]{:S(2)}, u32[]{:S(2)}) %collective-permute-start.3) | collective-permute-done | bytes 8224 | tf_op jit(solution)/shard_map/ppermute | solution.py:20
  9.7 1.6 %collective-permute-done.2 = bf16[4,8,128]{2,1,0:T(8,128)(2,1)S(1)} collective-permute-done((bf16[4,8,128]{2,1,0:T(8,128)(2,1)S(1)}, bf16[4,8,128]{2,1,0:T(8,128)(2,1)S(1)}, u32[]{:S(2)}, u32[]{:S(2)}) %collective-permute-start.2) | collective-permute-done | bytes 8224 | tf_op jit(solution)/shard_map/ppermute | solution.py:20
  11.3 0.1 collective-permute-start.4
  11.4 0.6 %shard_map.94 = (bf16[3,512,256]{2,1,0:T(8,128)(2,1)S(1)}, bf16[3,512,256]{2,1,0:T(8,128)(2,1)S(1)}, bf16[3,512,256]{2,1,0:T(8,128)(2,1)S(1)}) custom-call(bf16[3,3,3,512,256]{4,3,2,1,0:T(8,128)(2,1)S(1)} %copy-done), custom_call_target="tpu_custom_call" | custom-call | bytes 4000000 | tf_op jit(solution)/shard_map/pallas_call | solution.py:110
  12.0 0.5 %collective-permute-done.4.received = bf16[12,8,128]{2,1,0:T(8,128)(2,1)S(1)} collective-permute-done((bf16[12,8,128]{2,1,0:T(8,128)(2,1)S(1)}, bf16[12,8,128]{2,1,0:T(8,128)(2,1)S(1)}, u32[]{:S(2)}, u32[]{:S(2)}) %collective-permute-start.4) | collective-permute-done | bytes 24608 | tf_op jit(solution)/shard_map/ppermute | solution.py:20
  12.5 0.0 copy-done.1
  12.5 4.7 %shard_map.95 = bf16[2,4,128,128]{3,2,1,0:T(8,128)(2,1)} custom-call(bf16[12,8,128]{2,1,0:T(8,128)(2,1)S(1)} %constant_dynamic-update-slice_fusion.3.held, bf16[12,8,128]{2,1,0:T(8,128)(2,1)S(1)} %collective-permute-done.4.received, bf16[512,512]{1,0:T(8,128)(2,1)S(1)} %get-tuple-element.61.w1, f32[1,512]{1,0:T(1,128)S(1)} %get-tuple-element.62.b1, ...), custom_call_target="tpu_custom_call" | custom-call | flops 4000000000 | bytes 10000000 | tf_op jit(solution)/shard_map/pallas_call | solution.py:326
  (6 shorter events, 0.0 us)
Async XLA Ops:
  0.0 3.5 %collective-permute-start = (bf16[1,8,128]{2,1,0:T(8,128)(2,1)}, bf16[1,8,128]{2,1,0:T(8,128)(2,1)S(1)}, u32[]{:S(2)}, u32[]{:S(2)}) collective-permute-start(bf16[1,8,128]{2,1,0:T(8,128)(2,1)} %bitcast.10), channel_id=1, source_target_pairs={{0,3},{1,2},{2,1},{3,0},{4,7},{5,6},{6,5},{7,4},{8,11},{9,10},{10,... | collective-permute-start | bytes 6152 | tf_op jit(solution)/shard_map/ppermute | solution.py:20
  0.8 3.3 %copy-start = (bf16[3,3,3,512,256]{4,3,2,1,0:T(8,128)(2,1)S(1)}, bf16[3,3,3,512,256]{4,3,2,1,0:T(8,128)(2,1)}, u32[]{:S(2)}) copy-start(bf16[3,3,3,512,256]{4,3,2,1,0:T(8,128)(2,1)} %w2) | copy-start | bytes 21233668
  3.5 3.1 %collective-permute-start.1 = (bf16[2,8,128]{2,1,0:T(8,128)(2,1)S(1)}, bf16[2,8,128]{2,1,0:T(8,128)(2,1)S(1)}, u32[]{:S(2)}, u32[]{:S(2)}) collective-permute-start(bf16[2,8,128]{2,1,0:T(8,128)(2,1)S(1)} %pad_maximum_fusion), channel_id=1, source_target_pairs={{0,5},{1,4},{2,7},{3,6},{4,1},{5,0},{6,3},{7,2},{8,13},{9,12},{10,... | collective-permute-start | bytes 12296 | tf_op jit(solution)/shard_map/ppermute | solution.py:20
  6.6 5.9 %copy-start.1 = (bf16[3,3,3,256,128]{4,3,2,1,0:T(8,128)(2,1)S(1)}, bf16[3,3,3,256,128]{4,3,2,1,0:T(8,128)(2,1)}, u32[]{:S(2)}) copy-start(bf16[3,3,3,256,128]{4,3,2,1,0:T(8,128)(2,1)} %w3.1) | copy-start | bytes 5308420
  6.6 3.1 %collective-permute-start.3 = (bf16[4,8,128]{2,1,0:T(8,128)(2,1)S(1)}, bf16[4,8,128]{2,1,0:T(8,128)(2,1)S(1)}, u32[]{:S(2)}, u32[]{:S(2)}) collective-permute-start(bf16[4,8,128]{2,1,0:T(8,128)(2,1)S(1)} %get-tuple-element.77), channel_id=1, source_target_pairs={{0,9},{1,8},{2,11},{3,10},{4,13},{5,12},{6,15},{7,14},{8,1},{9,0},... | collective-permute-start | bytes 24584 | tf_op jit(solution)/shard_map/ppermute | solution.py:20
  8.2 3.1 %collective-permute-start.2 = (bf16[4,8,128]{2,1,0:T(8,128)(2,1)S(1)}, bf16[4,8,128]{2,1,0:T(8,128)(2,1)S(1)}, u32[]{:S(2)}, u32[]{:S(2)}) collective-permute-start(bf16[4,8,128]{2,1,0:T(8,128)(2,1)S(1)} %get-tuple-element.77), channel_id=1, source_target_pairs={{0,1},{1,0},{2,3},{3,2},{4,5},{5,4},{6,7},{7,6},{8,17},{9,16},{10,... | collective-permute-start | bytes 24584 | tf_op jit(solution)/shard_map/ppermute | solution.py:20
  11.3 1.2 %collective-permute-start.4 = (bf16[12,8,128]{2,1,0:T(8,128)(2,1)S(1)}, bf16[12,8,128]{2,1,0:T(8,128)(2,1)S(1)}, u32[]{:S(2)}, u32[]{:S(2)}) collective-permute-start(bf16[12,8,128]{2,1,0:T(8,128)(2,1)S(1)} %constant_dynamic-update-slice_fusion.3.held), channel_id=1, source_target_pairs={{0,1},{1,0},{2,3},{3,2},{4,5},{5,4},{6,7},{7,6},{8,9},{9,8},{10,11... | collective-permute-start | bytes 73736 | tf_op jit(solution)/shard_map/ppermute | solution.py:20

commit v10 on v8

--- a/solution.py
+++ b/solution.py
@@ -158,16 +158,16 @@
 ):
     s = lax.axis_index("seq")
     t = lax.axis_index("tm")
-    z, x, y, c = s // 2, s % 2, t // 2, t % 2
+    z, x, y, c = s >> 1, s & 1, t >> 1, t & 1
     n_frames = held.shape[1]
     pieces[:12] = held[...].astype(F32)
     pieces[12:] = received[...].astype(F32)
 
     def piece_of(row, chunk):
-        dz, dx = row // 2 - z, row % 2 ^ x
-        dy, dc = chunk // 2 ^ y, chunk % 2 ^ c
-        group = jnp.where(dz == 0, 0, jnp.where((dz == 1) == (z % 2 == 0), 1, 2))
-        half = (dx + dy + dc + jnp.where(dz == 0, 0, 1)) % 2
+        dz, dx = (row >> 1) - z, (row & 1) ^ x
+        dy, dc = (chunk >> 1) ^ y, (chunk & 1) ^ c
+        group = jnp.where(dz == 0, 0, jnp.where((dz == 1) == ((z & 1) == 0), 1, 2))
+        half = (dx + dy + dc + jnp.where(dz == 0, 0, 1)) & 1
         return half * 12 + group * 4 + 2 * dx + dy
 
     before = n_frames - 2 - 2 * t
@@ -226,14 +226,14 @@
             axis=0,
         )
 
+    middle_sums[...] = jnp.dot(
+        lhs(first_act, 1),
+        side_by_side([(full,) for full in (full0, full1, full2)]),
+        preferred_element_type=F32,
+    )
     upper_sums[...] = jnp.dot(
         lhs(difference, 0),
         side_by_side([(low, w2.at[i, 0]) for i, low in enumerate((low0, low1, low2))]),
-        preferred_element_type=F32,
-    )
-    middle_sums[...] = jnp.dot(
-        lhs(first_act, 1),
-        side_by_side([(full,) for full in (full0, full1, full2)]),
         preferred_element_type=F32,
     )
     lower_sums[...] = jnp.dot(

time: 17.4 us -> 17.4 us (level)
  the two profiles are of different devices: /device:TPU:23 before, /device:TPU:21 now
where the time goes in v10:
time: 17.4 us; the launch traced here: 17.3 us
  Pallas kernels  8 us (46%)
  waiting for transfers between devices  5.16 us (30%)
  starting transfers between devices  4 us (23%)
    ppermute x5, waiting for transfers between devices, hop(): return lax.ppermute(array, AXES, pairs)  5.16 us
    pallas_call x1, Pallas kernels, per_device(): pl.pallas_call(functools.partial(decode_kernel, rows_total), out_shape=ja...  4.73 us
    ppermute x5, starting transfers between devices, hop(): return lax.ppermute(array, AXES, pairs)  4 us
    pallas_call x3, Pallas kernels, tap_sums(): pl.pallas_call(functools.partial(tap_sums_kernel, i), out_shape=[pltpu.VM...  1.9 us
    pallas_call x1, Pallas kernels, fetched_first(): pl.pallas_call(first_weights_kernel, out_shape=shapes + [pltpu.VMEM((1,)...  1.38 us
  transfers between devices with their start and end apart: 5, of which 5 were waited for; matrix products, arithmetic and copies ran while one was open for 0% of the time, Pallas kernels for 19%

profile of v10, /device:TPU:21, one launch (start us, length us, event | category | flops | bytes accessed | tf_op | source)
XLA Modules:
  0.0 17.3 jit_solution(1288723367550378815)
XLA Ops:
  0.0 0.8 %collective-permute-start = (bf16[1,8,128]{2,1,0:T(8,128)(2,1)}, bf16[1,8,128]{2,1,0:T(8,128)(2,1)S(1)}, u32[]{:S(2)}, u32[]{:S(2)}) collective-permute-start(bf16[1,8,128]{2,1,0:T(8,128)(2,1)} %bitcast.10), channel_id=1, source_target_pairs={{0,3},{1,2},{2,1},{3,0},{4,7},{5,6},{6,5},{7,4},{8,11},{9,10},{10,... | collective-permute-start | bytes 6152 | tf_op jit(solution)/shard_map/ppermute | solution.py:20
  0.8 0.0 copy-start
  0.8 1.4 %shard_map.91 = (bf16[10,80,512]{2,1,0:T(8,128)(2,1)S(1)}, f32[1,512]{1,0:T(1,128)S(1)}, f32[1,512]{1,0:T(1,128)S(1)}, f32[1,256]{1,0:T(1,128)S(1)}, f32[1,256]{...) custom-call(bf16[3,9,16,512]{3,2,1,0:T(8,128)(2,1)} %bitcast.7, f32[1,512]{1,0:T(1,128)} %bitcast.8, ...), custom_call_target="tpu_custom_call" | custom-call | flops 10000000000 | bytes 40000000 | tf_op jit(solution)/shard_map/pallas_call | solution.py:86
  2.2 1.3 %collective-permute-done = bf16[1,8,128]{2,1,0:T(8,128)(2,1)S(1)} collective-permute-done((bf16[1,8,128]{2,1,0:T(8,128)(2,1)}, bf16[1,8,128]{2,1,0:T(8,128)(2,1)S(1)}, u32[]{:S(2)}, u32[]{:S(2)}) %collective-permute-start) | collective-permute-done | bytes 2080 | tf_op jit(solution)/shard_map/ppermute | solution.py:20
  3.5 1.6 %collective-permute-start.1 = (bf16[2,8,128]{2,1,0:T(8,128)(2,1)S(1)}, bf16[2,8,128]{2,1,0:T(8,128)(2,1)S(1)}, u32[]{:S(2)}, u32[]{:S(2)}) collective-permute-start(bf16[2,8,128]{2,1,0:T(8,128)(2,1)S(1)} %pad_maximum_fusion), channel_id=1, source_target_pairs={{0,5},{1,4},{2,7},{3,6},{4,1},{5,0},{6,3},{7,2},{8,13},{9,12},{10,... | collective-permute-start | bytes 12296 | tf_op jit(solution)/shard_map/ppermute | solution.py:20
  5.1 0.0 copy-done
  5.1 0.6 %shard_map.92 = (bf16[3,512,256]{2,1,0:T(8,128)(2,1)S(1)}, bf16[3,512,256]{2,1,0:T(8,128)(2,1)S(1)}, bf16[3,512,256]{2,1,0:T(8,128)(2,1)S(1)}) custom-call(bf16[3,3,3,512,256]{4,3,2,1,0:T(8,128)(2,1)S(1)} %copy-done), custom_call_target="tpu_custom_call" | custom-call | bytes 4000000 | tf_op jit(solution)/shard_map/pallas_call | solution.py:112
  5.7 0.9 %collective-permute-done.1 = bf16[2,8,128]{2,1,0:T(8,128)(2,1)S(1)} collective-permute-done((bf16[2,8,128]{2,1,0:T(8,128)(2,1)S(1)}, bf16[2,8,128]{2,1,0:T(8,128)(2,1)S(1)}, u32[]{:S(2)}, u32[]{:S(2)}) %collective-permute-start.1) | collective-permute-done | bytes 4128 | tf_op jit(solution)/shard_map/ppermute | solution.py:20
  6.6 0.0 copy-start.1
  6.6 1.6 %collective-permute-start.3 = (bf16[4,8,128]{2,1,0:T(8,128)(2,1)S(1)}, bf16[4,8,128]{2,1,0:T(8,128)(2,1)S(1)}, u32[]{:S(2)}, u32[]{:S(2)}) collective-permute-start(bf16[4,8,128]{2,1,0:T(8,128)(2,1)S(1)} %get-tuple-element.77), channel_id=1, source_target_pairs={{0,9},{1,8},{2,11},{3,10},{4,13},{5,12},{6,15},{7,14},{8,1},{9,0},... | collective-permute-start | bytes 24584 | tf_op jit(solution)/shard_map/ppermute | solution.py:20
  8.2 0.0 collective-permute-start.2
  8.2 0.6 %shard_map.93 = (bf16[3,512,256]{2,1,0:T(8,128)(2,1)S(1)}, bf16[3,512,256]{2,1,0:T(8,128)(2,1)S(1)}, bf16[3,512,256]{2,1,0:T(8,128)(2,1)S(1)}) custom-call(bf16[3,3,3,512,256]{4,3,2,1,0:T(8,128)(2,1)S(1)} %copy-done), custom_call_target="tpu_custom_call" | custom-call | bytes 4000000 | tf_op jit(solution)/shard_map/pallas_call | solution.py:112
  8.8 0.9 %collective-permute-done.3 = bf16[4,8,128]{2,1,0:T(8,128)(2,1)S(1)} collective-permute-done((bf16[4,8,128]{2,1,0:T(8,128)(2,1)S(1)}, bf16[4,8,128]{2,1,0:T(8,128)(2,1)S(1)}, u32[]{:S(2)}, u32[]{:S(2)}) %collective-permute-start.3) | collective-permute-done | bytes 8224 | tf_op jit(solution)/shard_map/ppermute | solution.py:20
  9.7 1.6 %collective-permute-done.2 = bf16[4,8,128]{2,1,0:T(8,128)(2,1)S(1)} collective-permute-done((bf16[4,8,128]{2,1,0:T(8,128)(2,1)S(1)}, bf16[4,8,128]{2,1,0:T(8,128)(2,1)S(1)}, u32[]{:S(2)}, u32[]{:S(2)}) %collective-permute-start.2) | collective-permute-done | bytes 8224 | tf_op jit(solution)/shard_map/ppermute | solution.py:20
  11.3 0.1 collective-permute-start.4
  11.4 0.6 %shard_map.94 = (bf16[3,512,256]{2,1,0:T(8,128)(2,1)S(1)}, bf16[3,512,256]{2,1,0:T(8,128)(2,1)S(1)}, bf16[3,512,256]{2,1,0:T(8,128)(2,1)S(1)}) custom-call(bf16[3,3,3,512,256]{4,3,2,1,0:T(8,128)(2,1)S(1)} %copy-done), custom_call_target="tpu_custom_call" | custom-call | bytes 4000000 | tf_op jit(solution)/shard_map/pallas_call | solution.py:112
  12.0 0.5 %collective-permute-done.4.received = bf16[12,8,128]{2,1,0:T(8,128)(2,1)S(1)} collective-permute-done((bf16[12,8,128]{2,1,0:T(8,128)(2,1)S(1)}, bf16[12,8,128]{2,1,0:T(8,128)(2,1)S(1)}, u32[]{:S(2)}, u32[]{:S(2)}) %collective-permute-start.4) | collective-permute-done | bytes 24608 | tf_op jit(solution)/shard_map/ppermute | solution.py:20
  12.5 0.0 copy-done.1
  12.5 4.7 %shard_map.95 = bf16[2,4,128,128]{3,2,1,0:T(8,128)(2,1)} custom-call(bf16[12,8,128]{2,1,0:T(8,128)(2,1)S(1)} %constant_dynamic-update-slice_fusion.3.held, bf16[12,8,128]{2,1,0:T(8,128)(2,1)S(1)} %collective-permute-done.4.received, bf16[10,80,512]{2,1,0:T(8,128)(2,1)S(1)} %get-tuple-element.61.w1, f32[1,512]{1,0:T(1,128)S(1)} %get-tuple-element.62.b1, ...), custom_call_target="tpu_custom_call" | custom-call | flops 4000000000 | bytes 10000000 | tf_op jit(solution)/shard_map/pallas_call | solution.py:324
  (6 shorter events, 0.0 us)
Async XLA Ops:
  0.0 3.5 %collective-permute-start = (bf16[1,8,128]{2,1,0:T(8,128)(2,1)}, bf16[1,8,128]{2,1,0:T(8,128)(2,1)S(1)}, u32[]{:S(2)}, u32[]{:S(2)}) collective-permute-start(bf16[1,8,128]{2,1,0:T(8,128)(2,1)} %bitcast.10), channel_id=1, source_target_pairs={{0,3},{1,2},{2,1},{3,0},{4,7},{5,6},{6,5},{7,4},{8,11},{9,10},{10,... | collective-permute-start | bytes 6152 | tf_op jit(solution)/shard_map/ppermute | solution.py:20
  0.8 4.3 %copy-start = (bf16[3,3,3,512,256]{4,3,2,1,0:T(8,128)(2,1)S(1)}, bf16[3,3,3,512,256]{4,3,2,1,0:T(8,128)(2,1)}, u32[]{:S(2)}) copy-start(bf16[3,3,3,512,256]{4,3,2,1,0:T(8,128)(2,1)} %w2) | copy-start | bytes 21233668
  3.5 3.1 %collective-permute-start.1 = (bf16[2,8,128]{2,1,0:T(8,128)(2,1)S(1)}, bf16[2,8,128]{2,1,0:T(8,128)(2,1)S(1)}, u32[]{:S(2)}, u32[]{:S(2)}) collective-permute-start(bf16[2,8,128]{2,1,0:T(8,128)(2,1)S(1)} %pad_maximum_fusion), channel_id=1, source_target_pairs={{0,5},{1,4},{2,7},{3,6},{4,1},{5,0},{6,3},{7,2},{8,13},{9,12},{10,... | collective-permute-start | bytes 12296 | tf_op jit(solution)/shard_map/ppermute | solution.py:20
  6.6 5.9 %copy-start.1 = (bf16[3,3,3,256,128]{4,3,2,1,0:T(8,128)(2,1)S(1)}, bf16[3,3,3,256,128]{4,3,2,1,0:T(8,128)(2,1)}, u32[]{:S(2)}) copy-start(bf16[3,3,3,256,128]{4,3,2,1,0:T(8,128)(2,1)} %w3.1) | copy-start | bytes 5308420
  6.6 3.1 %collective-permute-start.3 = (bf16[4,8,128]{2,1,0:T(8,128)(2,1)S(1)}, bf16[4,8,128]{2,1,0:T(8,128)(2,1)S(1)}, u32[]{:S(2)}, u32[]{:S(2)}) collective-permute-start(bf16[4,8,128]{2,1,0:T(8,128)(2,1)S(1)} %get-tuple-element.77), channel_id=1, source_target_pairs={{0,9},{1,8},{2,11},{3,10},{4,13},{5,12},{6,15},{7,14},{8,1},{9,0},... | collective-permute-start | bytes 24584 | tf_op jit(solution)/shard_map/ppermute | solution.py:20
  8.2 3.1 %collective-permute-start.2 = (bf16[4,8,128]{2,1,0:T(8,128)(2,1)S(1)}, bf16[4,8,128]{2,1,0:T(8,128)(2,1)S(1)}, u32[]{:S(2)}, u32[]{:S(2)}) collective-permute-start(bf16[4,8,128]{2,1,0:T(8,128)(2,1)S(1)} %get-tuple-element.77), channel_id=1, source_target_pairs={{0,1},{1,0},{2,3},{3,2},{4,5},{5,4},{6,7},{7,6},{8,17},{9,16},{10,... | collective-permute-start | bytes 24584 | tf_op jit(solution)/shard_map/ppermute | solution.py:20
  11.3 1.2 %collective-permute-start.4 = (bf16[12,8,128]{2,1,0:T(8,128)(2,1)S(1)}, bf16[12,8,128]{2,1,0:T(8,128)(2,1)S(1)}, u32[]{:S(2)}, u32[]{:S(2)}) collective-permute-start(bf16[12,8,128]{2,1,0:T(8,128)(2,1)S(1)} %constant_dynamic-update-slice_fusion.3.held), channel_id=1, source_target_pairs={{0,1},{1,0},{2,3},{3,2},{4,5},{5,4},{6,7},{7,6},{8,9},{9,8},{10,11... | collective-permute-start | bytes 73736 | tf_op jit(solution)/shard_map/ppermute | solution.py:20
